TPU v7x, 32 devices: a whole 2x2x4 slice. The times are simulated.
32 devices in a mesh: band: 2 (over y), exp: 16 (over z, x, core).
Axes of the slice: x: 2, y: 2, z: 4, core: 2. Of those that a mesh axis runs over, the one named last changes fastest.
Arguments:
- exposure: float32 [32768, 512], P(('band', 'exp')), parts along dimension 0, may hold values from -8 to 8, as said below
- psf_taps: bfloat16 [32, 15], P(('band', 'exp')), parts along dimension 0, may hold values from -1.5 to 1.5
- col_warp: bfloat16 [16384, 512], P(('band', 'exp')), parts along dimension 0, may hold values from -0.25 to 0.25
- row_warp: bfloat16 [16384, 1024], P(('band', 'exp')), parts along dimension 0, may hold values from -0.1875 to 0.1875
- row_patch: int32 [16384, 1], P(('band', 'exp')), parts along dimension 0, may hold values from 0 to 15; in each aligned block of 512 rows (0 to 511, 512 to 1023, ...) at most 64 rows name the same one
- row_prow: int32 [16384], P(('band', 'exp')), parts along dimension 0, may hold values from 0 to 31
- owner_map: int32 [32], P('band'), parts along dimension 0, may hold values from 0 to 15, each once
Outputs:
- coadd: float32 [1024, 512], P(('band', 'exp')), parts along dimension 0
There are 2 independent parts, one for each index of `band`. A program takes and returns all parts, laid end to end along the dimension named above; each array names one. Nothing has to cross between parts.
Inputs may be any that keep to these rules, and one draw needn't show every extreme that they name: `row_patch`: the 512 resampled rows of one exposure piece (aligned blocks) name any one patch at most 64 times, a bound that some block reaches. `exposure`: each piece carries a background level per block of 128 columns on top of the sky noise.
All inputs are finite; a program needn't handle non-finite values.
Results may differ from a plain program's by a relative error of at most 0.0051.
Values sent between devices are 32-bit elements; how exact they have to be, the bound alone decides.
No kernel may reach another device: no remote copies, remote signals or barrier semaphores. Data moves between devices by JAX's collectives and lax.ppermute only.
A program may use at most 64 MiB of HBM per device.

v0:
```python
import jax
import jax.numpy as jnp
from jax import lax
from jax.sharding import PartitionSpec as P

STRIP = 16
TAPS = 15
PATCH_ROWS = 32


def extended(block, sides, width):
    for axis, dim in sides:
        count = lax.axis_size(axis)
        forward = [(i, i + 1) for i in range(count - 1)]
        forward.append((count - 1, 0))
        backward = [(target, source) for source, target in forward]
        low = lax.ppermute(
            lax.slice_in_dim(block, block.shape[dim] - width, None, axis=dim), axis, forward
        )
        high = lax.ppermute(lax.slice_in_dim(block, 0, width, axis=dim), axis, backward)
        block = jnp.concatenate([low, block, high], axis=dim)
    return block


def make_band(taps, width):
    half = (TAPS - 1) // 2
    rows_idx = jnp.arange(width, dtype=jnp.int32)[:, None]
    cols_idx = jnp.arange(width, dtype=jnp.int32)[None, :]
    offset = rows_idx - cols_idx + half
    band = jnp.zeros((width, width), jnp.bfloat16)
    for tap in range(TAPS):
        band = jnp.where(offset == tap, taps[tap], band)
    return band


def block_mean(strip, width):
    return jnp.mean(strip.reshape(STRIP, width // 128, 128), axis=(0, 2))


def on_device(exposure, psf_taps, col_warp, row_warp, row_patch, row_prow, owner_map):
    rows, width = exposure.shape
    out_rows = row_warp.shape[0]
    devices = lax.axis_size("exp")
    padded = extended(exposure, (("exp", 0),), STRIP)
    prev_last = padded[:STRIP]
    next_first = padded[rows + STRIP :]
    off_next = block_mean(exposure[rows - STRIP :] - next_first, width)
    off_prev = block_mean(prev_last - exposure[:STRIP], width)
    shift = jnp.repeat(-0.5 * off_next + 0.5 * off_prev, 128)
    corrected = (exposure + shift[None, :]).astype(jnp.bfloat16)
    band = make_band(psf_taps[0], width)
    matched = jnp.dot(corrected, band, preferred_element_type=jnp.float32).astype(jnp.bfloat16)
    warped_cols = jnp.dot(matched, col_warp, preferred_element_type=jnp.float32).astype(
        jnp.bfloat16
    )
    warped = jnp.dot(row_warp, warped_cols, preferred_element_type=jnp.float32)
    slot_ids = jnp.arange(devices, dtype=jnp.int32)
    slot_of = jnp.sum(
        jnp.where(owner_map[:, None] == slot_ids[None, :], slot_ids[:, None], 0), axis=0
    )
    patch = row_patch[:, 0]
    dest = jnp.sum(jnp.where(patch[:, None] == slot_ids[None, :], slot_of[None, :], 0), axis=1)
    key = dest * PATCH_ROWS + row_prow
    count = PATCH_ROWS * lax.axis_size("exp")
    local = key
    inside = (local >= 0) & (local < count)
    local = jnp.where(inside, local, count)
    sums = lax.psum_scatter(
        jax.ops.segment_sum(warped, local, num_segments=count + 1)[:count],
        "exp",
        scatter_dimension=0,
        tiled=True,
    )
    ones_term = jax.ops.segment_sum(
        jnp.ones((out_rows,), jnp.float32), key, num_segments=devices * PATCH_ROWS
    )
    counts = lax.psum_scatter(ones_term, "exp", scatter_dimension=0, tiled=True)
    return sums / jnp.maximum(counts, 1.0)[:, None]


def solution(mesh):
    placed = (
        P(("band", "exp"), None),
        P(("band", "exp"), None),
        P(("band", "exp"), None),
        P(("band", "exp"), None),
        P(("band", "exp"), None),
        P(("band", "exp")),
        P("band"),
    )
    return jax.shard_map(
        on_device, mesh=mesh, in_specs=placed, out_specs=P(("band", "exp"), None), check_vma=False
    )
```

profile of v0, /device:TPU:0, one launch (start us, length us, event | category | flops | bytes accessed | tf_op | source)
XLA Modules:
  0.0 101.5 jit_solution(14961704403674908618)
XLA Ops:
  6.5 0.0 copy-start
  6.5 0.0 reduce-scatter.2.cloned.1.call-start
  6.5 0.9 fusion.132
  7.4 0.5 collective-permute-start.1
  7.9 5.0 %collective-permute-start = (f32[16,512]{1,0:T(8,128)S(1)}, f32[16,512]{1,0:T(8,128)S(1)}, u32[]{:S(2)}, u32[]{:S(2)}) collective-permute-start(f32[16,512]{1,0:T(8,128)S(1)} %get-tuple-element.10), channel_id=1, source_target_pairs={{1,0},{2,1},{3,2},{4,3},{5,4},{6,5},{7,6},{8,7},{9,8},{10,9},{11,1... | collective-permute-start | bytes 98312 | tf_op jit(solution)/shard_map/ppermute | solution.py:20
  12.9 0.7 select_reduce_fusion.1
  13.6 0.8 select_reduce_fusion
  14.4 0.7 and_select_fusion
  15.1 1.9 %fusion.133 = (bf16[1,1]{1,0:T(2,128)(2,1)}, bf16[1,1]{1,0:T(2,128)(2,1)}, bf16[1,1]{1,0:T(2,128)(2,1)}, bf16[1,1]{1,0:T(2,128)(2,1)}, bf16[1,1]{1,0:T(2,128)(2,...) fusion(bf16[1,15]{1,0:T(2,128)(2,1)} %param.8), kind=kLoop, calls=%fused_computation.104 | loop fusion | bytes 60 | tf_op jit(solution)/shard_map/slice | solution.py:32
  17.0 0.0 collective-permute-done.1
  17.0 0.0 collective-permute-done
  17.0 0.8 subtract_reduce_fusion.1
  17.8 0.1 bitcast_reduce_fusion
  18.0 0.1 broadcast_bitcast_fusion
  18.0 12.4 %convolution_convert_fusion = bf16[1024,512]{1,0:T(8,128)(2,1)S(1)} fusion(bf16[512,512]{1,0:T(8,128)(2,1)} %param.9, f32[1024,512]{1,0:T(8,128)} %param.7, f32[512]{0:T(512)S(1)} %broadcast_bitcast_fusion, bf16[]{:T(256)} %bitcast.18, bf16[]{:T(256)} %bitcast.17, bf16[]{:T(256)} %bitcast.16, bf16[]{:T(256)} %bitcast.15, bf16[]{:T(256)} %bitcast.14, ...), kind=kOutput, calls=%fused_computation.3 | convolution fusion | flops 1084227584 | bytes 3672094 | tf_op jit(solution)/shard_map/dot_general | solution.py:53
  30.5 0.0 copy-done
  30.5 0.8 convolution_bitcast_fusion
  31.3 0.3 copy.10
  31.6 0.0 copy-start.1
  31.6 3.8 %scatter_custom_fusion = f32[513,512]{1,0:T(8,128)S(1)} fusion(s32[512]{0:T(512)S(1)} %get-tuple-element.7, f32[512,512]{1,0:T(8,128)S(1)} %copy.10, f32[]{:T(128)} %constant.22.clone.1), kind=kCustom, calls=%fused_computation.38 | custom fusion | flops 262144 | bytes 1050628 | tf_op jit(solution)/shard_map/scatter-add | solution.py:69
  35.5 1.1 %slice.89 = f32[512,512]{1,0:T(8,128)} slice(f32[513,512]{1,0:T(8,128)S(1)} %scatter_custom_fusion), slice={[0:512], [0:512]} | slice | bytes 2097152 | tf_op jit(solution)/shard_map/slice | solution.py:69
  36.5 0.0 reduce-scatter.2.cloned.1.call-update
  36.5 0.0 copy-done.1
  36.6 0.6 dynamic-slice
  37.8 4.1 %scatter_custom_fusion.1 = f32[512]{0:T(512)S(1)} fusion(s32[512]{0:T(512)S(1)} %get-tuple-element.8, f32[512]{0:T(512)S(1)} %broadcast.14, f32[]{:T(128)} %constant.22.clone.1), kind=kCustom, calls=%fused_computation.82 | custom fusion | flops 512 | bytes 2052 | tf_op jit(solution)/shard_map/scatter-add | solution.py:74
  41.9 31.6 %all-reduce = f32[512]{0:T(512)S(1)} all-reduce(f32[512]{0:T(512)S(1)} %scatter_custom_fusion.1), channel_id=3, replica_groups=mesh['band'=2,'exp'=16] {'exp'}, use_global_device_ids=true, to_apply=%region_9.10.clone | all-reduce | flops 512 | bytes 4096
  73.5 0.1 dynamic-slice_maximum_fusion
  73.5 19.6 %reduce-scatter.2.cloned.1.call-done = f32[32,512]{1,0:T(8,128)} async-done(((f32[512,512]{1,0:T(8,128)}), f32[32,512]{1,0:T(8,128)}) %reduce-scatter.2.cloned.1.call-update) | async-done | bytes 65552 | tf_op jit(solution)/shard_map/reduce_scatter | solution.py:68
  93.1 1.5 %broadcast_divide_fusion = f32[32,512]{1,0:T(8,128)} fusion(f32[32,512]{1,0:T(8,128)} %reduce-scatter.2.cloned.1.call-done, f32[32]{0:T(128)S(1)} %dynamic-slice_maximum_fusion), kind=kLoop, calls=%fused_computation.71 | loop fusion | flops 16384 | bytes 131200 | tf_op jit(solution)/shard_map/div | solution.py:78
  (2 shorter events, 0.0 us)
Async XLA Ops:
  6.5 24.0 %copy-start = (bf16[512,1024]{1,0:T(8,128)(2,1)S(1)}, bf16[512,1024]{1,0:T(8,128)(2,1)}, u32[]{:S(2)}) copy-start(bf16[512,1024]{1,0:T(8,128)(2,1)} %param.10) | copy-start | bytes 3145732
  6.5 86.6 %reduce-scatter.2.cloned.1.call-start = ((), (), s32[]{:S(2)}) async-start(), calls=%async_computation.1 | async-start | bytes 1114112 | tf_op jit(solution)/shard_map/reduce_scatter | solution.py:68
  7.4 9.6 %collective-permute-start.1 = (f32[16,512]{1,0:T(8,128)S(1)}, f32[16,512]{1,0:T(8,128)S(1)}, u32[]{:S(2)}, u32[]{:S(2)}) collective-permute-start(f32[16,512]{1,0:T(8,128)S(1)} %get-tuple-element.9), channel_id=1, source_target_pairs={{0,1},{1,2},{2,3},{3,4},{4,5},{5,6},{6,7},{7,8},{8,9},{9,10},{10,1... | collective-permute-start | bytes 98312 | tf_op jit(solution)/shard_map/ppermute | solution.py:17
  7.9 9.1 %collective-permute-start = (f32[16,512]{1,0:T(8,128)S(1)}, f32[16,512]{1,0:T(8,128)S(1)}, u32[]{:S(2)}, u32[]{:S(2)}) collective-permute-start(f32[16,512]{1,0:T(8,128)S(1)} %get-tuple-element.10), channel_id=1, source_target_pairs={{1,0},{2,1},{3,2},{4,3},{5,4},{6,5},{7,6},{8,7},{9,8},{10,9},{11,1... | collective-permute-start | bytes 98312 | tf_op jit(solution)/shard_map/ppermute | solution.py:20
  31.6 4.9 %copy-start.1 = (u32[32]{0:T(128)S(1)}, u32[32]{0:T(128)}, u32[]{:S(2)}) copy-start(u32[32]{0:T(128)} %constant.58) | copy-start | bytes 388
Sparse Core Ops, SparseCore 0:
  36.7 56.4 reduce-scatter.1
where the time goes:
time: 102 us
  blocking collectives  31.6 us (31%)
  waiting for transfers between devices  19.6 us (19%)
  between operations  14.1 us (14%)
  matrix products  13.2 us (13%)
  other arithmetic  12.7 us (12%)
  starting transfers between devices  5.48 us (5%)
  local copies, waits for them, and re-layouts  4.83 us (5%)
    unnamed x1, blocking collectives  31.6 us
    reduce_scatter x1, waiting for transfers between devices, on_device(): lax.psum_scatter(jax.ops.segment_sum(warped, local, num_segments=count +...  19.6 us
    dot_general x1, matrix products, on_device(): jnp.dot(matched, col_warp, preferred_element_type=jnp.float32)  12.4 us
    ppermute x1, starting transfers between devices, extended(): lax.ppermute(lax.slice_in_dim(block, 0, width, axis=dim), axis, backward)  5.02 us
    scatter-add x1, other arithmetic, on_device(): jax.ops.segment_sum(jnp.ones((out_rows,), jnp.float32), key, num_segments...  4.09 us
    scatter-add x1, other arithmetic, on_device(): jax.ops.segment_sum(warped, local, num_segments=count + 1)[:count]  3.82 us
  transfers between devices with their start and end apart: 3, of which 1 were waited for; matrix products, arithmetic and copies ran while one was open for 9% of the time, Pallas kernels for 0%

commit v1 on v0

v1 whole, which is shorter than its diff:
```python
import functools

import jax
import jax.numpy as jnp
from jax import lax
from jax.experimental import pallas as pl
from jax.experimental.pallas import tpu as pltpu
from jax.sharding import PartitionSpec as P

STRIP = 16
TAPS = 15
PATCH_ROWS = 32
LANES = 128
SUB = 8
CHUNKS = 4
QUAD = 4
VMEM_LIMIT = 48 * 1024 * 1024

f32 = jnp.float32
bf16 = jnp.bfloat16


def swap(block, mask, count):
    return lax.ppermute(block, "exp", [(i, i ^ mask) for i in range(count)])


def swap_ring(block, count):
    pairs = [((2 * i + 1) % count, (2 * i + 2) % count) for i in range(count // 2)]
    return lax.ppermute(block, "exp", pairs + [(b, a) for a, b in pairs])


def call(body, outs, ins, args, scratch=(), flops=0, **more):
    moved = sum(a.size * a.dtype.itemsize for a in args)
    return pl.pallas_call(
        body,
        out_shape=outs,
        in_specs=ins,
        out_specs=jax.tree.map(lambda _: pl.BlockSpec(memory_space=pltpu.VMEM), outs),
        scratch_shapes=scratch,
        compiler_params=pltpu.CompilerParams(vmem_limit_bytes=VMEM_LIMIT),
        cost_estimate=pl.CostEstimate(flops=flops, bytes_accessed=moved, transcendentals=0),
        **more,
    )(*args)


def strips_body(first_ref, last_ref, pair_ref, ring_ref, own_ref):
    even = lax.rem(lax.axis_index("exp"), 2) == 0
    own_ref[...] = jnp.zeros_like(own_ref)
    pair_ref[...] = jnp.zeros_like(pair_ref)
    ring_ref[...] = jnp.zeros_like(ring_ref)
    scale = 1.0 / (STRIP * LANES)
    for b in range(first_ref.shape[1] // LANES):
        at = slice(b * LANES, (b + 1) * LANES)
        means = []
        for ref in (first_ref, last_ref):
            column = jnp.sum(ref[:, at], axis=0, keepdims=True)
            total = jnp.sum(column, axis=1, keepdims=True)
            means.append(jnp.broadcast_to(total * scale, (1, LANES)))
        first, last = means
        own_ref[b : b + 1] = 0.5 * (first + last)
        pair_ref[b : b + 1] = jnp.where(even, last, first)
        ring_ref[b : b + 1] = jnp.where(even, first, last)


def local_body(
    owner_ref, taps_ref, patch_ref, prow_ref, own_ref, exposure, col_warp, row_warp,
    sums_ref, rows_ref, count_ref, blocks_ref,
    image, cols, rows, band, merged, warped, high, low, select, sems,
):
    count = owner_ref.shape[0]
    height, width = exposure.shape
    nb = width // LANES
    step = height // CHUNKS
    copies = [pltpu.make_async_copy(col_warp, cols, sems.at[0])]
    for i in range(CHUNKS):
        at = pl.ds(i * step, step)
        copies.append(pltpu.make_async_copy(exposure.at[at], image.at[at], sems.at[1 + i]))
    copies.append(pltpu.make_async_copy(row_warp, rows, sems.at[1 + CHUNKS]))
    for copy in copies:
        copy.start()

    delta = lax.broadcasted_iota(jnp.int32, (LANES, LANES), 0) - lax.broadcasted_iota(
        jnp.int32, (LANES, LANES), 1
    )
    tiles = {}
    for side in (-1, 0, 1):
        offset = delta + side * LANES + (TAPS - 1) // 2
        tile = jnp.zeros((LANES, LANES), f32)
        for tap in range(TAPS):
            tile = jnp.where(offset == tap, taps_ref[0:1, tap : tap + 1].astype(f32), tile)
        tiles[side] = tile.astype(bf16)
    for i in range(nb):
        for k in range(nb):
            tile = tiles.get(i - k, jnp.zeros((LANES, LANES), bf16))
            band[i * LANES : (i + 1) * LANES, k * LANES : (k + 1) * LANES] = tile

    me = lax.axis_index("exp")
    patch = patch_ref[...]
    slot = jnp.zeros_like(patch)
    for k in range(count):
        mask = me ^ k
        place = (mask & 1) * (count // 2) + lax.shift_right_logical(mask, 1)
        slot = jnp.where(patch == owner_ref[k], place, slot)
    key = slot * PATCH_ROWS + prow_ref[...]
    slots = lax.broadcasted_iota(jnp.int32, select.shape, 0)
    select[...] = jnp.where(slots == key, 1.0, 0.0).astype(bf16)

    ones = jnp.ones((select.shape[1], LANES), bf16)
    held = jnp.dot(select[...], ones, preferred_element_type=f32)
    lane = lax.broadcasted_iota(jnp.int32, (SUB, LANES), 1)
    for j in range(count):
        tile = jnp.zeros((SUB, LANES), f32)
        for s in range(PATCH_ROWS // SUB):
            at = j * PATCH_ROWS + s * SUB
            tile = jnp.where(lane == s, held[at : at + SUB], tile)
        count_ref[j * SUB : (j + 1) * SUB] = tile

    copies[0].wait()
    both = jnp.dot(band[...], cols[...], preferred_element_type=f32)
    blocks_ref[...] = jnp.zeros_like(blocks_ref)
    for b in range(nb):
        part = both[b * LANES : (b + 1) * LANES]
        blocks_ref[b : b + 1] = jnp.sum(part, axis=0, keepdims=True)
    merged[...] = both.astype(bf16)

    warped[:, width:] = jnp.ones((height, LANES), bf16)
    for i in range(CHUNKS):
        copies[1 + i].wait()
        at = slice(i * step, (i + 1) * step)
        parts = []
        for b in range(nb):
            piece = image[at, b * LANES : (b + 1) * LANES] - own_ref[b : b + 1]
            parts.append(piece.astype(bf16))
        centred = jnp.concatenate(parts, axis=1)
        warped[at, :width] = jnp.dot(
            centred, merged[...], preferred_element_type=f32
        ).astype(bf16)
    copies[1 + CHUNKS].wait()
    values = jnp.dot(rows[...], warped[...], preferred_element_type=f32)
    top = values.astype(bf16)
    high[...] = top
    low[...] = (values - top.astype(f32)).astype(bf16)
    sums = jnp.dot(select[...], high[...], preferred_element_type=f32) + jnp.dot(
        select[...], low[...], preferred_element_type=f32
    )
    sums_ref[...] = sums[:, :width]
    rows_ref[...] = sums[:, width:]


def level_rows(pair_ref, ring_ref, blocks_ref):
    nb = blocks_ref.shape[1] // LANES
    out = []
    for c in range(nb):
        total = jnp.zeros((1, LANES), f32)
        for b in range(nb):
            level = 0.5 * (pair_ref[b : b + 1] + ring_ref[b : b + 1])
            total += level * blocks_ref[b : b + 1, c * LANES : (c + 1) * LANES]
        out.append(total)
    return out


def send_body(pair_ref, ring_ref, blocks_ref, sums_ref, rows_ref, count_ref, out_ref):
    level = level_rows(pair_ref, ring_ref, blocks_ref)
    half = count_ref.shape[0] // SUB // 2
    size = out_ref.shape[0] // half
    for j in range(half):
        at = (half + j) * PATCH_ROWS
        weight = rows_ref[at : at + PATCH_ROWS]
        for c, row in enumerate(level):
            to = j * size + c * PATCH_ROWS
            part = sums_ref[at : at + PATCH_ROWS, c * LANES : (c + 1) * LANES]
            out_ref[to : to + PATCH_ROWS] = part + weight * row
        to = j * size + len(level) * PATCH_ROWS
        out_ref[to : to + SUB] = count_ref[(half + j) * SUB : (half + j + 1) * SUB]


def merge_body(
    pair_ref, ring_ref, blocks_ref, sums_ref, rows_ref, count_ref, got_ref, *out_refs
):
    level = level_rows(pair_ref, ring_ref, blocks_ref)
    half = count_ref.shape[0] // SUB // 2
    size = got_ref.shape[0] // half
    for j in range(half):
        quad, far = j % QUAD, j // QUAD
        ref = out_refs[quad] if far == 0 else out_refs[QUAD + quad]
        base = 0 if far == 0 else (far - 1) * size
        at = j * PATCH_ROWS
        weight = rows_ref[at : at + PATCH_ROWS]
        for c, row in enumerate(level):
            to = c * PATCH_ROWS
            part = sums_ref[at : at + PATCH_ROWS, c * LANES : (c + 1) * LANES]
            got = got_ref[j * size + to : j * size + to + PATCH_ROWS]
            ref[base + to : base + to + PATCH_ROWS] = part + weight * row + got
        to = len(level) * PATCH_ROWS
        got = got_ref[j * size + to : j * size + to + SUB]
        ref[base + to : base + to + SUB] = count_ref[j * SUB : (j + 1) * SUB] + got


def far_body(a_ref, b_ref, c_ref, d_ref, *out_refs):
    size = out_refs[0].shape[0]
    for i, ref in enumerate(out_refs):
        at = slice(i * size, (i + 1) * size)
        ref[...] = (a_ref[at] + b_ref[at]) + (c_ref[at] + d_ref[at])


def final_body(*refs):
    out_ref = refs[-1]
    total = refs[0][...]
    for ref in refs[1:-1]:
        total = total + ref[...]
    nb = out_ref.shape[1] // LANES
    held = total[nb * PATCH_ROWS :]
    for s in range(PATCH_ROWS // SUB):
        number = jnp.maximum(held[:, s : s + 1], 1.0)
        for c in range(nb):
            at = c * PATCH_ROWS + s * SUB
            out_ref[s * SUB : (s + 1) * SUB, c * LANES : (c + 1) * LANES] = (
                total[at : at + SUB] / number
            )


def on_device(exposure, psf_taps, col_warp, row_warp, row_patch, row_prow, owner_map):
    height, width = exposure.shape
    out_rows = row_warp.shape[0]
    count = lax.axis_size("exp")
    nb = width // LANES
    slots = count * PATCH_ROWS
    half, high_groups = count // 2, count // (2 * QUAD)
    size = PATCH_ROWS * nb + SUB
    vmem = pl.BlockSpec(memory_space=pltpu.VMEM)
    smem = pl.BlockSpec(memory_space=pltpu.SMEM)
    anywhere = pl.BlockSpec(memory_space=pl.ANY)

    def shape(*dims):
        return jax.ShapeDtypeStruct(dims, f32)

    tile = shape(-(-nb // SUB) * SUB, LANES)
    pair, ring, own = pl.pallas_call(
        strips_body,
        grid=(1,),
        out_shape=[tile, tile, tile],
        in_specs=[
            pl.BlockSpec((STRIP, width), lambda i: (0, 0)),
            pl.BlockSpec((STRIP, width), lambda i: (height // STRIP - 1, 0)),
        ],
        out_specs=[pl.BlockSpec(tile.shape, lambda i: (0, 0))] * 3,
    )(exposure, exposure)
    pair = swap(pair, 1, count)
    ring = swap_ring(ring, count)

    wide = width + LANES
    sums, rows, held, blocks = call(
        local_body,
        [shape(slots, width), shape(slots, LANES), shape(count * SUB, LANES),
         shape(tile.shape[0], width)],
        [smem, vmem, vmem, vmem, vmem, anywhere, anywhere, anywhere],
        (owner_map, psf_taps, row_patch.reshape(1, out_rows), row_prow.reshape(1, out_rows),
         own, exposure, col_warp, row_warp),
        scratch=[
            pltpu.VMEM((height, width), f32),
            pltpu.VMEM((width, width), bf16),
            pltpu.VMEM((out_rows, height), bf16),
            pltpu.VMEM((width, width), bf16),
            pltpu.VMEM((width, width), bf16),
            pltpu.VMEM((height, wide), bf16),
            pltpu.VMEM((out_rows, wide), bf16),
            pltpu.VMEM((out_rows, wide), bf16),
            pltpu.VMEM((slots, out_rows), bf16),
            pltpu.SemaphoreType.DMA((CHUNKS + 2,)),
        ],
        flops=2 * height * width * (width + out_rows) + 4 * slots * out_rows * width,
    )
    common = (pair, ring, blocks, sums, rows, held)
    send = call(send_body, shape(half * size, LANES), [vmem] * 6, common)
    got = swap(send, 1, count)

    shapes = [shape(size, LANES)] * QUAD
    if high_groups > 1:
        shapes += [shape((high_groups - 1) * size, LANES)] * QUAD
    parts = call(merge_body, shapes, [vmem] * 7, common + (got,))
    near, far = parts[:QUAD], parts[QUAD:]
    terms = [near[0]]
    if high_groups > 1:
        far = [far[0]] + [swap(far[q], 2 * q, count) for q in range(QUAD - 1, 0, -1)]
    near_got = [swap(near[q], 2 * q, count) for q in range(QUAD - 1, 0, -1)]
    if high_groups > 1:
        sent = call(far_body, [shape(size, LANES)] * (high_groups - 1), [vmem] * QUAD, far)
        terms += [swap(sent[h - 1], 2 * QUAD * h, count) for h in range(1, high_groups)]
    terms += near_got
    return call(final_body, shape(PATCH_ROWS, width), [vmem] * len(terms), tuple(terms))


def solution(mesh):
    placed = (
        P(("band", "exp"), None),
        P(("band", "exp"), None),
        P(("band", "exp"), None),
        P(("band", "exp"), None),
        P(("band", "exp"), None),
        P(("band", "exp")),
        P("band"),
    )
    return jax.shard_map(
        on_device, mesh=mesh, in_specs=placed, out_specs=P(("band", "exp"), None), check_vma=False
    )
```

time: 102 us -> 30.4 us (0.30)
  blocking collectives: 31.6 us -> 0 us
  between operations: 14.1 us -> 0.11 us
  matrix products: 13.2 us -> 0 us
  other arithmetic: 12.7 us -> 0 us
  waiting for transfers between devices: 19.6 us -> 8.05 us
  Pallas kernels: 0 us -> 7.79 us
  starting transfers between devices: 5.48 us -> 12.6 us
  local copies, waits for them, and re-layouts: 4.83 us -> 1.73 us
    unnamed x1 -> x0, blocking collectives: 31.6 us -> none
    reduce_scatter x1 -> x0, waiting for transfers between devices: 19.6 us -> none  [on_device(): lax.psum_scatter(jax.ops.segment_sum(warped, local, num_segments=count +...]
    dot_general x2 -> x0, matrix products: 13.2 us -> none  [the longest x1 12.4 us: on_device(): jnp.dot(matched, col_warp, preferred_element_type=jnp.float32)]
    ppermute x2 -> x10, waiting for transfers between devices: 0.01 us -> 8.05 us  [the longest x9 8.04 us: swap(): return lax.ppermute(block, 'exp', [(i, i ^ mask) for i in range(count)])]
    scatter-add x2 -> x0, other arithmetic: 7.91 us -> none  [the longest x1 4.09 us: on_device(): jax.ops.segment_sum(jnp.ones((out_rows,), jnp.float32), key, num_segments...]
    pallas_call x0 -> x6, Pallas kernels: none -> 7.79 us  [the longest x5 6.17 us: call(): pl.pallas_call(body, out_shape=outs, in_specs=ins, out_specs=jax.tree.map...]
    ppermute x2 -> x10, starting transfers between devices: 5.47 us -> 12.6 us  [the longest x9 6.93 us: swap(): return lax.ppermute(block, 'exp', [(i, i ^ mask) for i in range(count)])]
    slice x3 -> x0, local copies, waits for them, and re-layouts: 3.83 us -> none  [the longest x1 1.91 us: make_band(): band = jnp.where(offset == tap, taps[tap], band)]
  transfers between devices with their start and end apart: 3 -> 10, of which waited for: 1 -> 5; matrix products, arithmetic and copies ran while one was open for 9% -> 0% of each run, Pallas kernels for 0% -> 18%
where the time goes in v1:
time: 30.4 us; the launch traced here: 30.2 us
  starting transfers between devices  12.6 us (41%)
  waiting for transfers between devices  8.05 us (26%)
  Pallas kernels  7.79 us (26%)
  local copies, waits for them, and re-layouts  1.73 us (6%)
    ppermute x9, waiting for transfers between devices, swap(): return lax.ppermute(block, 'exp', [(i, i ^ mask) for i in range(count)])  8.04 us
    ppermute x9, starting transfers between devices, swap(): return lax.ppermute(block, 'exp', [(i, i ^ mask) for i in range(count)])  6.93 us
    pallas_call x5, Pallas kernels, call(): pl.pallas_call(body, out_shape=outs, in_specs=ins, out_specs=jax.tree.map...  6.17 us
    ppermute x1, starting transfers between devices, swap_ring(): return lax.ppermute(block, 'exp', pairs + [(b, a) for a, b in pairs])  5.64 us
    unnamed x16, local copies, waits for them, and re-layouts  1.73 us
    pallas_call x1, Pallas kernels, on_device(): pl.pallas_call(strips_body, grid=(1,), out_shape=[tile, tile, tile], in_s...  1.62 us
  transfers between devices with their start and end apart: 10, of which 5 were waited for; matrix products, arithmetic and copies ran while one was open for 0% of the time, Pallas kernels for 18%

profile of v1, /device:TPU:0, one launch (start us, length us, event | category | flops | bytes accessed | tf_op | source)
XLA Modules:
  0.0 30.2 jit_solution(9694146424024812306)
XLA Ops:
  0.0 0.0 copy-start.7
  0.0 1.6 %shard_map.73 = (f32[8,128]{1,0:T(8,128)}, f32[8,128]{1,0:T(8,128)}, f32[8,128]{1,0:T(8,128)}) custom-call(f32[1024,512]{1,0:T(8,128)} %exposure.1, f32[1024,512]{1,0:T(8,128)} %exposure.1), custom_call_target="tpu_custom_call" | custom-call | tf_op jit(solution)/shard_map/pallas_call | solution.py:238
  1.6 0.5 %collective-permute-start = (f32[8,128]{1,0:T(8,128)}, f32[8,128]{1,0:T(8,128)S(1)}, u32[]{:S(2)}, u32[]{:S(2)}) collective-permute-start(f32[8,128]{1,0:T(8,128)} %get-tuple-element.20), channel_id=1, source_target_pairs={{0,1},{1,0},{2,3},{3,2},{4,5},{5,4},{6,7},{7,6},{8,9},{9,8},{10,11... | collective-permute-start | bytes 12296 | tf_op jit(solution)/shard_map/ppermute | solution.py:24
  2.1 5.6 %collective-permute-start.1 = (f32[8,128]{1,0:T(8,128)}, f32[8,128]{1,0:T(8,128)S(1)}, u32[]{:S(2)}, u32[]{:S(2)}) collective-permute-start(f32[8,128]{1,0:T(8,128)} %get-tuple-element.21), channel_id=1, source_target_pairs={{1,2},{3,4},{5,6},{7,8},{9,10},{11,12},{13,14},{15,0},{2,1},{4,3},... | collective-permute-start | bytes 12296 | tf_op jit(solution)/shard_map/ppermute | solution.py:29
  7.7 0.0 copy-done
  7.8 0.0 copy-done.1
  7.8 0.0 copy-done.7
  7.8 0.0 copy-start.2
  7.8 1.0 %copy-done.2 = bf16[512,512]{1,0:T(8,128)(2,1)S(1)} copy-done((bf16[512,512]{1,0:T(8,128)(2,1)S(1)}, bf16[512,512]{1,0:T(8,128)(2,1)}, u32[]{:S(2)}) %copy-start.2) | copy-done | bytes 524312
  8.8 0.7 %copy-done.3 = f32[8,128]{1,0:T(8,128)S(1)} copy-done((f32[8,128]{1,0:T(8,128)S(1)}, f32[8,128]{1,0:T(8,128)}, u32[]{:S(2)}) %copy-start.3) | copy-done | bytes 4120
  9.5 5.3 %shard_map.74 = (f32[512,512]{1,0:T(8,128)S(1)}, f32[512,128]{1,0:T(8,128)S(1)}, f32[128,128]{1,0:T(8,128)S(1)}, f32[8,512]{1,0:T(8,128)S(1)}) custom-call(s32[16]{0:T(128)S(1)} %copy-done.6, bf16[1,15]{1,0:T(2,128)(2,1)S(1)} %copy-done.7, s32[1,512]{1,0:T(1,128)S(1)} %bitcast.2, s32[1,512]{1,0:T(1,128)S(1)} %bitcast.3, f32[8,128]{1,0:T(8,128)S(1)} %copy-done.3, ...), custom_call_target="tpu_custom_call" | custom-call | flops 1610612736 | bytes 3678302 | tf_op jit(solution)/shard_map/pallas_call | solution.py:34
  14.8 0.0 collective-permute-done.pair_ref
  14.8 0.0 collective-permute-done.1.ring_ref
  14.8 0.1 shard_map.75
  14.9 0.1 collective-permute-start.2
  15.0 1.9 %collective-permute-done.2.got_ref = f32[1088,128]{1,0:T(8,128)S(1)} collective-permute-done((f32[1088,128]{1,0:T(8,128)S(1)}, f32[1088,128]{1,0:T(8,128)S(1)}, u32[]{:S(2)}, u32[]{:S(2)}) %collective-permute-start.2) | collective-permute-done | bytes 557088 | tf_op jit(solution)/shard_map/ppermute | solution.py:24
  16.9 0.1 shard_map.76
  17.0 0.1 collective-permute-start.3
  17.1 0.1 collective-permute-start.4
  17.2 3.4 %collective-permute-start.5 = (f32[136,128]{1,0:T(8,128)S(1)}, f32[136,128]{1,0:T(8,128)S(1)}, u32[]{:S(2)}, u32[]{:S(2)}) collective-permute-start(f32[136,128]{1,0:T(8,128)S(1)} %get-tuple-element.31), channel_id=1, source_target_pairs={{0,2},{1,3},{2,0},{3,1},{4,6},{5,7},{6,4},{7,5},{8,10},{9,11},{10,... | collective-permute-start | bytes 208904 | tf_op jit(solution)/shard_map/ppermute | solution.py:24
  20.6 0.1 collective-permute-start.7
  20.6 1.4 %collective-permute-start.8 = (f32[136,128]{1,0:T(8,128)S(1)}, f32[136,128]{1,0:T(8,128)S(1)}, u32[]{:S(2)}, u32[]{:S(2)}) collective-permute-start(f32[136,128]{1,0:T(8,128)S(1)} %get-tuple-element.33), channel_id=1, source_target_pairs={{0,4},{1,5},{2,6},{3,7},{4,0},{5,1},{6,2},{7,3},{8,12},{9,13},{10,... | collective-permute-start | bytes 208904 | tf_op jit(solution)/shard_map/ppermute | solution.py:24
  22.0 0.9 %collective-permute-done.3.b_ref = f32[136,128]{1,0:T(8,128)S(1)} collective-permute-done((f32[136,128]{1,0:T(8,128)S(1)}, f32[136,128]{1,0:T(8,128)S(1)}, u32[]{:S(2)}, u32[]{:S(2)}) %collective-permute-start.3) | collective-permute-done | bytes 69664 | tf_op jit(solution)/shard_map/ppermute | solution.py:24
  22.9 1.1 %collective-permute-start.9 = (f32[136,128]{1,0:T(8,128)S(1)}, f32[136,128]{1,0:T(8,128)S(1)}, u32[]{:S(2)}, u32[]{:S(2)}) collective-permute-start(f32[136,128]{1,0:T(8,128)S(1)} %get-tuple-element.34), channel_id=1, source_target_pairs={{0,2},{1,3},{2,0},{3,1},{4,6},{5,7},{6,4},{7,5},{8,10},{9,11},{10,... | collective-permute-start | bytes 208904 | tf_op jit(solution)/shard_map/ppermute | solution.py:24
  24.0 0.0 collective-permute-done.4.c_ref
  24.0 0.0 collective-permute-done.5.d_ref
  24.1 0.3 collective-permute-start.6
  24.4 1.6 %collective-permute-done.7.refs_2_ = f32[136,128]{1,0:T(8,128)S(1)} collective-permute-done((f32[136,128]{1,0:T(8,128)S(1)}, f32[136,128]{1,0:T(8,128)S(1)}, u32[]{:S(2)}, u32[]{:S(2)}) %collective-permute-start.7) | collective-permute-done | bytes 69664 | tf_op jit(solution)/shard_map/ppermute | solution.py:24
  25.9 0.0 collective-permute-done.8.refs_3_
  25.9 1.3 %collective-permute-done.9.refs_4_ = f32[136,128]{1,0:T(8,128)S(1)} collective-permute-done((f32[136,128]{1,0:T(8,128)S(1)}, f32[136,128]{1,0:T(8,128)S(1)}, u32[]{:S(2)}, u32[]{:S(2)}) %collective-permute-start.9) | collective-permute-done | bytes 69664 | tf_op jit(solution)/shard_map/ppermute | solution.py:24
  27.2 2.3 %collective-permute-done.6.refs_1_ = f32[136,128]{1,0:T(8,128)S(1)} collective-permute-done((f32[136,128]{1,0:T(8,128)S(1)}, f32[136,128]{1,0:T(8,128)S(1)}, u32[]{:S(2)}, u32[]{:S(2)}) %collective-permute-start.6) | collective-permute-done | bytes 69664 | tf_op jit(solution)/shard_map/ppermute | solution.py:24
  29.5 0.7 %shard_map.78 = f32[32,512]{1,0:T(8,128)} custom-call(f32[136,128]{1,0:T(8,128)S(1)} %get-tuple-element.27.refs_0_, f32[136,128]{1,0:T(8,128)S(1)} %collective-permute-done.6.refs_1_, f32[136,128]{1,0:T(8,128)S(1)} %collective-permute-done.7.refs_2_, f32[136,128]{1,0:T(8,128)S(1)} %collective-permute-done.8.refs_3_, ...), custom_call_target="tpu_custom_call" | custom-call | bytes 348160 | tf_op jit(solution)/shard_map/pallas_call | solution.py:34
  (10 shorter events, 0.0 us)
Async XLA Ops:
  0.0 7.7 %copy-start = (f32[1024,512]{1,0:T(8,128)S(1)}, f32[1024,512]{1,0:T(8,128)}, u32[]{:S(2)}) copy-start(f32[1024,512]{1,0:T(8,128)} %exposure.1) | copy-start | bytes 6291460
  0.0 7.8 %copy-start.6 = (s32[16]{0:T(128)S(1)}, s32[16]{0:T(128)}, u32[]{:S(2)}) copy-start(s32[16]{0:T(128)} %owner_ref.1) | copy-start | bytes 196
  0.0 7.8 %copy-start.5 = (s32[512]{0:T(512)S(1)}, s32[512]{0:T(512)}, u32[]{:S(2)}) copy-start(s32[512]{0:T(512)} %param.12) | copy-start | bytes 6148
  0.0 7.8 %copy-start.4 = (s32[512,1]{0,1:T(1,128)S(1)}, s32[512,1]{0,1:T(1,128)}, u32[]{:S(2)}) copy-start(s32[512,1]{0,1:T(1,128)} %param.11) | copy-start | bytes 6148
  0.0 7.8 %copy-start.1 = (bf16[512,1024]{1,0:T(8,128)(2,1)S(1)}, bf16[512,1024]{1,0:T(8,128)(2,1)}, u32[]{:S(2)}) copy-start(bf16[512,1024]{1,0:T(8,128)(2,1)} %row_warp.1) | copy-start | bytes 3145732
  0.0 7.8 %copy-start.7 = (bf16[1,15]{1,0:T(2,128)(2,1)S(1)}, bf16[1,15]{1,0:T(2,128)(2,1)}, u32[]{:S(2)}) copy-start(bf16[1,15]{1,0:T(2,128)(2,1)} %taps_ref.1) | copy-start | bytes 94
  1.6 13.2 %collective-permute-start = (f32[8,128]{1,0:T(8,128)}, f32[8,128]{1,0:T(8,128)S(1)}, u32[]{:S(2)}, u32[]{:S(2)}) collective-permute-start(f32[8,128]{1,0:T(8,128)} %get-tuple-element.20), channel_id=1, source_target_pairs={{0,1},{1,0},{2,3},{3,2},{4,5},{5,4},{6,7},{7,6},{8,9},{9,8},{10,11... | collective-permute-start | bytes 12296 | tf_op jit(solution)/shard_map/ppermute | solution.py:24
  2.1 12.7 %collective-permute-start.1 = (f32[8,128]{1,0:T(8,128)}, f32[8,128]{1,0:T(8,128)S(1)}, u32[]{:S(2)}, u32[]{:S(2)}) collective-permute-start(f32[8,128]{1,0:T(8,128)} %get-tuple-element.21), channel_id=1, source_target_pairs={{1,2},{3,4},{5,6},{7,8},{9,10},{11,12},{13,14},{15,0},{2,1},{4,3},... | collective-permute-start | bytes 12296 | tf_op jit(solution)/shard_map/ppermute | solution.py:29
  7.8 1.0 %copy-start.2 = (bf16[512,512]{1,0:T(8,128)(2,1)S(1)}, bf16[512,512]{1,0:T(8,128)(2,1)}, u32[]{:S(2)}) copy-start(bf16[512,512]{1,0:T(8,128)(2,1)} %col_warp.1) | copy-start | bytes 1572868
  8.8 0.7 %copy-start.3 = (f32[8,128]{1,0:T(8,128)S(1)}, f32[8,128]{1,0:T(8,128)}, u32[]{:S(2)}) copy-start(f32[8,128]{1,0:T(8,128)} %get-tuple-element.22.own_ref) | copy-start | bytes 12292
  14.9 2.0 %collective-permute-start.2 = (f32[1088,128]{1,0:T(8,128)S(1)}, f32[1088,128]{1,0:T(8,128)S(1)}, u32[]{:S(2)}, u32[]{:S(2)}) collective-permute-start(f32[1088,128]{1,0:T(8,128)S(1)} %shard_map.75), channel_id=1, source_target_pairs={{0,1},{1,0},{2,3},{3,2},{4,5},{5,4},{6,7},{7,6},{8,9},{9,8},{10,11... | collective-permute-start | bytes 1671176 | tf_op jit(solution)/shard_map/ppermute | solution.py:24
  17.0 5.9 %collective-permute-start.3 = (f32[136,128]{1,0:T(8,128)S(1)}, f32[136,128]{1,0:T(8,128)S(1)}, u32[]{:S(2)}, u32[]{:S(2)}) collective-permute-start(f32[136,128]{1,0:T(8,128)S(1)} %get-tuple-element.29), channel_id=1, source_target_pairs={{0,6},{1,7},{2,4},{3,5},{4,2},{5,3},{6,0},{7,1},{8,14},{9,15},{10,... | collective-permute-start | bytes 208904 | tf_op jit(solution)/shard_map/ppermute | solution.py:24
  17.1 7.0 %collective-permute-start.4 = (f32[136,128]{1,0:T(8,128)S(1)}, f32[136,128]{1,0:T(8,128)S(1)}, u32[]{:S(2)}, u32[]{:S(2)}) collective-permute-start(f32[136,128]{1,0:T(8,128)S(1)} %get-tuple-element.30), channel_id=1, source_target_pairs={{0,4},{1,5},{2,6},{3,7},{4,0},{5,1},{6,2},{7,3},{8,12},{9,13},{10,... | collective-permute-start | bytes 208904 | tf_op jit(solution)/shard_map/ppermute | solution.py:24
  17.2 6.9 %collective-permute-start.5 = (f32[136,128]{1,0:T(8,128)S(1)}, f32[136,128]{1,0:T(8,128)S(1)}, u32[]{:S(2)}, u32[]{:S(2)}) collective-permute-start(f32[136,128]{1,0:T(8,128)S(1)} %get-tuple-element.31), channel_id=1, source_target_pairs={{0,2},{1,3},{2,0},{3,1},{4,6},{5,7},{6,4},{7,5},{8,10},{9,11},{10,... | collective-permute-start | bytes 208904 | tf_op jit(solution)/shard_map/ppermute | solution.py:24
  20.6 5.4 %collective-permute-start.7 = (f32[136,128]{1,0:T(8,128)S(1)}, f32[136,128]{1,0:T(8,128)S(1)}, u32[]{:S(2)}, u32[]{:S(2)}) collective-permute-start(f32[136,128]{1,0:T(8,128)S(1)} %get-tuple-element.32), channel_id=1, source_target_pairs={{0,6},{1,7},{2,4},{3,5},{4,2},{5,3},{6,0},{7,1},{8,14},{9,15},{10,... | collective-permute-start | bytes 208904 | tf_op jit(solution)/shard_map/ppermute | solution.py:24
  20.6 5.3 %collective-permute-start.8 = (f32[136,128]{1,0:T(8,128)S(1)}, f32[136,128]{1,0:T(8,128)S(1)}, u32[]{:S(2)}, u32[]{:S(2)}) collective-permute-start(f32[136,128]{1,0:T(8,128)S(1)} %get-tuple-element.33), channel_id=1, source_target_pairs={{0,4},{1,5},{2,6},{3,7},{4,0},{5,1},{6,2},{7,3},{8,12},{9,13},{10,... | collective-permute-start | bytes 208904 | tf_op jit(solution)/shard_map/ppermute | solution.py:24
  22.9 4.3 %collective-permute-start.9 = (f32[136,128]{1,0:T(8,128)S(1)}, f32[136,128]{1,0:T(8,128)S(1)}, u32[]{:S(2)}, u32[]{:S(2)}) collective-permute-start(f32[136,128]{1,0:T(8,128)S(1)} %get-tuple-element.34), channel_id=1, source_target_pairs={{0,2},{1,3},{2,0},{3,1},{4,6},{5,7},{6,4},{7,5},{8,10},{9,11},{10,... | collective-permute-start | bytes 208904 | tf_op jit(solution)/shard_map/ppermute | solution.py:24
  24.1 5.5 %collective-permute-start.6 = (f32[136,128]{1,0:T(8,128)S(1)}, f32[136,128]{1,0:T(8,128)S(1)}, u32[]{:S(2)}, u32[]{:S(2)}) collective-permute-start(f32[136,128]{1,0:T(8,128)S(1)} %shard_map.77), channel_id=1, source_target_pairs={{0,8},{1,9},{2,10},{3,11},{4,12},{5,13},{6,14},{7,15},{8,0},{9,1},... | collective-permute-start | bytes 208904 | tf_op jit(solution)/shard_map/ppermute | solution.py:24

commit v2 on v1

v2 whole, which is shorter than its diff:
```python
import jax
import jax.numpy as jnp
from jax import lax
from jax.experimental import pallas as pl
from jax.experimental.pallas import tpu as pltpu
from jax.sharding import PartitionSpec as P

STRIP = 16
TAPS = 15
PATCH_ROWS = 32
LANES = 128
SUB = 8
CHUNKS = 4
QUAD = 4
VMEM_LIMIT = 32 * 1024 * 1024

f32 = jnp.float32
bf16 = jnp.bfloat16


def in_hbm(array):
    return pltpu.with_memory_space_constraint(array, pltpu.HBM)


def swap(block, mask, count):
    return lax.ppermute(block, "exp", [(i, i ^ mask) for i in range(count)])


def call(body, outs, ins, args, scratch=(), flops=0):
    moved = sum(a.size * a.dtype.itemsize for a in args)
    return pl.pallas_call(
        body,
        out_shape=outs,
        in_specs=ins,
        out_specs=jax.tree.map(lambda _: pl.BlockSpec(memory_space=pltpu.VMEM), outs),
        scratch_shapes=scratch,
        compiler_params=pltpu.CompilerParams(vmem_limit_bytes=VMEM_LIMIT),
        cost_estimate=pl.CostEstimate(flops=flops, bytes_accessed=moved, transcendentals=0),
    )(*args)


def weights_body(
    owner, taps, patch, prow, exposure, col_warp, row_warp,
    ring_ref, own_ref, first_ref, band, cols, rows_ref, select_ref, sums_ref,
    count_ref, blocks_ref,
    owner_ref, taps_ref, patch_ref, prow_ref, first_rows, last_rows, sems,
):
    height, width = exposure.shape
    nb = width // LANES
    count = owner_ref.shape[0]
    moves = [(taps, taps_ref), (owner, owner_ref), (patch, patch_ref), (prow, prow_ref)]
    small = [
        pltpu.make_async_copy(source, to, sems.at[4 + i]) for i, (source, to) in enumerate(moves)
    ]
    copies = [
        pltpu.make_async_copy(exposure.at[pl.ds(0, STRIP)], first_rows, sems.at[0]),
        pltpu.make_async_copy(exposure.at[pl.ds(height - STRIP, STRIP)], last_rows, sems.at[1]),
        pltpu.make_async_copy(col_warp, cols, sems.at[2]),
        pltpu.make_async_copy(row_warp, rows_ref, sems.at[3]),
    ]
    for copy in small + copies:
        copy.start()
    small[0].wait()

    delta = lax.broadcasted_iota(jnp.int32, (LANES, LANES), 0) - lax.broadcasted_iota(
        jnp.int32, (LANES, LANES), 1
    )
    tiles = {}
    for side in (-1, 0, 1):
        offset = delta + side * LANES + (TAPS - 1) // 2
        tile = jnp.zeros((LANES, LANES), f32)
        for tap in range(TAPS):
            tile = jnp.where(offset == tap, taps_ref[0:1, tap : tap + 1].astype(f32), tile)
        tiles[side] = tile.astype(bf16)
    for i in range(nb):
        for k in range(nb):
            tile = tiles.get(i - k, jnp.zeros((LANES, LANES), bf16))
            band[i * LANES : (i + 1) * LANES, k * LANES : (k + 1) * LANES] = tile

    for copy in small[1:]:
        copy.wait()
    me = lax.axis_index("exp")
    patch = patch_ref[...]
    slot = jnp.zeros_like(patch)
    for k in range(count):
        slot = jnp.where(patch == owner_ref[k], place_of(me ^ k, count), slot)
    key = slot * PATCH_ROWS + prow_ref[...]
    slots = lax.broadcasted_iota(jnp.int32, select_ref.shape, 0)
    select_ref[...] = jnp.where(slots == key, 1.0, 0.0).astype(bf16)

    ones = jnp.ones((select_ref.shape[1], LANES), bf16)
    held = jnp.dot(select_ref[...], ones, preferred_element_type=f32)
    lane = lax.broadcasted_iota(jnp.int32, (SUB, LANES), 1)
    for j in range(count):
        tile = jnp.zeros((SUB, LANES), f32)
        for s in range(PATCH_ROWS // SUB):
            at = j * PATCH_ROWS + s * SUB
            tile = jnp.where(lane == s, held[at : at + SUB], tile)
        count_ref[j * SUB : (j + 1) * SUB] = tile

    copies[0].wait()
    copies[1].wait()
    scale = 1.0 / (STRIP * LANES)
    for ref in (ring_ref, own_ref, first_ref):
        ref[...] = jnp.zeros_like(ref)
    for b in range(nb):
        at = slice(b * LANES, (b + 1) * LANES)
        means = []
        for ref in (first_rows, last_rows):
            column = jnp.sum(ref[:, at], axis=0, keepdims=True)
            total = jnp.sum(column, axis=1, keepdims=True)
            means.append(jnp.broadcast_to(total * scale, (1, LANES)))
        first, last = means
        own_ref[b : b + 1] = 0.5 * (first + last)
        first_ref[b : b + 1] = first
        ring_ref[b : b + 1] = last

    copies[2].wait()
    heads = {side: jnp.sum(tile.astype(f32), axis=0, keepdims=True) for side, tile in tiles.items()}
    blank = jnp.zeros((1, LANES), f32)
    lines = [
        jnp.concatenate([heads.get(b - k, blank) for k in range(nb)], axis=1) for b in range(nb)
    ]
    lines.append(jnp.zeros((own_ref.shape[0] - nb, width), f32))
    head = jnp.concatenate(lines, axis=0)
    upper = head.astype(bf16).astype(f32)
    stacked = jnp.concatenate([upper, head - upper], axis=0).astype(bf16)
    both = jnp.dot(stacked, cols[...], preferred_element_type=f32)
    total = both[: head.shape[0]] + both[head.shape[0] :]
    blocks_ref[...] = total
    base = own_ref.shape[0]
    for b in range(nb):
        for c in range(nb):
            to = base + b * nb + c
            ring_ref[to : to + 1] = total[b : b + 1, c * LANES : (c + 1) * LANES]

    copies[3].wait()
    ones = jnp.ones((row_warp.shape[1], LANES), bf16)
    rest = jnp.dot(rows_ref[...], ones, preferred_element_type=f32)
    total = jnp.zeros(sums_ref.shape, f32)
    for _ in range(2):
        part = rest.astype(bf16)
        rest = rest - part.astype(f32)
        total += jnp.dot(select_ref[...], part, preferred_element_type=f32)
    sums_ref[...] = total
    lane = lax.broadcasted_iota(jnp.int32, (PATCH_ROWS, LANES), 1)
    packed = jnp.zeros((PATCH_ROWS, LANES), f32)
    for j in range(count):
        packed = jnp.where(lane == j, total[j * PATCH_ROWS : (j + 1) * PATCH_ROWS], packed)
    ring_ref[ring_ref.shape[0] - PATCH_ROWS :] = packed


def local_body(own_ref, image, band, cols, rows, select, sums_ref, merged, warped):
    height, width = image.shape
    nb = width // LANES
    step = height // CHUNKS
    merged[...] = jnp.dot(band[...], cols[...], preferred_element_type=f32).astype(bf16)
    for i in range(CHUNKS):
        at = slice(i * step, (i + 1) * step)
        parts = []
        for b in range(nb):
            piece = image[at, b * LANES : (b + 1) * LANES] - own_ref[b : b + 1]
            parts.append(piece.astype(bf16))
        centred = jnp.concatenate(parts, axis=1)
        warped[at] = jnp.dot(centred, merged[...], preferred_element_type=f32).astype(bf16)
    values = jnp.dot(rows[...], warped[...], preferred_element_type=f32)
    high = values.astype(bf16)
    low = (values - high.astype(f32)).astype(bf16)
    sums_ref[...] = jnp.dot(select[...], high, preferred_element_type=f32) + jnp.dot(
        select[...], low, preferred_element_type=f32
    )


def place_of(mask, count):
    return (mask & 1) * (count // 2) + lax.shift_right_logical(mask, 1)


class Levels:
    def __init__(self, got_ref, first_ref, blocks_ref, rows_ref, count):
        nb = blocks_ref.shape[1] // LANES
        base = first_ref.shape[0]
        self.count, self.rows_ref = count, rows_ref
        self.packed = got_ref[got_ref.shape[0] - PATCH_ROWS :]
        self.lane = lax.broadcasted_iota(jnp.int32, (PATCH_ROWS, LANES), 1)
        self.own, self.other = [], []
        for c in range(nb):
            own = jnp.zeros((1, LANES), f32)
            other = jnp.zeros((1, LANES), f32)
            for b in range(nb):
                level = 0.5 * got_ref[b : b + 1]
                own += level * blocks_ref[b : b + 1, c * LANES : (c + 1) * LANES]
                at = base + b * nb + c
                other += 0.5 * first_ref[b : b + 1] * got_ref[at : at + 1]
            self.own.append(own)
            self.other.append(other)

    def terms(self, j):
        count = self.count
        me = lax.axis_index("exp")
        mask = (j % (count // 2)) * 2 + j // (count // 2)
        sender = lax.rem(me + count - 1, count)
        place = place_of(sender ^ me ^ mask, count)
        weight = self.rows_ref[j * PATCH_ROWS : (j + 1) * PATCH_ROWS]
        far = jnp.sum(jnp.where(self.lane == place, self.packed, 0.0), axis=1, keepdims=True)
        return [weight * own + far * other for own, other in zip(self.own, self.other)]


def send_body(got_ref, first_ref, blocks_ref, rows_ref, sums_ref, count_ref, out_ref):
    count = count_ref.shape[0] // SUB
    half = count // 2
    size = out_ref.shape[0] // half
    levels = Levels(got_ref, first_ref, blocks_ref, rows_ref, count)
    for j in range(half):
        at = (half + j) * PATCH_ROWS
        terms = levels.terms(half + j)
        for c, term in enumerate(terms):
            to = j * size + c * PATCH_ROWS
            part = sums_ref[at : at + PATCH_ROWS, c * LANES : (c + 1) * LANES]
            out_ref[to : to + PATCH_ROWS] = part + term
        to = j * size + len(terms) * PATCH_ROWS
        out_ref[to : to + SUB] = count_ref[(half + j) * SUB : (half + j + 1) * SUB]


def merge_body(
    got_ref, first_ref, blocks_ref, rows_ref, sums_ref, count_ref, half_ref, *out_refs
):
    count = count_ref.shape[0] // SUB
    half = count // 2
    size = half_ref.shape[0] // half
    levels = Levels(got_ref, first_ref, blocks_ref, rows_ref, count)
    for j in range(half):
        quad, far = j % QUAD, j // QUAD
        ref = out_refs[quad] if far == 0 else out_refs[QUAD + quad]
        base = 0 if far == 0 else (far - 1) * size
        at = j * PATCH_ROWS
        terms = levels.terms(j)
        for c, term in enumerate(terms):
            to = c * PATCH_ROWS
            part = sums_ref[at : at + PATCH_ROWS, c * LANES : (c + 1) * LANES]
            got = half_ref[j * size + to : j * size + to + PATCH_ROWS]
            ref[base + to : base + to + PATCH_ROWS] = part + term + got
        to = len(terms) * PATCH_ROWS
        got = half_ref[j * size + to : j * size + to + SUB]
        ref[base + to : base + to + SUB] = count_ref[j * SUB : (j + 1) * SUB] + got


def far_body(a_ref, b_ref, c_ref, d_ref, *out_refs):
    size = out_refs[0].shape[0]
    for i, ref in enumerate(out_refs):
        at = slice(i * size, (i + 1) * size)
        ref[...] = (a_ref[at] + b_ref[at]) + (c_ref[at] + d_ref[at])


def final_body(*refs):
    out_ref = refs[-1]
    total = refs[0][...]
    for ref in refs[1:-1]:
        total = total + ref[...]
    nb = out_ref.shape[1] // LANES
    held = total[nb * PATCH_ROWS :]
    for s in range(PATCH_ROWS // SUB):
        number = jnp.maximum(held[:, s : s + 1], 1.0)
        for c in range(nb):
            at = c * PATCH_ROWS + s * SUB
            out_ref[s * SUB : (s + 1) * SUB, c * LANES : (c + 1) * LANES] = (
                total[at : at + SUB] / number
            )


def on_device(exposure, psf_taps, col_warp, row_warp, row_patch, row_prow, owner_map):
    height, width = exposure.shape
    out_rows = row_warp.shape[0]
    count = lax.axis_size("exp")
    nb = width // LANES
    slots = count * PATCH_ROWS
    half, high_groups = count // 2, count // (2 * QUAD)
    size = PATCH_ROWS * nb + SUB
    vmem = pl.BlockSpec(memory_space=pltpu.VMEM)
    hbm = pl.BlockSpec(memory_space=pltpu.HBM)

    def shape(*dims):
        return jax.ShapeDtypeStruct(dims, f32)

    tile = shape(-(-nb // SUB) * SUB, LANES)
    ring, own, first, band, cols, rows, select, weights, held, blocks = call(
        weights_body,
        [shape(tile.shape[0] + nb * nb + PATCH_ROWS, LANES), tile, tile,
         jax.ShapeDtypeStruct((width, width), bf16), jax.ShapeDtypeStruct(col_warp.shape, bf16),
         jax.ShapeDtypeStruct(row_warp.shape, bf16),
         jax.ShapeDtypeStruct((slots, out_rows), bf16), shape(slots, LANES),
         shape(count * SUB, LANES), shape(tile.shape[0], width)],
        [hbm] * 7,
        tuple(in_hbm(array) for array in (
            owner_map, psf_taps, row_patch.reshape(1, out_rows), row_prow.reshape(1, out_rows),
            exposure, col_warp, row_warp,
        )),
        scratch=[
            pltpu.SMEM(owner_map.shape, jnp.int32),
            pltpu.VMEM(psf_taps.shape, bf16),
            pltpu.VMEM((1, out_rows), jnp.int32),
            pltpu.VMEM((1, out_rows), jnp.int32),
            pltpu.VMEM((STRIP, width), f32),
            pltpu.VMEM((STRIP, width), f32),
            pltpu.SemaphoreType.DMA((8,)),
        ],
        flops=2 * width * width * width,
    )
    ring = lax.ppermute(ring, "exp", [(i, (i + 1) % count) for i in range(count)])
    sums = call(
        local_body, shape(slots, width), [vmem] * 6,
        (own, exposure, band, cols, rows, select),
        scratch=[pltpu.VMEM((width, width), bf16), pltpu.VMEM((height, width), bf16)],
        flops=2 * height * width * (width + out_rows) + 4 * slots * out_rows * width,
    )
    common = (ring, first, blocks, weights, sums, held)
    send = call(send_body, shape(half * size, LANES), [vmem] * 6, common)
    got = swap(send, 1, count)

    shapes = [shape(size, LANES)] * QUAD
    if high_groups > 1:
        shapes += [shape((high_groups - 1) * size, LANES)] * QUAD
    parts = call(merge_body, shapes, [vmem] * 7, common + (got,))
    near, far = parts[:QUAD], parts[QUAD:]
    terms = [near[0]]
    if high_groups > 1:
        far = [far[0]] + [swap(far[q], 2 * q, count) for q in range(QUAD - 1, 0, -1)]
    near_got = [swap(near[q], 2 * q, count) for q in range(QUAD - 1, 0, -1)]
    if high_groups > 1:
        sent = call(far_body, [shape(size, LANES)] * (high_groups - 1), [vmem] * QUAD, far)
        terms += [swap(sent[h - 1], 2 * QUAD * h, count) for h in range(1, high_groups)]
    terms += near_got
    return call(final_body, shape(PATCH_ROWS, width), [vmem] * len(terms), tuple(terms))


def solution(mesh):
    placed = (
        P(("band", "exp"), None),
        P(("band", "exp"), None),
        P(("band", "exp"), None),
        P(("band", "exp"), None),
        P(("band", "exp"), None),
        P(("band", "exp")),
        P("band"),
    )
    return jax.shard_map(
        on_device, mesh=mesh, in_specs=placed, out_specs=P(("band", "exp"), None), check_vma=False
    )
```

time: 30.4 us -> 26.4 us (0.87)
  starting transfers between devices: 12.6 us -> 8.16 us
  waiting for transfers between devices: 8.05 us -> 11.5 us
  local copies, waits for them, and re-layouts: 1.73 us -> 0.01 us
  Pallas kernels: 7.79 us -> 6.62 us
    ppermute x1, starting transfers between devices: 5.64 us -> 0.5 us  [on_device(): lax.ppermute(ring, 'exp', [(i, (i + 1) % count) for i in range(count)])]
    ppermute x1, waiting for transfers between devices: 0.01 us -> 4.27 us  [on_device(): lax.ppermute(ring, 'exp', [(i, (i + 1) % count) for i in range(count)])]
    unnamed x16 -> x2, local copies, waits for them, and re-layouts: 1.73 us -> 0.01 us
    pallas_call x1 -> x0, Pallas kernels: 1.62 us -> none  [on_device(): pl.pallas_call(strips_body, grid=(1,), out_shape=[tile, tile, tile], in_s...]
    ppermute x9 -> x8, waiting for transfers between devices: 8.04 us -> 7.2 us  [swap(): return lax.ppermute(block, 'exp', [(i, i ^ mask) for i in range(count)])]
    ppermute x9 -> x8, starting transfers between devices: 6.93 us -> 7.65 us  [swap(): return lax.ppermute(block, 'exp', [(i, i ^ mask) for i in range(count)])]
    pallas_call x5 -> x6, Pallas kernels: 6.17 us -> 6.62 us  [call(): pl.pallas_call(body, out_shape=outs, in_specs=ins, out_specs=jax.tree.map...]
  transfers between devices with their start and end apart: 10 -> 9, of which waited for: 5 -> 6; matrix products, arithmetic and copies ran while one was open for 0% -> 0% of each run, Pallas kernels for 18% -> 9%
where the time goes in v2:
time: 26.4 us; the launch traced here: 26.3 us
  waiting for transfers between devices  11.5 us (44%)
  starting transfers between devices  8.16 us (31%)
  Pallas kernels  6.62 us (25%)
    ppermute x8, starting transfers between devices, swap(): return lax.ppermute(block, 'exp', [(i, i ^ mask) for i in range(count)])  7.65 us
    ppermute x8, waiting for transfers between devices, swap(): return lax.ppermute(block, 'exp', [(i, i ^ mask) for i in range(count)])  7.2 us
    pallas_call x6, Pallas kernels, call(): pl.pallas_call(body, out_shape=outs, in_specs=ins, out_specs=jax.tree.map...  6.62 us
    ppermute x1, waiting for transfers between devices, on_device(): lax.ppermute(ring, 'exp', [(i, (i + 1) % count) for i in range(count)])  4.27 us
  transfers between devices with their start and end apart: 9, of which 6 were waited for; matrix products, arithmetic and copies ran while one was open for 0% of the time, Pallas kernels for 9%

profile of v2, /device:TPU:0, one launch (start us, length us, event | category | flops | bytes accessed | tf_op | source)
XLA Modules:
  0.0 26.3 jit_solution(1548006824845552897)
XLA Ops:
  0.0 0.0 copy-start
  0.0 3.3 %shard_map.73 = (f32[56,128]{1,0:T(8,128)S(1)}, f32[8,128]{1,0:T(8,128)S(1)}, f32[8,128]{1,0:T(8,128)S(1)}, bf16[512,512]{1,0:T(8,128)(2,1)S(1)}, bf16[512,512]{...) custom-call(s32[16]{0:T(128)} %owner.1, ...), custom_call_target="tpu_custom_call" | custom-call | flops 268435456 | bytes 3674206 | tf_op jit(solution)/shard_map/pallas_call | solution.py:31
  3.3 0.5 %collective-permute-start = (f32[56,128]{1,0:T(8,128)S(1)}, f32[56,128]{1,0:T(8,128)S(1)}, u32[]{:S(2)}, u32[]{:S(2)}) collective-permute-start(f32[56,128]{1,0:T(8,128)S(1)} %get-tuple-element.23), channel_id=1, source_target_pairs={{0,1},{1,2},{2,3},{3,4},{4,5},{5,6},{6,7},{7,8},{8,9},{9,10},{10,1... | collective-permute-start | bytes 86024 | tf_op jit(solution)/shard_map/ppermute | solution.py:308
  3.8 0.0 copy-done
  3.8 2.2 %shard_map.74.sums_ref = f32[512,512]{1,0:T(8,128)S(1)} custom-call(f32[8,128]{1,0:T(8,128)S(1)} %get-tuple-element.27.own_ref, f32[1024,512]{1,0:T(8,128)S(1)} %copy-done, bf16[512,512]{1,0:T(8,128)(2,1)S(1)} %get-tuple-element.28.band, bf16[512,512]{1,0:T(8,128)(2,1)S(1)} %get-tuple-element.29.cols, bf16[512,1024]{1,0:T(8,128)(2,1)S(1)} %get-tuple-element.30.rows, ...), custom_call_target="tpu_custom_call" | custom-call | flops 1610612736 | bytes 4722688 | tf_op jit(solution)/shard_map/pallas_call | solution.py:31
  6.1 4.3 %collective-permute-done.got_ref = f32[56,128]{1,0:T(8,128)S(1)} collective-permute-done((f32[56,128]{1,0:T(8,128)S(1)}, f32[56,128]{1,0:T(8,128)S(1)}, u32[]{:S(2)}, u32[]{:S(2)}) %collective-permute-start) | collective-permute-done | bytes 28704 | tf_op jit(solution)/shard_map/ppermute | solution.py:308
  10.4 0.2 shard_map.75
  10.5 0.1 collective-permute-start.1
  10.6 1.9 %collective-permute-done.1.half_ref = f32[1088,128]{1,0:T(8,128)S(1)} collective-permute-done((f32[1088,128]{1,0:T(8,128)S(1)}, f32[1088,128]{1,0:T(8,128)S(1)}, u32[]{:S(2)}, u32[]{:S(2)}) %collective-permute-start.1) | collective-permute-done | bytes 557088 | tf_op jit(solution)/shard_map/ppermute | solution.py:26
  12.5 0.2 shard_map.76
  12.7 0.6 %collective-permute-start.2 = (f32[136,128]{1,0:T(8,128)S(1)}, f32[136,128]{1,0:T(8,128)S(1)}, u32[]{:S(2)}, u32[]{:S(2)}) collective-permute-start(f32[136,128]{1,0:T(8,128)S(1)} %get-tuple-element.35), channel_id=1, source_target_pairs={{0,6},{1,7},{2,4},{3,5},{4,2},{5,3},{6,0},{7,1},{8,14},{9,15},{10,... | collective-permute-start | bytes 208904 | tf_op jit(solution)/shard_map/ppermute | solution.py:26
  13.3 0.4 %collective-permute-start.3 = (f32[136,128]{1,0:T(8,128)S(1)}, f32[136,128]{1,0:T(8,128)S(1)}, u32[]{:S(2)}, u32[]{:S(2)}) collective-permute-start(f32[136,128]{1,0:T(8,128)S(1)} %get-tuple-element.36), channel_id=1, source_target_pairs={{0,4},{1,5},{2,6},{3,7},{4,0},{5,1},{6,2},{7,3},{8,12},{9,13},{10,... | collective-permute-start | bytes 208904 | tf_op jit(solution)/shard_map/ppermute | solution.py:26
  13.8 2.5 %collective-permute-start.4 = (f32[136,128]{1,0:T(8,128)S(1)}, f32[136,128]{1,0:T(8,128)S(1)}, u32[]{:S(2)}, u32[]{:S(2)}) collective-permute-start(f32[136,128]{1,0:T(8,128)S(1)} %get-tuple-element.37), channel_id=1, source_target_pairs={{0,2},{1,3},{2,0},{3,1},{4,6},{5,7},{6,4},{7,5},{8,10},{9,11},{10,... | collective-permute-start | bytes 208904 | tf_op jit(solution)/shard_map/ppermute | solution.py:26
  16.3 0.6 %collective-permute-start.6 = (f32[136,128]{1,0:T(8,128)S(1)}, f32[136,128]{1,0:T(8,128)S(1)}, u32[]{:S(2)}, u32[]{:S(2)}) collective-permute-start(f32[136,128]{1,0:T(8,128)S(1)} %get-tuple-element.38), channel_id=1, source_target_pairs={{0,6},{1,7},{2,4},{3,5},{4,2},{5,3},{6,0},{7,1},{8,14},{9,15},{10,... | collective-permute-start | bytes 208904 | tf_op jit(solution)/shard_map/ppermute | solution.py:26
  16.8 0.9 %collective-permute-start.7 = (f32[136,128]{1,0:T(8,128)S(1)}, f32[136,128]{1,0:T(8,128)S(1)}, u32[]{:S(2)}, u32[]{:S(2)}) collective-permute-start(f32[136,128]{1,0:T(8,128)S(1)} %get-tuple-element.39), channel_id=1, source_target_pairs={{0,4},{1,5},{2,6},{3,7},{4,0},{5,1},{6,2},{7,3},{8,12},{9,13},{10,... | collective-permute-start | bytes 208904 | tf_op jit(solution)/shard_map/ppermute | solution.py:26
  17.7 0.9 %collective-permute-done.2.b_ref = f32[136,128]{1,0:T(8,128)S(1)} collective-permute-done((f32[136,128]{1,0:T(8,128)S(1)}, f32[136,128]{1,0:T(8,128)S(1)}, u32[]{:S(2)}, u32[]{:S(2)}) %collective-permute-start.2) | collective-permute-done | bytes 69664 | tf_op jit(solution)/shard_map/ppermute | solution.py:26
  18.7 1.1 %collective-permute-start.8 = (f32[136,128]{1,0:T(8,128)S(1)}, f32[136,128]{1,0:T(8,128)S(1)}, u32[]{:S(2)}, u32[]{:S(2)}) collective-permute-start(f32[136,128]{1,0:T(8,128)S(1)} %get-tuple-element.40), channel_id=1, source_target_pairs={{0,2},{1,3},{2,0},{3,1},{4,6},{5,7},{6,4},{7,5},{8,10},{9,11},{10,... | collective-permute-start | bytes 208904 | tf_op jit(solution)/shard_map/ppermute | solution.py:26
  19.8 0.0 collective-permute-done.3.c_ref
  19.8 0.0 collective-permute-done.4.d_ref
  19.8 1.5 %collective-permute-start.5 = (f32[136,128]{1,0:T(8,128)S(1)}, f32[136,128]{1,0:T(8,128)S(1)}, u32[]{:S(2)}, u32[]{:S(2)}) collective-permute-start(f32[136,128]{1,0:T(8,128)S(1)} %shard_map.77), channel_id=1, source_target_pairs={{0,8},{1,9},{2,10},{3,11},{4,12},{5,13},{6,14},{7,15},{8,0},{9,1},... | collective-permute-start | bytes 208904 | tf_op jit(solution)/shard_map/ppermute | solution.py:26
  21.2 0.4 %collective-permute-done.6.refs_2_ = f32[136,128]{1,0:T(8,128)S(1)} collective-permute-done((f32[136,128]{1,0:T(8,128)S(1)}, f32[136,128]{1,0:T(8,128)S(1)}, u32[]{:S(2)}, u32[]{:S(2)}) %collective-permute-start.6) | collective-permute-done | bytes 69664 | tf_op jit(solution)/shard_map/ppermute | solution.py:26
  21.6 0.0 collective-permute-done.7.refs_3_
  21.6 1.3 %collective-permute-done.8.refs_4_ = f32[136,128]{1,0:T(8,128)S(1)} collective-permute-done((f32[136,128]{1,0:T(8,128)S(1)}, f32[136,128]{1,0:T(8,128)S(1)}, u32[]{:S(2)}, u32[]{:S(2)}) %collective-permute-start.8) | collective-permute-done | bytes 69664 | tf_op jit(solution)/shard_map/ppermute | solution.py:26
  23.0 2.6 %collective-permute-done.5.refs_1_ = f32[136,128]{1,0:T(8,128)S(1)} collective-permute-done((f32[136,128]{1,0:T(8,128)S(1)}, f32[136,128]{1,0:T(8,128)S(1)}, u32[]{:S(2)}, u32[]{:S(2)}) %collective-permute-start.5) | collective-permute-done | bytes 69664 | tf_op jit(solution)/shard_map/ppermute | solution.py:26
  25.6 0.7 %shard_map.78 = f32[32,512]{1,0:T(8,128)} custom-call(f32[136,128]{1,0:T(8,128)S(1)} %get-tuple-element.33.refs_0_, f32[136,128]{1,0:T(8,128)S(1)} %collective-permute-done.5.refs_1_, f32[136,128]{1,0:T(8,128)S(1)} %collective-permute-done.6.refs_2_, f32[136,128]{1,0:T(8,128)S(1)} %collective-permute-done.7.refs_3_, ...), custom_call_target="tpu_custom_call" | custom-call | bytes 348160 | tf_op jit(solution)/shard_map/pallas_call | solution.py:31
  (1 shorter events, 0.0 us)
Async XLA Ops:
  0.0 3.8 %copy-start = (f32[1024,512]{1,0:T(8,128)S(1)}, f32[1024,512]{1,0:T(8,128)}, u32[]{:S(2)}) copy-start(f32[1024,512]{1,0:T(8,128)} %image.1) | copy-start | bytes 6291460
  3.3 7.0 %collective-permute-start = (f32[56,128]{1,0:T(8,128)S(1)}, f32[56,128]{1,0:T(8,128)S(1)}, u32[]{:S(2)}, u32[]{:S(2)}) collective-permute-start(f32[56,128]{1,0:T(8,128)S(1)} %get-tuple-element.23), channel_id=1, source_target_pairs={{0,1},{1,2},{2,3},{3,4},{4,5},{5,6},{6,7},{7,8},{8,9},{9,10},{10,1... | collective-permute-start | bytes 86024 | tf_op jit(solution)/shard_map/ppermute | solution.py:308
  10.5 2.0 %collective-permute-start.1 = (f32[1088,128]{1,0:T(8,128)S(1)}, f32[1088,128]{1,0:T(8,128)S(1)}, u32[]{:S(2)}, u32[]{:S(2)}) collective-permute-start(f32[1088,128]{1,0:T(8,128)S(1)} %shard_map.75), channel_id=1, source_target_pairs={{0,1},{1,0},{2,3},{3,2},{4,5},{5,4},{6,7},{7,6},{8,9},{9,8},{10,11... | collective-permute-start | bytes 1671176 | tf_op jit(solution)/shard_map/ppermute | solution.py:26
  12.7 5.9 %collective-permute-start.2 = (f32[136,128]{1,0:T(8,128)S(1)}, f32[136,128]{1,0:T(8,128)S(1)}, u32[]{:S(2)}, u32[]{:S(2)}) collective-permute-start(f32[136,128]{1,0:T(8,128)S(1)} %get-tuple-element.35), channel_id=1, source_target_pairs={{0,6},{1,7},{2,4},{3,5},{4,2},{5,3},{6,0},{7,1},{8,14},{9,15},{10,... | collective-permute-start | bytes 208904 | tf_op jit(solution)/shard_map/ppermute | solution.py:26
  13.3 6.4 %collective-permute-start.3 = (f32[136,128]{1,0:T(8,128)S(1)}, f32[136,128]{1,0:T(8,128)S(1)}, u32[]{:S(2)}, u32[]{:S(2)}) collective-permute-start(f32[136,128]{1,0:T(8,128)S(1)} %get-tuple-element.36), channel_id=1, source_target_pairs={{0,4},{1,5},{2,6},{3,7},{4,0},{5,1},{6,2},{7,3},{8,12},{9,13},{10,... | collective-permute-start | bytes 208904 | tf_op jit(solution)/shard_map/ppermute | solution.py:26
  13.8 6.0 %collective-permute-start.4 = (f32[136,128]{1,0:T(8,128)S(1)}, f32[136,128]{1,0:T(8,128)S(1)}, u32[]{:S(2)}, u32[]{:S(2)}) collective-permute-start(f32[136,128]{1,0:T(8,128)S(1)} %get-tuple-element.37), channel_id=1, source_target_pairs={{0,2},{1,3},{2,0},{3,1},{4,6},{5,7},{6,4},{7,5},{8,10},{9,11},{10,... | collective-permute-start | bytes 208904 | tf_op jit(solution)/shard_map/ppermute | solution.py:26
  16.3 5.4 %collective-permute-start.6 = (f32[136,128]{1,0:T(8,128)S(1)}, f32[136,128]{1,0:T(8,128)S(1)}, u32[]{:S(2)}, u32[]{:S(2)}) collective-permute-start(f32[136,128]{1,0:T(8,128)S(1)} %get-tuple-element.38), channel_id=1, source_target_pairs={{0,6},{1,7},{2,4},{3,5},{4,2},{5,3},{6,0},{7,1},{8,14},{9,15},{10,... | collective-permute-start | bytes 208904 | tf_op jit(solution)/shard_map/ppermute | solution.py:26
  16.8 4.8 %collective-permute-start.7 = (f32[136,128]{1,0:T(8,128)S(1)}, f32[136,128]{1,0:T(8,128)S(1)}, u32[]{:S(2)}, u32[]{:S(2)}) collective-permute-start(f32[136,128]{1,0:T(8,128)S(1)} %get-tuple-element.39), channel_id=1, source_target_pairs={{0,4},{1,5},{2,6},{3,7},{4,0},{5,1},{6,2},{7,3},{8,12},{9,13},{10,... | collective-permute-start | bytes 208904 | tf_op jit(solution)/shard_map/ppermute | solution.py:26
  18.7 4.3 %collective-permute-start.8 = (f32[136,128]{1,0:T(8,128)S(1)}, f32[136,128]{1,0:T(8,128)S(1)}, u32[]{:S(2)}, u32[]{:S(2)}) collective-permute-start(f32[136,128]{1,0:T(8,128)S(1)} %get-tuple-element.40), channel_id=1, source_target_pairs={{0,2},{1,3},{2,0},{3,1},{4,6},{5,7},{6,4},{7,5},{8,10},{9,11},{10,... | collective-permute-start | bytes 208904 | tf_op jit(solution)/shard_map/ppermute | solution.py:26
  19.8 5.8 %collective-permute-start.5 = (f32[136,128]{1,0:T(8,128)S(1)}, f32[136,128]{1,0:T(8,128)S(1)}, u32[]{:S(2)}, u32[]{:S(2)}) collective-permute-start(f32[136,128]{1,0:T(8,128)S(1)} %shard_map.77), channel_id=1, source_target_pairs={{0,8},{1,9},{2,10},{3,11},{4,12},{5,13},{6,14},{7,15},{8,0},{9,1},... | collective-permute-start | bytes 208904 | tf_op jit(solution)/shard_map/ppermute | solution.py:26

commit v3 on v2

v3 whole, which is shorter than its diff:
```python
import jax
import jax.numpy as jnp
from jax import lax
from jax.experimental import pallas as pl
from jax.experimental.pallas import tpu as pltpu
from jax.sharding import PartitionSpec as P

STRIP = 16
TAPS = 15
PATCH_ROWS = 32
LANES = 128
SUB = 8
CHUNKS = 4
QUAD = 4
VMEM_LIMIT = 32 * 1024 * 1024

f32 = jnp.float32
bf16 = jnp.bfloat16


def in_hbm(array):
    return pltpu.with_memory_space_constraint(array, pltpu.HBM)


def swap(block, mask, count):
    return lax.ppermute(block, "exp", [(i, i ^ mask) for i in range(count)])


def call(body, outs, ins, args, scratch=(), flops=0):
    moved = sum(a.size * a.dtype.itemsize for a in args)
    return pl.pallas_call(
        body,
        out_shape=outs,
        in_specs=ins,
        out_specs=jax.tree.map(lambda _: pl.BlockSpec(memory_space=pltpu.VMEM), outs),
        scratch_shapes=scratch,
        compiler_params=pltpu.CompilerParams(vmem_limit_bytes=VMEM_LIMIT),
        cost_estimate=pl.CostEstimate(flops=flops, bytes_accessed=moved, transcendentals=0),
    )(*args)


def lane_dot(left, right):
    return lax.dot_general(left, right, (((1,), (1,)), ((), ())), preferred_element_type=f32)


def parts_of(values):
    high = values.astype(bf16)
    return high, (values - high.astype(f32)).astype(bf16)


def band_tiles(taps):
    half = (TAPS - 1) // 2
    delta = lax.broadcasted_iota(jnp.int32, (LANES, LANES), 0) - lax.broadcasted_iota(
        jnp.int32, (LANES, LANES), 1
    )
    middle = jnp.zeros((LANES, LANES), f32)
    upper = jnp.zeros((SUB, LANES), f32)
    lower = jnp.zeros((SUB, LANES), f32)
    for tap in range(TAPS):
        value = jnp.broadcast_to(taps[:, tap : tap + 1], (1, LANES))
        middle = jnp.where(delta == tap - half, value, middle)
        if tap > half:
            upper = jnp.where(delta[:SUB] == tap - half - LANES, value, upper)
        if tap < half:
            lower = jnp.where(delta[LANES - SUB :] == tap - half + LANES, value, lower)
    rest = jnp.zeros((LANES - SUB, LANES), f32)
    return {
        0: middle,
        -1: jnp.concatenate([rest, lower], axis=0),
        1: jnp.concatenate([upper, rest], axis=0),
    }


def weights_body(
    owner, taps, patch, prow, exposure, col_warp, row_warp,
    ring_ref, own_ref, first_ref, merged_ref, rows_ref, select_ref, lines_ref, blocks_ref,
    owner_ref, taps_ref, patch_ref, prow_ref, first_rows, last_rows, cols, band, sems,
):
    height, width = exposure.shape
    nb = width // LANES
    count = owner_ref.shape[0]
    moves = [
        (taps, taps_ref), (owner, owner_ref), (patch, patch_ref), (prow, prow_ref),
        (col_warp, cols),
        (exposure.at[pl.ds(0, STRIP)], first_rows),
        (exposure.at[pl.ds(height - STRIP, STRIP)], last_rows),
        (row_warp, rows_ref),
    ]
    copies = [pltpu.make_async_copy(*move, sems.at[i]) for i, move in enumerate(moves)]
    for copy in copies:
        copy.start()

    copies[0].wait()
    tiles = band_tiles(taps_ref[...].astype(f32))
    tiles = {side: tile.astype(bf16) for side, tile in tiles.items()}
    for i in range(nb):
        for k in range(nb):
            tile = tiles.get(k - i, jnp.zeros((LANES, LANES), bf16))
            band[k * LANES : (k + 1) * LANES, i * LANES : (i + 1) * LANES] = tile

    for copy in copies[1:4]:
        copy.wait()
    me = lax.axis_index("exp")
    patch = patch_ref[...]
    slot = jnp.zeros_like(patch)
    for k in range(count):
        slot = jnp.where(patch == owner_ref[k], place_of(me ^ k, count), slot)
    key = slot * PATCH_ROWS + prow_ref[...]
    slots = lax.broadcasted_iota(jnp.int32, select_ref.shape, 0)
    select_ref[...] = jnp.where(slots == key, 1.0, 0.0).astype(bf16)

    copies[4].wait()
    both = jnp.dot(band[...], cols[...], preferred_element_type=f32)
    merged_ref[...] = both.astype(bf16)
    for ref in (ring_ref, own_ref, first_ref, blocks_ref, lines_ref):
        ref[...] = jnp.zeros_like(ref)
    base = own_ref.shape[0]
    for b in range(nb):
        total = jnp.sum(both[b * LANES : (b + 1) * LANES], axis=0, keepdims=True)
        blocks_ref[b : b + 1] = total
        for c in range(nb):
            to = base + b * nb + c
            ring_ref[to : to + 1] = total[:, c * LANES : (c + 1) * LANES]

    copies[5].wait()
    copies[6].wait()
    scale = 1.0 / (STRIP * LANES)
    for b in range(nb):
        at = slice(b * LANES, (b + 1) * LANES)
        means = []
        for ref in (first_rows, last_rows):
            column = jnp.sum(ref[:, at], axis=0, keepdims=True)
            total = jnp.sum(column, axis=1, keepdims=True)
            means.append(jnp.broadcast_to(total * scale, (1, LANES)))
        first, last = means
        own_ref[b : b + 1] = 0.5 * (first + last)
        first_ref[b : b + 1] = first
        ring_ref[b : b + 1] = last

    copies[7].wait()
    partial = rows_ref[:, :LANES].astype(f32)
    for i in range(1, height // LANES):
        partial += rows_ref[:, i * LANES : (i + 1) * LANES].astype(f32)
    ones = jnp.ones((2 * SUB, LANES), bf16)
    high, low = parts_of(partial)
    high, low = parts_of(lane_dot(ones, high) + lane_dot(ones, low))
    line = lax.broadcasted_iota(jnp.int32, high.shape, 0)
    left = jnp.where(line == 0, high.astype(f32), jnp.where(line == 1, low.astype(f32), 1.0))
    found = lane_dot(left.astype(bf16), select_ref[...])
    weight = found[0:1] + found[1:2]
    lines_ref[0:1] = weight
    lines_ref[1:2] = found[2:3]
    base += nb * nb
    for i in range(weight.shape[1] // LANES):
        ring_ref[base + i : base + i + 1] = weight[:, i * LANES : (i + 1) * LANES]


def local_body(own_ref, image, merged, rows, select, sums_ref, warped):
    height, width = image.shape
    nb = width // LANES
    step = height // CHUNKS
    for i in range(CHUNKS):
        at = slice(i * step, (i + 1) * step)
        parts = []
        for b in range(nb):
            piece = image[at, b * LANES : (b + 1) * LANES] - own_ref[b : b + 1]
            parts.append(piece.astype(bf16))
        centred = jnp.concatenate(parts, axis=1)
        warped[at] = jnp.dot(centred, merged[...], preferred_element_type=f32).astype(bf16)
    values = jnp.dot(rows[...], warped[...], preferred_element_type=f32)
    high, low = parts_of(values)
    sums_ref[...] = jnp.dot(select[...], high, preferred_element_type=f32) + jnp.dot(
        select[...], low, preferred_element_type=f32
    )


def place_of(mask, count):
    return (mask & 1) * (count // 2) + lax.shift_right_logical(mask, 1)


def upright(line, start):
    shape = (PATCH_ROWS, LANES)
    wanted = lax.broadcasted_iota(jnp.int32, shape, 1) == start + lax.broadcasted_iota(
        jnp.int32, shape, 0
    )
    return jnp.sum(jnp.where(wanted, line, 0.0), axis=1, keepdims=True)


class Levels:
    def __init__(self, got_ref, first_ref, blocks_ref, lines_ref, count):
        nb = blocks_ref.shape[1] // LANES
        base = first_ref.shape[0]
        self.count, self.lines_ref, self.got_ref = count, lines_ref, got_ref
        self.base = base + nb * nb
        self.own, self.other = [], []
        for c in range(nb):
            own = jnp.zeros((1, LANES), f32)
            other = jnp.zeros((1, LANES), f32)
            for b in range(nb):
                level = 0.5 * got_ref[b : b + 1]
                own += level * blocks_ref[b : b + 1, c * LANES : (c + 1) * LANES]
                at = base + b * nb + c
                other += 0.5 * first_ref[b : b + 1] * got_ref[at : at + 1]
            self.own.append(own)
            self.other.append(other)

    def terms(self, j):
        count, each = self.count, LANES // PATCH_ROWS
        me = lax.axis_index("exp")
        mask = (j % (count // 2)) * 2 + j // (count // 2)
        sender = lax.rem(me + count - 1, count)
        place = place_of(sender ^ me ^ mask, count)
        at = j // each * LANES
        weight = upright(self.lines_ref[0:1, at : at + LANES], j % each * PATCH_ROWS)
        line = self.got_ref[pl.ds(self.base + place // each, 1)]
        far = upright(line, lax.rem(place, each) * PATCH_ROWS)
        return [weight * own + far * other for own, other in zip(self.own, self.other)]

    def held(self, j):
        each = LANES // PATCH_ROWS
        at = j // each * LANES
        line = jnp.broadcast_to(self.lines_ref[1:2, at : at + LANES], (SUB, LANES))
        start = j % each * PATCH_ROWS
        return pltpu.roll(line, LANES - start, 1) if start else line


def send_body(got_ref, first_ref, blocks_ref, lines_ref, sums_ref, out_ref):
    count = sums_ref.shape[0] // PATCH_ROWS
    half = count // 2
    size = out_ref.shape[0] // half
    levels = Levels(got_ref, first_ref, blocks_ref, lines_ref, count)
    for j in range(half):
        at = (half + j) * PATCH_ROWS
        terms = levels.terms(half + j)
        for c, term in enumerate(terms):
            to = j * size + c * PATCH_ROWS
            part = sums_ref[at : at + PATCH_ROWS, c * LANES : (c + 1) * LANES]
            out_ref[to : to + PATCH_ROWS] = part + term
        to = j * size + len(terms) * PATCH_ROWS
        out_ref[to : to + SUB] = levels.held(half + j)


def merge_body(got_ref, first_ref, blocks_ref, lines_ref, sums_ref, half_ref, *out_refs):
    count = sums_ref.shape[0] // PATCH_ROWS
    half = count // 2
    size = half_ref.shape[0] // half
    levels = Levels(got_ref, first_ref, blocks_ref, lines_ref, count)
    for j in range(half):
        quad, far = j % QUAD, j // QUAD
        ref = out_refs[quad] if far == 0 else out_refs[QUAD + quad]
        base = 0 if far == 0 else (far - 1) * size
        at = j * PATCH_ROWS
        terms = levels.terms(j)
        for c, term in enumerate(terms):
            to = c * PATCH_ROWS
            part = sums_ref[at : at + PATCH_ROWS, c * LANES : (c + 1) * LANES]
            got = half_ref[j * size + to : j * size + to + PATCH_ROWS]
            ref[base + to : base + to + PATCH_ROWS] = part + term + got
        to = len(terms) * PATCH_ROWS
        got = half_ref[j * size + to : j * size + to + SUB]
        ref[base + to : base + to + SUB] = levels.held(j) + got


def far_body(a_ref, b_ref, c_ref, d_ref, *out_refs):
    size = out_refs[0].shape[0]
    for i, ref in enumerate(out_refs):
        at = slice(i * size, (i + 1) * size)
        ref[...] = (a_ref[at] + b_ref[at]) + (c_ref[at] + d_ref[at])


def final_body(*refs):
    out_ref = refs[-1]
    total = refs[0][...]
    for ref in refs[1:-1]:
        total = total + ref[...]
    nb = out_ref.shape[1] // LANES
    number = jnp.maximum(upright(total[nb * PATCH_ROWS : nb * PATCH_ROWS + 1], 0), 1.0)
    for c in range(nb):
        part = total[c * PATCH_ROWS : (c + 1) * PATCH_ROWS]
        out_ref[:, c * LANES : (c + 1) * LANES] = part / number


def on_device(exposure, psf_taps, col_warp, row_warp, row_patch, row_prow, owner_map):
    height, width = exposure.shape
    out_rows = row_warp.shape[0]
    count = lax.axis_size("exp")
    nb = width // LANES
    slots = count * PATCH_ROWS
    half, high_groups = count // 2, count // (2 * QUAD)
    size = PATCH_ROWS * nb + SUB
    vmem = pl.BlockSpec(memory_space=pltpu.VMEM)
    hbm = pl.BlockSpec(memory_space=pltpu.HBM)

    def shape(*dims):
        return jax.ShapeDtypeStruct(dims, f32)

    tile = shape(-(-nb // SUB) * SUB, LANES)
    ring_rows = tile.shape[0] + nb * nb + slots // LANES
    ring, own, first, merged, rows, select, lines, blocks = call(
        weights_body,
        [shape(-(-ring_rows // SUB) * SUB, LANES), tile, tile,
         jax.ShapeDtypeStruct((width, width), bf16), jax.ShapeDtypeStruct(row_warp.shape, bf16),
         jax.ShapeDtypeStruct((slots, out_rows), bf16), shape(SUB, slots),
         shape(tile.shape[0], width)],
        [hbm] * 7,
        tuple(in_hbm(array) for array in (
            owner_map, psf_taps, row_patch.reshape(1, out_rows), row_prow.reshape(1, out_rows),
            exposure, col_warp, row_warp,
        )),
        scratch=[
            pltpu.SMEM(owner_map.shape, jnp.int32),
            pltpu.VMEM(psf_taps.shape, bf16),
            pltpu.VMEM((1, out_rows), jnp.int32),
            pltpu.VMEM((1, out_rows), jnp.int32),
            pltpu.VMEM((STRIP, width), f32),
            pltpu.VMEM((STRIP, width), f32),
            pltpu.VMEM(col_warp.shape, bf16),
            pltpu.VMEM((width, width), bf16),
            pltpu.SemaphoreType.DMA((8,)),
        ],
        flops=2 * width * width * width,
    )
    ring = lax.ppermute(ring, "exp", [(i, (i + 1) % count) for i in range(count)])
    sums = call(
        local_body, shape(slots, width), [vmem] * 5, (own, exposure, merged, rows, select),
        scratch=[pltpu.VMEM((height, width), bf16)],
        flops=2 * height * width * (width + out_rows) + 4 * slots * out_rows * width,
    )
    common = (ring, first, blocks, lines, sums)
    send = call(send_body, shape(half * size, LANES), [vmem] * 5, common)
    got = swap(send, 1, count)

    shapes = [shape(size, LANES)] * QUAD
    if high_groups > 1:
        shapes += [shape((high_groups - 1) * size, LANES)] * QUAD
    parts = call(merge_body, shapes, [vmem] * 6, common + (got,))
    near, far = parts[:QUAD], parts[QUAD:]
    terms = [near[0]]
    if high_groups > 1:
        far = [far[0]] + [swap(far[q], 2 * q, count) for q in range(QUAD - 1, 0, -1)]
    near_got = [swap(near[q], 2 * q, count) for q in range(QUAD - 1, 0, -1)]
    if high_groups > 1:
        sent = call(far_body, [shape(size, LANES)] * (high_groups - 1), [vmem] * QUAD, far)
        terms += [swap(sent[h - 1], 2 * QUAD * h, count) for h in range(1, high_groups)]
    terms += near_got
    return call(final_body, shape(PATCH_ROWS, width), [vmem] * len(terms), tuple(terms))


def solution(mesh):
    placed = (
        P(("band", "exp"), None),
        P(("band", "exp"), None),
        P(("band", "exp"), None),
        P(("band", "exp"), None),
        P(("band", "exp"), None),
        P(("band", "exp")),
        P("band"),
    )
    return jax.shard_map(
        on_device, mesh=mesh, in_specs=placed, out_specs=P(("band", "exp"), None), check_vma=False
    )
```

time: 26.4 us -> 25.4 us (0.962)
  Pallas kernels: 6.62 us -> 5.43 us
    pallas_call x6, Pallas kernels: 6.62 us -> 5.43 us  [call(): pl.pallas_call(body, out_shape=outs, in_specs=ins, out_specs=jax.tree.map...]
  transfers between devices with their start and end apart: 9 -> 9, of which waited for: 6 -> 6; matrix products, arithmetic and copies ran while one was open for 0% -> 0% of each run, Pallas kernels for 9% -> 8%
where the time goes in v3:
time: 25.4 us; the launch traced here: 25.3 us
  waiting for transfers between devices  11.6 us (46%)
  starting transfers between devices  8.16 us (32%)
  Pallas kernels  5.43 us (21%)
    ppermute x8, starting transfers between devices, swap(): return lax.ppermute(block, 'exp', [(i, i ^ mask) for i in range(count)])  7.65 us
    ppermute x8, waiting for transfers between devices, swap(): return lax.ppermute(block, 'exp', [(i, i ^ mask) for i in range(count)])  7.2 us
    pallas_call x6, Pallas kernels, call(): pl.pallas_call(body, out_shape=outs, in_specs=ins, out_specs=jax.tree.map...  5.43 us
    ppermute x1, waiting for transfers between devices, on_device(): lax.ppermute(ring, 'exp', [(i, (i + 1) % count) for i in range(count)])  4.45 us
  transfers between devices with their start and end apart: 9, of which 6 were waited for; matrix products, arithmetic and copies ran while one was open for 0% of the time, Pallas kernels for 8%

profile of v3, /device:TPU:0, one launch (start us, length us, event | category | flops | bytes accessed | tf_op | source)
XLA Modules:
  0.0 25.3 jit_solution(17984947818695937059)
XLA Ops:
  0.0 0.0 copy-start
  0.0 2.3 %shard_map.73 = (f32[32,128]{1,0:T(8,128)S(1)}, f32[8,128]{1,0:T(8,128)S(1)}, f32[8,128]{1,0:T(8,128)S(1)}, bf16[512,512]{1,0:T(8,128)(2,1)S(1)}, bf16[512,1024]...) custom-call(s32[16]{0:T(128)} %owner.1, bf16[1,15]{1,0:T(2,128)(2,1)} %taps.1, ...), custom_call_target="tpu_custom_call" | custom-call | flops 268435456 | bytes 3674206 | tf_op jit(solution)/shard_map/pallas_call | solution.py:31
  2.3 0.5 %collective-permute-start = (f32[32,128]{1,0:T(8,128)S(1)}, f32[32,128]{1,0:T(8,128)S(1)}, u32[]{:S(2)}, u32[]{:S(2)}) collective-permute-start(f32[32,128]{1,0:T(8,128)S(1)} %get-tuple-element.21), channel_id=1, source_target_pairs={{0,1},{1,2},{2,3},{3,4},{4,5},{5,6},{6,7},{7,8},{8,9},{9,10},{10,1... | collective-permute-start | bytes 49160 | tf_op jit(solution)/shard_map/ppermute | solution.py:323
  2.8 0.0 copy-done
  2.8 1.9 %shard_map.74.sums_ref = f32[512,512]{1,0:T(8,128)S(1)} custom-call(f32[8,128]{1,0:T(8,128)S(1)} %get-tuple-element.25.own_ref, f32[1024,512]{1,0:T(8,128)S(1)} %copy-done, bf16[512,512]{1,0:T(8,128)(2,1)S(1)} %get-tuple-element.26.merged, bf16[512,1024]{1,0:T(8,128)(2,1)S(1)} %get-tuple-element.27.rows, bf16[512,512]{1,0:T(8,128)(2,1)S(1)} %get-tuple-element.28.select), custom_call_target="tpu_custom_call" | custom-call | flops 1610612736 | bytes 4198400 | tf_op jit(solution)/shard_map/pallas_call | solution.py:31
  4.8 4.4 %collective-permute-done.got_ref = f32[32,128]{1,0:T(8,128)S(1)} collective-permute-done((f32[32,128]{1,0:T(8,128)S(1)}, f32[32,128]{1,0:T(8,128)S(1)}, u32[]{:S(2)}, u32[]{:S(2)}) %collective-permute-start) | collective-permute-done | bytes 16416 | tf_op jit(solution)/shard_map/ppermute | solution.py:323
  9.2 0.2 shard_map.75
  9.4 0.1 collective-permute-start.1
  9.5 1.9 %collective-permute-done.1.half_ref = f32[1088,128]{1,0:T(8,128)S(1)} collective-permute-done((f32[1088,128]{1,0:T(8,128)S(1)}, f32[1088,128]{1,0:T(8,128)S(1)}, u32[]{:S(2)}, u32[]{:S(2)}) %collective-permute-start.1) | collective-permute-done | bytes 557088 | tf_op jit(solution)/shard_map/ppermute | solution.py:26
  11.5 0.2 shard_map.76
  11.7 0.4 %collective-permute-start.2 = (f32[136,128]{1,0:T(8,128)S(1)}, f32[136,128]{1,0:T(8,128)S(1)}, u32[]{:S(2)}, u32[]{:S(2)}) collective-permute-start(f32[136,128]{1,0:T(8,128)S(1)} %get-tuple-element.31), channel_id=1, source_target_pairs={{0,6},{1,7},{2,4},{3,5},{4,2},{5,3},{6,0},{7,1},{8,14},{9,15},{10,... | collective-permute-start | bytes 208904 | tf_op jit(solution)/shard_map/ppermute | solution.py:26
  12.1 0.4 %collective-permute-start.3 = (f32[136,128]{1,0:T(8,128)S(1)}, f32[136,128]{1,0:T(8,128)S(1)}, u32[]{:S(2)}, u32[]{:S(2)}) collective-permute-start(f32[136,128]{1,0:T(8,128)S(1)} %get-tuple-element.32), channel_id=1, source_target_pairs={{0,4},{1,5},{2,6},{3,7},{4,0},{5,1},{6,2},{7,3},{8,12},{9,13},{10,... | collective-permute-start | bytes 208904 | tf_op jit(solution)/shard_map/ppermute | solution.py:26
  12.6 2.7 %collective-permute-start.4 = (f32[136,128]{1,0:T(8,128)S(1)}, f32[136,128]{1,0:T(8,128)S(1)}, u32[]{:S(2)}, u32[]{:S(2)}) collective-permute-start(f32[136,128]{1,0:T(8,128)S(1)} %get-tuple-element.33), channel_id=1, source_target_pairs={{0,2},{1,3},{2,0},{3,1},{4,6},{5,7},{6,4},{7,5},{8,10},{9,11},{10,... | collective-permute-start | bytes 208904 | tf_op jit(solution)/shard_map/ppermute | solution.py:26
  15.2 0.4 %collective-permute-start.6 = (f32[136,128]{1,0:T(8,128)S(1)}, f32[136,128]{1,0:T(8,128)S(1)}, u32[]{:S(2)}, u32[]{:S(2)}) collective-permute-start(f32[136,128]{1,0:T(8,128)S(1)} %get-tuple-element.34), channel_id=1, source_target_pairs={{0,6},{1,7},{2,4},{3,5},{4,2},{5,3},{6,0},{7,1},{8,14},{9,15},{10,... | collective-permute-start | bytes 208904 | tf_op jit(solution)/shard_map/ppermute | solution.py:26
  15.6 1.1 %collective-permute-start.7 = (f32[136,128]{1,0:T(8,128)S(1)}, f32[136,128]{1,0:T(8,128)S(1)}, u32[]{:S(2)}, u32[]{:S(2)}) collective-permute-start(f32[136,128]{1,0:T(8,128)S(1)} %get-tuple-element.35), channel_id=1, source_target_pairs={{0,4},{1,5},{2,6},{3,7},{4,0},{5,1},{6,2},{7,3},{8,12},{9,13},{10,... | collective-permute-start | bytes 208904 | tf_op jit(solution)/shard_map/ppermute | solution.py:26
  16.7 0.9 %collective-permute-done.2.b_ref = f32[136,128]{1,0:T(8,128)S(1)} collective-permute-done((f32[136,128]{1,0:T(8,128)S(1)}, f32[136,128]{1,0:T(8,128)S(1)}, u32[]{:S(2)}, u32[]{:S(2)}) %collective-permute-start.2) | collective-permute-done | bytes 69664 | tf_op jit(solution)/shard_map/ppermute | solution.py:26
  17.6 1.1 %collective-permute-start.8 = (f32[136,128]{1,0:T(8,128)S(1)}, f32[136,128]{1,0:T(8,128)S(1)}, u32[]{:S(2)}, u32[]{:S(2)}) collective-permute-start(f32[136,128]{1,0:T(8,128)S(1)} %get-tuple-element.36), channel_id=1, source_target_pairs={{0,2},{1,3},{2,0},{3,1},{4,6},{5,7},{6,4},{7,5},{8,10},{9,11},{10,... | collective-permute-start | bytes 208904 | tf_op jit(solution)/shard_map/ppermute | solution.py:26
  18.7 0.0 collective-permute-done.3.c_ref
  18.7 0.0 collective-permute-done.4.d_ref
  18.8 1.5 %collective-permute-start.5 = (f32[136,128]{1,0:T(8,128)S(1)}, f32[136,128]{1,0:T(8,128)S(1)}, u32[]{:S(2)}, u32[]{:S(2)}) collective-permute-start(f32[136,128]{1,0:T(8,128)S(1)} %shard_map.77), channel_id=1, source_target_pairs={{0,8},{1,9},{2,10},{3,11},{4,12},{5,13},{6,14},{7,15},{8,0},{9,1},... | collective-permute-start | bytes 208904 | tf_op jit(solution)/shard_map/ppermute | solution.py:26
  20.2 0.4 %collective-permute-done.6.refs_2_ = f32[136,128]{1,0:T(8,128)S(1)} collective-permute-done((f32[136,128]{1,0:T(8,128)S(1)}, f32[136,128]{1,0:T(8,128)S(1)}, u32[]{:S(2)}, u32[]{:S(2)}) %collective-permute-start.6) | collective-permute-done | bytes 69664 | tf_op jit(solution)/shard_map/ppermute | solution.py:26
  20.6 0.0 collective-permute-done.7.refs_3_
  20.6 1.3 %collective-permute-done.8.refs_4_ = f32[136,128]{1,0:T(8,128)S(1)} collective-permute-done((f32[136,128]{1,0:T(8,128)S(1)}, f32[136,128]{1,0:T(8,128)S(1)}, u32[]{:S(2)}, u32[]{:S(2)}) %collective-permute-start.8) | collective-permute-done | bytes 69664 | tf_op jit(solution)/shard_map/ppermute | solution.py:26
  21.9 2.6 %collective-permute-done.5.refs_1_ = f32[136,128]{1,0:T(8,128)S(1)} collective-permute-done((f32[136,128]{1,0:T(8,128)S(1)}, f32[136,128]{1,0:T(8,128)S(1)}, u32[]{:S(2)}, u32[]{:S(2)}) %collective-permute-start.5) | collective-permute-done | bytes 69664 | tf_op jit(solution)/shard_map/ppermute | solution.py:26
  24.6 0.7 %shard_map.78 = f32[32,512]{1,0:T(8,128)} custom-call(f32[136,128]{1,0:T(8,128)S(1)} %get-tuple-element.29.refs_0_, f32[136,128]{1,0:T(8,128)S(1)} %collective-permute-done.5.refs_1_, f32[136,128]{1,0:T(8,128)S(1)} %collective-permute-done.6.refs_2_, f32[136,128]{1,0:T(8,128)S(1)} %collective-permute-done.7.refs_3_, ...), custom_call_target="tpu_custom_call" | custom-call | bytes 348160 | tf_op jit(solution)/shard_map/pallas_call | solution.py:31
  (1 shorter events, 0.0 us)
Async XLA Ops:
  0.0 2.8 %copy-start = (f32[1024,512]{1,0:T(8,128)S(1)}, f32[1024,512]{1,0:T(8,128)}, u32[]{:S(2)}) copy-start(f32[1024,512]{1,0:T(8,128)} %image.1) | copy-start | bytes 6291460
  2.3 6.9 %collective-permute-start = (f32[32,128]{1,0:T(8,128)S(1)}, f32[32,128]{1,0:T(8,128)S(1)}, u32[]{:S(2)}, u32[]{:S(2)}) collective-permute-start(f32[32,128]{1,0:T(8,128)S(1)} %get-tuple-element.21), channel_id=1, source_target_pairs={{0,1},{1,2},{2,3},{3,4},{4,5},{5,6},{6,7},{7,8},{8,9},{9,10},{10,1... | collective-permute-start | bytes 49160 | tf_op jit(solution)/shard_map/ppermute | solution.py:323
  9.4 2.0 %collective-permute-start.1 = (f32[1088,128]{1,0:T(8,128)S(1)}, f32[1088,128]{1,0:T(8,128)S(1)}, u32[]{:S(2)}, u32[]{:S(2)}) collective-permute-start(f32[1088,128]{1,0:T(8,128)S(1)} %shard_map.75), channel_id=1, source_target_pairs={{0,1},{1,0},{2,3},{3,2},{4,5},{5,4},{6,7},{7,6},{8,9},{9,8},{10,11... | collective-permute-start | bytes 1671176 | tf_op jit(solution)/shard_map/ppermute | solution.py:26
  11.7 5.9 %collective-permute-start.2 = (f32[136,128]{1,0:T(8,128)S(1)}, f32[136,128]{1,0:T(8,128)S(1)}, u32[]{:S(2)}, u32[]{:S(2)}) collective-permute-start(f32[136,128]{1,0:T(8,128)S(1)} %get-tuple-element.31), channel_id=1, source_target_pairs={{0,6},{1,7},{2,4},{3,5},{4,2},{5,3},{6,0},{7,1},{8,14},{9,15},{10,... | collective-permute-start | bytes 208904 | tf_op jit(solution)/shard_map/ppermute | solution.py:26
  12.1 6.6 %collective-permute-start.3 = (f32[136,128]{1,0:T(8,128)S(1)}, f32[136,128]{1,0:T(8,128)S(1)}, u32[]{:S(2)}, u32[]{:S(2)}) collective-permute-start(f32[136,128]{1,0:T(8,128)S(1)} %get-tuple-element.32), channel_id=1, source_target_pairs={{0,4},{1,5},{2,6},{3,7},{4,0},{5,1},{6,2},{7,3},{8,12},{9,13},{10,... | collective-permute-start | bytes 208904 | tf_op jit(solution)/shard_map/ppermute | solution.py:26
  12.6 6.2 %collective-permute-start.4 = (f32[136,128]{1,0:T(8,128)S(1)}, f32[136,128]{1,0:T(8,128)S(1)}, u32[]{:S(2)}, u32[]{:S(2)}) collective-permute-start(f32[136,128]{1,0:T(8,128)S(1)} %get-tuple-element.33), channel_id=1, source_target_pairs={{0,2},{1,3},{2,0},{3,1},{4,6},{5,7},{6,4},{7,5},{8,10},{9,11},{10,... | collective-permute-start | bytes 208904 | tf_op jit(solution)/shard_map/ppermute | solution.py:26
  15.2 5.4 %collective-permute-start.6 = (f32[136,128]{1,0:T(8,128)S(1)}, f32[136,128]{1,0:T(8,128)S(1)}, u32[]{:S(2)}, u32[]{:S(2)}) collective-permute-start(f32[136,128]{1,0:T(8,128)S(1)} %get-tuple-element.34), channel_id=1, source_target_pairs={{0,6},{1,7},{2,4},{3,5},{4,2},{5,3},{6,0},{7,1},{8,14},{9,15},{10,... | collective-permute-start | bytes 208904 | tf_op jit(solution)/shard_map/ppermute | solution.py:26
  15.6 5.0 %collective-permute-start.7 = (f32[136,128]{1,0:T(8,128)S(1)}, f32[136,128]{1,0:T(8,128)S(1)}, u32[]{:S(2)}, u32[]{:S(2)}) collective-permute-start(f32[136,128]{1,0:T(8,128)S(1)} %get-tuple-element.35), channel_id=1, source_target_pairs={{0,4},{1,5},{2,6},{3,7},{4,0},{5,1},{6,2},{7,3},{8,12},{9,13},{10,... | collective-permute-start | bytes 208904 | tf_op jit(solution)/shard_map/ppermute | solution.py:26
  17.6 4.3 %collective-permute-start.8 = (f32[136,128]{1,0:T(8,128)S(1)}, f32[136,128]{1,0:T(8,128)S(1)}, u32[]{:S(2)}, u32[]{:S(2)}) collective-permute-start(f32[136,128]{1,0:T(8,128)S(1)} %get-tuple-element.36), channel_id=1, source_target_pairs={{0,2},{1,3},{2,0},{3,1},{4,6},{5,7},{6,4},{7,5},{8,10},{9,11},{10,... | collective-permute-start | bytes 208904 | tf_op jit(solution)/shard_map/ppermute | solution.py:26
  18.8 5.8 %collective-permute-start.5 = (f32[136,128]{1,0:T(8,128)S(1)}, f32[136,128]{1,0:T(8,128)S(1)}, u32[]{:S(2)}, u32[]{:S(2)}) collective-permute-start(f32[136,128]{1,0:T(8,128)S(1)} %shard_map.77), channel_id=1, source_target_pairs={{0,8},{1,9},{2,10},{3,11},{4,12},{5,13},{6,14},{7,15},{8,0},{9,1},... | collective-permute-start | bytes 208904 | tf_op jit(solution)/shard_map/ppermute | solution.py:26

commit v4 on v3

--- a/solution.py
+++ b/solution.py
@@ -1,3 +1,5 @@
+import functools
+
 import jax
 import jax.numpy as jnp
 from jax import lax
@@ -12,6 +14,8 @@
 SUB = 8
 CHUNKS = 4
 QUAD = 4
+FAR_ORDER = (2, 1, 3)
+NEAR_ORDER = (3, 2, 1)
 VMEM_LIMIT = 32 * 1024 * 1024
 
 f32 = jnp.float32
@@ -155,7 +159,7 @@
         ring_ref[base + i : base + i + 1] = weight[:, i * LANES : (i + 1) * LANES]
 
 
-def local_body(own_ref, image, merged, rows, select, sums_ref, warped):
+def local_body(own_ref, image, merged, rows, select, sums_ref, high_ref, low_ref, warped):
     height, width = image.shape
     nb = width // LANES
     step = height // CHUNKS
@@ -167,15 +171,26 @@
             parts.append(piece.astype(bf16))
         centred = jnp.concatenate(parts, axis=1)
         warped[at] = jnp.dot(centred, merged[...], preferred_element_type=f32).astype(bf16)
-    values = jnp.dot(rows[...], warped[...], preferred_element_type=f32)
-    high, low = parts_of(values)
-    sums_ref[...] = jnp.dot(select[...], high, preferred_element_type=f32) + jnp.dot(
-        select[...], low, preferred_element_type=f32
+    high, low = parts_of(jnp.dot(rows[...], warped[...], preferred_element_type=f32))
+    high_ref[...] = high
+    low_ref[...] = low
+    far = select[: sums_ref.shape[0]]
+    sums_ref[...] = jnp.dot(far, high, preferred_element_type=f32) + jnp.dot(
+        far, low, preferred_element_type=f32
     )
 
 
 def place_of(mask, count):
-    return (mask & 1) * (count // 2) + lax.shift_right_logical(mask, 1)
+    other, at = mask & 1, lax.shift_right_logical(mask, 1)
+    far = count // 2 - QUAD
+    return jnp.where(at < QUAD, 2 * far + other * QUAD + at, other * far + at - QUAD)
+
+
+def mask_of(place, count):
+    far = count // 2 - QUAD
+    if place < 2 * far:
+        return (place % far + QUAD) * 2 + place // far
+    return (place - 2 * far) % QUAD * 2 + (place - 2 * far) // QUAD
 
 
 def upright(line, start):
@@ -207,7 +222,7 @@
     def terms(self, j):
         count, each = self.count, LANES // PATCH_ROWS
         me = lax.axis_index("exp")
-        mask = (j % (count // 2)) * 2 + j // (count // 2)
+        mask = mask_of(j, count)
         sender = lax.rem(me + count - 1, count)
         place = place_of(sender ^ me ^ mask, count)
         at = j // each * LANES
@@ -224,41 +239,62 @@
         return pltpu.roll(line, LANES - start, 1) if start else line
 
 
-def send_body(got_ref, first_ref, blocks_ref, lines_ref, sums_ref, out_ref):
-    count = sums_ref.shape[0] // PATCH_ROWS
-    half = count // 2
-    size = out_ref.shape[0] // half
+def put_block(ref, at, size, sums, levels, place, got=None):
+    terms = levels.terms(place)
+    for c, term in enumerate(terms):
+        to = slice(at * size + c * PATCH_ROWS, at * size + (c + 1) * PATCH_ROWS)
+        value = sums[:, c * LANES : (c + 1) * LANES] + term
+        ref[to] = value if got is None else value + got[c * PATCH_ROWS : (c + 1) * PATCH_ROWS]
+    to = at * size + len(terms) * PATCH_ROWS
+    held = levels.held(place)
+    ref[to : to + SUB] = held if got is None else held + got[size - SUB :]
+
+
+def far_send_body(count, got_ref, first_ref, blocks_ref, lines_ref, sums_ref, out_ref):
+    far = count // 2 - QUAD
+    size = out_ref.shape[0] // far
     levels = Levels(got_ref, first_ref, blocks_ref, lines_ref, count)
-    for j in range(half):
-        at = (half + j) * PATCH_ROWS
-        terms = levels.terms(half + j)
-        for c, term in enumerate(terms):
-            to = j * size + c * PATCH_ROWS
-            part = sums_ref[at : at + PATCH_ROWS, c * LANES : (c + 1) * LANES]
-            out_ref[to : to + PATCH_ROWS] = part + term
-        to = j * size + len(terms) * PATCH_ROWS
-        out_ref[to : to + SUB] = levels.held(half + j)
-
-
-def merge_body(got_ref, first_ref, blocks_ref, lines_ref, sums_ref, half_ref, *out_refs):
-    count = sums_ref.shape[0] // PATCH_ROWS
-    half = count // 2
-    size = half_ref.shape[0] // half
+    for j in range(far):
+        at = (far + j) * PATCH_ROWS
+        put_block(out_ref, j, size, sums_ref[at : at + PATCH_ROWS], levels, far + j)
+
+
+def near_body(
+    count, got_ref, first_ref, blocks_ref, lines_ref, select, high, low, send_ref, keep_ref
+):
+    far = count // 2 - QUAD
+    size = send_ref.shape[0] // QUAD
     levels = Levels(got_ref, first_ref, blocks_ref, lines_ref, count)
-    for j in range(half):
-        quad, far = j % QUAD, j // QUAD
-        ref = out_refs[quad] if far == 0 else out_refs[QUAD + quad]
-        base = 0 if far == 0 else (far - 1) * size
+    near = select[2 * far * PATCH_ROWS :]
+    sums = jnp.dot(near, high[...], preferred_element_type=f32) + jnp.dot(
+        near, low[...], preferred_element_type=f32
+    )
+    for part, ref in enumerate((keep_ref, send_ref)):
+        for j in range(QUAD):
+            at = (part * QUAD + j) * PATCH_ROWS
+            place = 2 * far + part * QUAD + j
+            put_block(ref, j, size, sums[at : at + PATCH_ROWS], levels, place)
+
+
+def far_merge_body(
+    count, got_ref, first_ref, blocks_ref, lines_ref, sums_ref, half_ref, *out_refs
+):
+    far = count // 2 - QUAD
+    size = half_ref.shape[0] // far
+    levels = Levels(got_ref, first_ref, blocks_ref, lines_ref, count)
+    for j in range(far):
         at = j * PATCH_ROWS
-        terms = levels.terms(j)
-        for c, term in enumerate(terms):
-            to = c * PATCH_ROWS
-            part = sums_ref[at : at + PATCH_ROWS, c * LANES : (c + 1) * LANES]
-            got = half_ref[j * size + to : j * size + to + PATCH_ROWS]
-            ref[base + to : base + to + PATCH_ROWS] = part + term + got
-        to = len(terms) * PATCH_ROWS
-        got = half_ref[j * size + to : j * size + to + SUB]
-        ref[base + to : base + to + SUB] = levels.held(j) + got
+        got = half_ref[j * size : (j + 1) * size]
+        put_block(
+            out_refs[j % QUAD], j // QUAD, size, sums_ref[at : at + PATCH_ROWS], levels, j, got
+        )
+
+
+def near_merge_body(keep_ref, got_ref, *out_refs):
+    size = out_refs[0].shape[0]
+    for j, ref in enumerate(out_refs):
+        at = slice(j * size, (j + 1) * size)
+        ref[...] = keep_ref[at] + got_ref[at]
 
 
 def far_body(a_ref, b_ref, c_ref, d_ref, *out_refs):
@@ -321,29 +357,35 @@
         flops=2 * width * width * width,
     )
     ring = lax.ppermute(ring, "exp", [(i, (i + 1) % count) for i in range(count)])
-    sums = call(
-        local_body, shape(slots, width), [vmem] * 5, (own, exposure, merged, rows, select),
+    far = half - QUAD
+    sums, high, low = call(
+        local_body,
+        [shape(2 * far * PATCH_ROWS, width)] + [jax.ShapeDtypeStruct((out_rows, width), bf16)] * 2,
+        [vmem] * 5, (own, exposure, merged, rows, select),
         scratch=[pltpu.VMEM((height, width), bf16)],
         flops=2 * height * width * (width + out_rows) + 4 * slots * out_rows * width,
     )
-    common = (ring, first, blocks, lines, sums)
-    send = call(send_body, shape(half * size, LANES), [vmem] * 5, common)
-    got = swap(send, 1, count)
-
-    shapes = [shape(size, LANES)] * QUAD
-    if high_groups > 1:
-        shapes += [shape((high_groups - 1) * size, LANES)] * QUAD
-    parts = call(merge_body, shapes, [vmem] * 6, common + (got,))
-    near, far = parts[:QUAD], parts[QUAD:]
-    terms = [near[0]]
-    if high_groups > 1:
-        far = [far[0]] + [swap(far[q], 2 * q, count) for q in range(QUAD - 1, 0, -1)]
-    near_got = [swap(near[q], 2 * q, count) for q in range(QUAD - 1, 0, -1)]
-    if high_groups > 1:
-        sent = call(far_body, [shape(size, LANES)] * (high_groups - 1), [vmem] * QUAD, far)
-        terms += [swap(sent[h - 1], 2 * QUAD * h, count) for h in range(1, high_groups)]
-    terms += near_got
-    return call(final_body, shape(PATCH_ROWS, width), [vmem] * len(terms), tuple(terms))
+    common = (ring, first, blocks, lines)
+    far_send = call(
+        functools.partial(far_send_body, count), shape(far * size, LANES), [vmem] * 5,
+        common + (sums,),
+    )
+    far_got = swap(far_send, 1, count)
+    near_send, near_keep = call(
+        functools.partial(near_body, count), [shape(QUAD * size, LANES)] * 2, [vmem] * 7,
+        common + (select, high, low),
+    )
+    near_got = swap(near_send, 1, count)
+    parts = call(
+        functools.partial(far_merge_body, count),
+        [shape((high_groups - 1) * size, LANES)] * QUAD, [vmem] * 6, common + (sums, far_got),
+    )
+    terms = [parts[0]] + [swap(parts[q], 2 * q, count) for q in FAR_ORDER]
+    near = call(near_merge_body, [shape(size, LANES)] * QUAD, [vmem] * 2, (near_keep, near_got))
+    rest = [near[0]] + [swap(near[q], 2 * q, count) for q in NEAR_ORDER]
+    sent = call(far_body, [shape(size, LANES)] * (high_groups - 1), [vmem] * QUAD, terms)
+    rest = [swap(sent[h - 1], 2 * QUAD * h, count) for h in range(1, high_groups)] + rest
+    return call(final_body, shape(PATCH_ROWS, width), [vmem] * len(rest), tuple(rest))
 
 
 def solution(mesh):

time: 25.4 us -> 24.5 us (0.965)
  waiting for transfers between devices: 11.6 us -> 7.88 us
  starting transfers between devices: 8.16 us -> 10.9 us
    ppermute x8 -> x9, waiting for transfers between devices: 7.2 us -> 3.13 us  [swap(): return lax.ppermute(block, 'exp', [(i, i ^ mask) for i in range(count)])]
    ppermute x8 -> x9, starting transfers between devices: 7.65 us -> 10.4 us  [swap(): return lax.ppermute(block, 'exp', [(i, i ^ mask) for i in range(count)])]
    ppermute x1, waiting for transfers between devices: 4.45 us -> 4.75 us  [on_device(): lax.ppermute(ring, 'exp', [(i, (i + 1) % count) for i in range(count)])]
    pallas_call x6 -> x8, Pallas kernels: 5.43 us -> 5.43 us  [call(): pl.pallas_call(body, out_shape=outs, in_specs=ins, out_specs=jax.tree.map...]
  transfers between devices with their start and end apart: 9 -> 10, of which waited for: 6 -> 3; matrix products, arithmetic and copies ran while one was open for 0% -> 0% of each run, Pallas kernels for 8% -> 9%
where the time goes in v4:
time: 24.5 us; the launch traced here: 24.3 us
  starting transfers between devices  10.9 us (44%)
  waiting for transfers between devices  7.88 us (32%)
  Pallas kernels  5.43 us (22%)
    ppermute x9, starting transfers between devices, swap(): return lax.ppermute(block, 'exp', [(i, i ^ mask) for i in range(count)])  10.4 us
    pallas_call x8, Pallas kernels, call(): pl.pallas_call(body, out_shape=outs, in_specs=ins, out_specs=jax.tree.map...  5.43 us
    ppermute x1, waiting for transfers between devices, on_device(): lax.ppermute(ring, 'exp', [(i, (i + 1) % count) for i in range(count)])  4.75 us
    ppermute x9, waiting for transfers between devices, swap(): return lax.ppermute(block, 'exp', [(i, i ^ mask) for i in range(count)])  3.13 us
    ppermute x1, starting transfers between devices, on_device(): lax.ppermute(ring, 'exp', [(i, (i + 1) % count) for i in range(count)])  0.5 us
  transfers between devices with their start and end apart: 10, of which 3 were waited for; matrix products, arithmetic and copies ran while one was open for 0% of the time, Pallas kernels for 9%

profile of v4, /device:TPU:0, one launch (start us, length us, event | category | flops | bytes accessed | tf_op | source)
XLA Modules:
  0.0 24.3 jit_solution(17326427396232896305)
XLA Ops:
  0.0 0.0 copy-start
  0.0 2.3 %shard_map.73 = (f32[32,128]{1,0:T(8,128)S(1)}, f32[8,128]{1,0:T(8,128)S(1)}, f32[8,128]{1,0:T(8,128)S(1)}, bf16[512,512]{1,0:T(8,128)(2,1)S(1)}, bf16[512,1024]...) custom-call(s32[16]{0:T(128)} %owner.1, bf16[1,15]{1,0:T(2,128)(2,1)} %taps.1, ...), custom_call_target="tpu_custom_call" | custom-call | flops 268435456 | bytes 3674206 | tf_op jit(solution)/shard_map/pallas_call | solution.py:35
  2.3 0.5 %collective-permute-start = (f32[32,128]{1,0:T(8,128)S(1)}, f32[32,128]{1,0:T(8,128)S(1)}, u32[]{:S(2)}, u32[]{:S(2)}) collective-permute-start(f32[32,128]{1,0:T(8,128)S(1)} %get-tuple-element.26), channel_id=1, source_target_pairs={{0,1},{1,2},{2,3},{3,4},{4,5},{5,6},{6,7},{7,8},{8,9},{9,10},{10,1... | collective-permute-start | bytes 49160 | tf_op jit(solution)/shard_map/ppermute | solution.py:359
  2.8 0.0 copy-done
  2.8 1.6 %shard_map.74 = (f32[256,512]{1,0:T(8,128)S(1)}, bf16[512,512]{1,0:T(8,128)(2,1)S(1)}, bf16[512,512]{1,0:T(8,128)(2,1)S(1)}) custom-call(f32[8,128]{1,0:T(8,128)S(1)} %get-tuple-element.30.own_ref, f32[1024,512]{1,0:T(8,128)S(1)} %copy-done, bf16[512,512]{1,0:T(8,128)(2,1)S(1)} %get-tuple-element.31.merged, bf16[512,1024]{1,0:T(8,128)(2,1)S(1)} %get-tuple-element.32.rows, ...), custom_call_target="tpu_custom_call" | custom-call | flops 1610612736 | bytes 4198400 | tf_op jit(solution)/shard_map/pallas_call | solution.py:35
  4.5 4.7 %collective-permute-done.got_ref = f32[32,128]{1,0:T(8,128)S(1)} collective-permute-done((f32[32,128]{1,0:T(8,128)S(1)}, f32[32,128]{1,0:T(8,128)S(1)}, u32[]{:S(2)}, u32[]{:S(2)}) %collective-permute-start) | collective-permute-done | bytes 16416 | tf_op jit(solution)/shard_map/ppermute | solution.py:359
  9.2 0.1 shard_map.75
  9.4 0.1 collective-permute-start.1
  9.4 0.4 %shard_map.78 = (f32[544,128]{1,0:T(8,128)S(1)}, f32[544,128]{1,0:T(8,128)S(1)}) custom-call(f32[32,128]{1,0:T(8,128)S(1)} %collective-permute-done.got_ref, f32[8,128]{1,0:T(8,128)S(1)} %get-tuple-element.27.first_ref, f32[8,512]{1,0:T(8,128)S(1)} %get-tuple-element.28.blocks_ref, f32[8,512]{1,0:T(8,128)S(1)} %get-tuple-element.29.lines_ref, ...), custom_call_target="tpu_custom_call" | custom-call | bytes 1626112 | tf_op jit(solution)/shard_map/pallas_call | solution.py:35
  9.9 0.6 %collective-permute-start.6 = (f32[544,128]{1,0:T(8,128)S(1)}, f32[544,128]{1,0:T(8,128)S(1)}, u32[]{:S(2)}, u32[]{:S(2)}) collective-permute-start(f32[544,128]{1,0:T(8,128)S(1)} %get-tuple-element.42), channel_id=1, source_target_pairs={{0,1},{1,0},{2,3},{3,2},{4,5},{5,4},{6,7},{7,6},{8,9},{9,8},{10,11... | collective-permute-start | bytes 835592 | tf_op jit(solution)/shard_map/ppermute | solution.py:30
  10.4 0.5 %collective-permute-done.1.half_ref = f32[544,128]{1,0:T(8,128)S(1)} collective-permute-done((f32[544,128]{1,0:T(8,128)S(1)}, f32[544,128]{1,0:T(8,128)S(1)}, u32[]{:S(2)}, u32[]{:S(2)}) %collective-permute-start.1) | collective-permute-done | bytes 278560 | tf_op jit(solution)/shard_map/ppermute | solution.py:30
  11.0 0.1 shard_map.76
  11.1 0.3 %collective-permute-start.2 = (f32[136,128]{1,0:T(8,128)S(1)}, f32[136,128]{1,0:T(8,128)S(1)}, u32[]{:S(2)}, u32[]{:S(2)}) collective-permute-start(f32[136,128]{1,0:T(8,128)S(1)} %get-tuple-element.36), channel_id=1, source_target_pairs={{0,4},{1,5},{2,6},{3,7},{4,0},{5,1},{6,2},{7,3},{8,12},{9,13},{10,... | collective-permute-start | bytes 208904 | tf_op jit(solution)/shard_map/ppermute | solution.py:30
  11.5 0.6 %collective-permute-start.3 = (f32[136,128]{1,0:T(8,128)S(1)}, f32[136,128]{1,0:T(8,128)S(1)}, u32[]{:S(2)}, u32[]{:S(2)}) collective-permute-start(f32[136,128]{1,0:T(8,128)S(1)} %get-tuple-element.37), channel_id=1, source_target_pairs={{0,2},{1,3},{2,0},{3,1},{4,6},{5,7},{6,4},{7,5},{8,10},{9,11},{10,... | collective-permute-start | bytes 208904 | tf_op jit(solution)/shard_map/ppermute | solution.py:30
  12.0 2.6 %collective-permute-start.4 = (f32[136,128]{1,0:T(8,128)S(1)}, f32[136,128]{1,0:T(8,128)S(1)}, u32[]{:S(2)}, u32[]{:S(2)}) collective-permute-start(f32[136,128]{1,0:T(8,128)S(1)} %get-tuple-element.38), channel_id=1, source_target_pairs={{0,6},{1,7},{2,4},{3,5},{4,2},{5,3},{6,0},{7,1},{8,14},{9,15},{10,... | collective-permute-start | bytes 208904 | tf_op jit(solution)/shard_map/ppermute | solution.py:30
  14.7 0.0 collective-permute-done.6.got_ref
  14.7 0.3 %collective-permute-start.7 = (f32[136,128]{1,0:T(8,128)S(1)}, f32[136,128]{1,0:T(8,128)S(1)}, u32[]{:S(2)}, u32[]{:S(2)}) collective-permute-start(f32[136,128]{1,0:T(8,128)S(1)} %get-tuple-element.44), channel_id=1, source_target_pairs={{0,6},{1,7},{2,4},{3,5},{4,2},{5,3},{6,0},{7,1},{8,14},{9,15},{10,... | collective-permute-start | bytes 208904 | tf_op jit(solution)/shard_map/ppermute | solution.py:30
  15.1 1.2 %collective-permute-start.8 = (f32[136,128]{1,0:T(8,128)S(1)}, f32[136,128]{1,0:T(8,128)S(1)}, u32[]{:S(2)}, u32[]{:S(2)}) collective-permute-start(f32[136,128]{1,0:T(8,128)S(1)} %get-tuple-element.45), channel_id=1, source_target_pairs={{0,4},{1,5},{2,6},{3,7},{4,0},{5,1},{6,2},{7,3},{8,12},{9,13},{10,... | collective-permute-start | bytes 208904 | tf_op jit(solution)/shard_map/ppermute | solution.py:30
  16.3 0.0 collective-permute-done.2.b_ref
  16.3 2.0 %collective-permute-start.9 = (f32[136,128]{1,0:T(8,128)S(1)}, f32[136,128]{1,0:T(8,128)S(1)}, u32[]{:S(2)}, u32[]{:S(2)}) collective-permute-start(f32[136,128]{1,0:T(8,128)S(1)} %get-tuple-element.46), channel_id=1, source_target_pairs={{0,2},{1,3},{2,0},{3,1},{4,6},{5,7},{6,4},{7,5},{8,10},{9,11},{10,... | collective-permute-start | bytes 208904 | tf_op jit(solution)/shard_map/ppermute | solution.py:30
  18.3 0.0 collective-permute-done.3.c_ref
  18.3 0.0 collective-permute-done.4.d_ref
  18.3 2.7 %collective-permute-start.5 = (f32[136,128]{1,0:T(8,128)S(1)}, f32[136,128]{1,0:T(8,128)S(1)}, u32[]{:S(2)}, u32[]{:S(2)}) collective-permute-start(f32[136,128]{1,0:T(8,128)S(1)} %shard_map.77), channel_id=1, source_target_pairs={{0,8},{1,9},{2,10},{3,11},{4,12},{5,13},{6,14},{7,15},{8,0},{9,1},... | collective-permute-start | bytes 208904 | tf_op jit(solution)/shard_map/ppermute | solution.py:30
  21.0 0.0 collective-permute-done.7.refs_2_
  21.0 0.0 collective-permute-done.8.refs_3_
  21.0 0.0 collective-permute-done.9.refs_4_
  21.0 2.6 %collective-permute-done.5.refs_0_ = f32[136,128]{1,0:T(8,128)S(1)} collective-permute-done((f32[136,128]{1,0:T(8,128)S(1)}, f32[136,128]{1,0:T(8,128)S(1)}, u32[]{:S(2)}, u32[]{:S(2)}) %collective-permute-start.5) | collective-permute-done | bytes 69664 | tf_op jit(solution)/shard_map/ppermute | solution.py:30
  23.6 0.7 %shard_map.80 = f32[32,512]{1,0:T(8,128)} custom-call(f32[136,128]{1,0:T(8,128)S(1)} %collective-permute-done.5.refs_0_, f32[136,128]{1,0:T(8,128)S(1)} %get-tuple-element.43.refs_1_, f32[136,128]{1,0:T(8,128)S(1)} %collective-permute-done.7.refs_2_, f32[136,128]{1,0:T(8,128)S(1)} %collective-permute-done.8.refs_3_, ...), custom_call_target="tpu_custom_call" | custom-call | bytes 348160 | tf_op jit(solution)/shard_map/pallas_call | solution.py:35
  (2 shorter events, 0.0 us)
Async XLA Ops:
  0.0 2.8 %copy-start = (f32[1024,512]{1,0:T(8,128)S(1)}, f32[1024,512]{1,0:T(8,128)}, u32[]{:S(2)}) copy-start(f32[1024,512]{1,0:T(8,128)} %image.1) | copy-start | bytes 6291460
  2.3 6.9 %collective-permute-start = (f32[32,128]{1,0:T(8,128)S(1)}, f32[32,128]{1,0:T(8,128)S(1)}, u32[]{:S(2)}, u32[]{:S(2)}) collective-permute-start(f32[32,128]{1,0:T(8,128)S(1)} %get-tuple-element.26), channel_id=1, source_target_pairs={{0,1},{1,2},{2,3},{3,4},{4,5},{5,6},{6,7},{7,8},{8,9},{9,10},{10,1... | collective-permute-start | bytes 49160 | tf_op jit(solution)/shard_map/ppermute | solution.py:359
  9.4 1.6 %collective-permute-start.1 = (f32[544,128]{1,0:T(8,128)S(1)}, f32[544,128]{1,0:T(8,128)S(1)}, u32[]{:S(2)}, u32[]{:S(2)}) collective-permute-start(f32[544,128]{1,0:T(8,128)S(1)} %shard_map.75), channel_id=1, source_target_pairs={{0,1},{1,0},{2,3},{3,2},{4,5},{5,4},{6,7},{7,6},{8,9},{9,8},{10,11... | collective-permute-start | bytes 835592 | tf_op jit(solution)/shard_map/ppermute | solution.py:30
  9.9 4.8 %collective-permute-start.6 = (f32[544,128]{1,0:T(8,128)S(1)}, f32[544,128]{1,0:T(8,128)S(1)}, u32[]{:S(2)}, u32[]{:S(2)}) collective-permute-start(f32[544,128]{1,0:T(8,128)S(1)} %get-tuple-element.42), channel_id=1, source_target_pairs={{0,1},{1,0},{2,3},{3,2},{4,5},{5,4},{6,7},{7,6},{8,9},{9,8},{10,11... | collective-permute-start | bytes 835592 | tf_op jit(solution)/shard_map/ppermute | solution.py:30
  11.1 5.1 %collective-permute-start.2 = (f32[136,128]{1,0:T(8,128)S(1)}, f32[136,128]{1,0:T(8,128)S(1)}, u32[]{:S(2)}, u32[]{:S(2)}) collective-permute-start(f32[136,128]{1,0:T(8,128)S(1)} %get-tuple-element.36), channel_id=1, source_target_pairs={{0,4},{1,5},{2,6},{3,7},{4,0},{5,1},{6,2},{7,3},{8,12},{9,13},{10,... | collective-permute-start | bytes 208904 | tf_op jit(solution)/shard_map/ppermute | solution.py:30
  11.5 6.8 %collective-permute-start.3 = (f32[136,128]{1,0:T(8,128)S(1)}, f32[136,128]{1,0:T(8,128)S(1)}, u32[]{:S(2)}, u32[]{:S(2)}) collective-permute-start(f32[136,128]{1,0:T(8,128)S(1)} %get-tuple-element.37), channel_id=1, source_target_pairs={{0,2},{1,3},{2,0},{3,1},{4,6},{5,7},{6,4},{7,5},{8,10},{9,11},{10,... | collective-permute-start | bytes 208904 | tf_op jit(solution)/shard_map/ppermute | solution.py:30
  12.0 6.3 %collective-permute-start.4 = (f32[136,128]{1,0:T(8,128)S(1)}, f32[136,128]{1,0:T(8,128)S(1)}, u32[]{:S(2)}, u32[]{:S(2)}) collective-permute-start(f32[136,128]{1,0:T(8,128)S(1)} %get-tuple-element.38), channel_id=1, source_target_pairs={{0,6},{1,7},{2,4},{3,5},{4,2},{5,3},{6,0},{7,1},{8,14},{9,15},{10,... | collective-permute-start | bytes 208904 | tf_op jit(solution)/shard_map/ppermute | solution.py:30
  14.7 6.3 %collective-permute-start.7 = (f32[136,128]{1,0:T(8,128)S(1)}, f32[136,128]{1,0:T(8,128)S(1)}, u32[]{:S(2)}, u32[]{:S(2)}) collective-permute-start(f32[136,128]{1,0:T(8,128)S(1)} %get-tuple-element.44), channel_id=1, source_target_pairs={{0,6},{1,7},{2,4},{3,5},{4,2},{5,3},{6,0},{7,1},{8,14},{9,15},{10,... | collective-permute-start | bytes 208904 | tf_op jit(solution)/shard_map/ppermute | solution.py:30
  15.1 5.9 %collective-permute-start.8 = (f32[136,128]{1,0:T(8,128)S(1)}, f32[136,128]{1,0:T(8,128)S(1)}, u32[]{:S(2)}, u32[]{:S(2)}) collective-permute-start(f32[136,128]{1,0:T(8,128)S(1)} %get-tuple-element.45), channel_id=1, source_target_pairs={{0,4},{1,5},{2,6},{3,7},{4,0},{5,1},{6,2},{7,3},{8,12},{9,13},{10,... | collective-permute-start | bytes 208904 | tf_op jit(solution)/shard_map/ppermute | solution.py:30
  16.3 4.8 %collective-permute-start.9 = (f32[136,128]{1,0:T(8,128)S(1)}, f32[136,128]{1,0:T(8,128)S(1)}, u32[]{:S(2)}, u32[]{:S(2)}) collective-permute-start(f32[136,128]{1,0:T(8,128)S(1)} %get-tuple-element.46), channel_id=1, source_target_pairs={{0,2},{1,3},{2,0},{3,1},{4,6},{5,7},{6,4},{7,5},{8,10},{9,11},{10,... | collective-permute-start | bytes 208904 | tf_op jit(solution)/shard_map/ppermute | solution.py:30
  18.3 5.3 %collective-permute-start.5 = (f32[136,128]{1,0:T(8,128)S(1)}, f32[136,128]{1,0:T(8,128)S(1)}, u32[]{:S(2)}, u32[]{:S(2)}) collective-permute-start(f32[136,128]{1,0:T(8,128)S(1)} %shard_map.77), channel_id=1, source_target_pairs={{0,8},{1,9},{2,10},{3,11},{4,12},{5,13},{6,14},{7,15},{8,0},{9,1},... | collective-permute-start | bytes 208904 | tf_op jit(solution)/shard_map/ppermute | solution.py:30

commit v5 on v4

--- a/solution.py
+++ b/solution.py
@@ -77,8 +77,8 @@
 
 def weights_body(
     owner, taps, patch, prow, exposure, col_warp, row_warp,
-    ring_ref, own_ref, first_ref, merged_ref, rows_ref, select_ref, lines_ref, blocks_ref,
-    owner_ref, taps_ref, patch_ref, prow_ref, first_rows, last_rows, cols, band, sems,
+    ring_ref, own_ref, first_ref, band, cols, rows_ref, select_ref, lines_ref, blocks_ref,
+    owner_ref, taps_ref, patch_ref, prow_ref, first_rows, last_rows, sems,
 ):
     height, width = exposure.shape
     nb = width // LANES
@@ -91,8 +91,8 @@
         (row_warp, rows_ref),
     ]
     copies = [pltpu.make_async_copy(*move, sems.at[i]) for i, move in enumerate(moves)]
-    for copy in copies:
-        copy.start()
+    for i in (0, 1, 2, 3, 7, 5, 6, 4):
+        copies[i].start()
 
     copies[0].wait()
     tiles = band_tiles(taps_ref[...].astype(f32))
@@ -113,18 +113,9 @@
     slots = lax.broadcasted_iota(jnp.int32, select_ref.shape, 0)
     select_ref[...] = jnp.where(slots == key, 1.0, 0.0).astype(bf16)
 
-    copies[4].wait()
-    both = jnp.dot(band[...], cols[...], preferred_element_type=f32)
-    merged_ref[...] = both.astype(bf16)
     for ref in (ring_ref, own_ref, first_ref, blocks_ref, lines_ref):
         ref[...] = jnp.zeros_like(ref)
     base = own_ref.shape[0]
-    for b in range(nb):
-        total = jnp.sum(both[b * LANES : (b + 1) * LANES], axis=0, keepdims=True)
-        blocks_ref[b : b + 1] = total
-        for c in range(nb):
-            to = base + b * nb + c
-            ring_ref[to : to + 1] = total[:, c * LANES : (c + 1) * LANES]
 
     copies[5].wait()
     copies[6].wait()
@@ -154,15 +145,34 @@
     weight = found[0:1] + found[1:2]
     lines_ref[0:1] = weight
     lines_ref[1:2] = found[2:3]
-    base += nb * nb
     for i in range(weight.shape[1] // LANES):
-        ring_ref[base + i : base + i + 1] = weight[:, i * LANES : (i + 1) * LANES]
-
-
-def local_body(own_ref, image, merged, rows, select, sums_ref, high_ref, low_ref, warped):
+        ring_ref[base + nb * nb + i : base + nb * nb + i + 1] = weight[:, i * LANES : (i + 1) * LANES]
+
+    copies[4].wait()
+    heads = {side: jnp.sum(tile.astype(f32), axis=0, keepdims=True) for side, tile in tiles.items()}
+    blank = jnp.zeros((1, LANES), f32)
+    lines = [
+        jnp.concatenate([heads.get(b - k, blank) for k in range(nb)], axis=1) for b in range(nb)
+    ]
+    lines.append(jnp.zeros((base - nb, width), f32))
+    high, low = parts_of(jnp.concatenate(lines, axis=0))
+    stacked = jnp.concatenate([high.astype(f32), low.astype(f32)], axis=0).astype(bf16)
+    both = jnp.dot(stacked, cols[...], preferred_element_type=f32)
+    total = both[:base] + both[base:]
+    blocks_ref[...] = total
+    for b in range(nb):
+        for c in range(nb):
+            to = base + b * nb + c
+            ring_ref[to : to + 1] = total[b : b + 1, c * LANES : (c + 1) * LANES]
+
+
+def local_body(
+    own_ref, image, band, cols, rows, select, sums_ref, high_ref, low_ref, merged, warped
+):
     height, width = image.shape
     nb = width // LANES
     step = height // CHUNKS
+    merged[...] = jnp.dot(band[...], cols[...], preferred_element_type=f32).astype(bf16)
     for i in range(CHUNKS):
         at = slice(i * step, (i + 1) * step)
         parts = []
@@ -332,10 +342,11 @@
 
     tile = shape(-(-nb // SUB) * SUB, LANES)
     ring_rows = tile.shape[0] + nb * nb + slots // LANES
-    ring, own, first, merged, rows, select, lines, blocks = call(
+    ring, own, first, band, cols, rows, select, lines, blocks = call(
         weights_body,
         [shape(-(-ring_rows // SUB) * SUB, LANES), tile, tile,
-         jax.ShapeDtypeStruct((width, width), bf16), jax.ShapeDtypeStruct(row_warp.shape, bf16),
+         jax.ShapeDtypeStruct((width, width), bf16), jax.ShapeDtypeStruct(col_warp.shape, bf16),
+         jax.ShapeDtypeStruct(row_warp.shape, bf16),
          jax.ShapeDtypeStruct((slots, out_rows), bf16), shape(SUB, slots),
          shape(tile.shape[0], width)],
         [hbm] * 7,
@@ -350,8 +361,6 @@
             pltpu.VMEM((1, out_rows), jnp.int32),
             pltpu.VMEM((STRIP, width), f32),
             pltpu.VMEM((STRIP, width), f32),
-            pltpu.VMEM(col_warp.shape, bf16),
-            pltpu.VMEM((width, width), bf16),
             pltpu.SemaphoreType.DMA((8,)),
         ],
         flops=2 * width * width * width,
@@ -361,8 +370,8 @@
     sums, high, low = call(
         local_body,
         [shape(2 * far * PATCH_ROWS, width)] + [jax.ShapeDtypeStruct((out_rows, width), bf16)] * 2,
-        [vmem] * 5, (own, exposure, merged, rows, select),
-        scratch=[pltpu.VMEM((height, width), bf16)],
+        [vmem] * 6, (own, exposure, band, cols, rows, select),
+        scratch=[pltpu.VMEM((width, width), bf16), pltpu.VMEM((height, width), bf16)],
         flops=2 * height * width * (width + out_rows) + 4 * slots * out_rows * width,
     )
     common = (ring, first, blocks, lines)

time: 24.5 us -> 24.3 us (level)
  waiting for transfers between devices: 7.88 us -> 7.52 us
    ppermute x1, waiting for transfers between devices: 4.75 us -> 4.39 us  [on_device(): lax.ppermute(ring, 'exp', [(i, (i + 1) % count) for i in range(count)])]
  transfers between devices with their start and end apart: 10 -> 10, of which waited for: 3 -> 3; matrix products, arithmetic and copies ran while one was open for 0% -> 0% of each run, Pallas kernels for 9% -> 11%
where the time goes in v5:
time: 24.3 us; the launch traced here: 24.1 us
  starting transfers between devices  10.9 us (45%)
  waiting for transfers between devices  7.52 us (31%)
  Pallas kernels  5.61 us (23%)
    ppermute x9, starting transfers between devices, swap(): return lax.ppermute(block, 'exp', [(i, i ^ mask) for i in range(count)])  10.4 us
    pallas_call x8, Pallas kernels, call(): pl.pallas_call(body, out_shape=outs, in_specs=ins, out_specs=jax.tree.map...  5.61 us
    ppermute x1, waiting for transfers between devices, on_device(): lax.ppermute(ring, 'exp', [(i, (i + 1) % count) for i in range(count)])  4.39 us
    ppermute x9, waiting for transfers between devices, swap(): return lax.ppermute(block, 'exp', [(i, i ^ mask) for i in range(count)])  3.13 us
    ppermute x1, starting transfers between devices, on_device(): lax.ppermute(ring, 'exp', [(i, (i + 1) % count) for i in range(count)])  0.5 us
  transfers between devices with their start and end apart: 10, of which 3 were waited for; matrix products, arithmetic and copies ran while one was open for 0% of the time, Pallas kernels for 11%

profile of v5, /device:TPU:0, one launch (start us, length us, event | category | flops | bytes accessed | tf_op | source)
XLA Modules:
  0.0 24.1 jit_solution(18278939333870078274)
XLA Ops:
  0.0 0.0 copy-start
  0.0 2.1 %shard_map.73 = (f32[32,128]{1,0:T(8,128)S(1)}, f32[8,128]{1,0:T(8,128)S(1)}, f32[8,128]{1,0:T(8,128)S(1)}, bf16[512,512]{1,0:T(8,128)(2,1)S(1)}, bf16[512,512]{...) custom-call(s32[16]{0:T(128)} %owner.1, ...), custom_call_target="tpu_custom_call" | custom-call | flops 268435456 | bytes 3674206 | tf_op jit(solution)/shard_map/pallas_call | solution.py:35
  2.2 0.5 %collective-permute-start = (f32[32,128]{1,0:T(8,128)S(1)}, f32[32,128]{1,0:T(8,128)S(1)}, u32[]{:S(2)}, u32[]{:S(2)}) collective-permute-start(f32[32,128]{1,0:T(8,128)S(1)} %get-tuple-element.27), channel_id=1, source_target_pairs={{0,1},{1,2},{2,3},{3,4},{4,5},{5,6},{6,7},{7,8},{8,9},{9,10},{10,1... | collective-permute-start | bytes 49160 | tf_op jit(solution)/shard_map/ppermute | solution.py:368
  2.7 0.0 copy-done
  2.7 2.0 %shard_map.74 = (f32[256,512]{1,0:T(8,128)S(1)}, bf16[512,512]{1,0:T(8,128)(2,1)S(1)}, bf16[512,512]{1,0:T(8,128)(2,1)S(1)}) custom-call(f32[8,128]{1,0:T(8,128)S(1)} %get-tuple-element.31.own_ref, f32[1024,512]{1,0:T(8,128)S(1)} %copy-done, bf16[512,512]{1,0:T(8,128)(2,1)S(1)} %get-tuple-element.32.band, bf16[512,512]{1,0:T(8,128)(2,1)S(1)} %get-tuple-element.33.cols, ...), custom_call_target="tpu_custom_call" | custom-call | flops 1610612736 | bytes 4722688 | tf_op jit(solution)/shard_map/pallas_call | solution.py:35
  4.7 4.4 %collective-permute-done.got_ref = f32[32,128]{1,0:T(8,128)S(1)} collective-permute-done((f32[32,128]{1,0:T(8,128)S(1)}, f32[32,128]{1,0:T(8,128)S(1)}, u32[]{:S(2)}, u32[]{:S(2)}) %collective-permute-start) | collective-permute-done | bytes 16416 | tf_op jit(solution)/shard_map/ppermute | solution.py:368
  9.1 0.1 shard_map.75
  9.2 0.1 collective-permute-start.1
  9.3 0.4 %shard_map.78 = (f32[544,128]{1,0:T(8,128)S(1)}, f32[544,128]{1,0:T(8,128)S(1)}) custom-call(f32[32,128]{1,0:T(8,128)S(1)} %collective-permute-done.got_ref, f32[8,128]{1,0:T(8,128)S(1)} %get-tuple-element.28.first_ref, f32[8,512]{1,0:T(8,128)S(1)} %get-tuple-element.29.blocks_ref, f32[8,512]{1,0:T(8,128)S(1)} %get-tuple-element.30.lines_ref, ...), custom_call_target="tpu_custom_call" | custom-call | bytes 1626112 | tf_op jit(solution)/shard_map/pallas_call | solution.py:35
  9.7 0.6 %collective-permute-start.6 = (f32[544,128]{1,0:T(8,128)S(1)}, f32[544,128]{1,0:T(8,128)S(1)}, u32[]{:S(2)}, u32[]{:S(2)}) collective-permute-start(f32[544,128]{1,0:T(8,128)S(1)} %get-tuple-element.44), channel_id=1, source_target_pairs={{0,1},{1,0},{2,3},{3,2},{4,5},{5,4},{6,7},{7,6},{8,9},{9,8},{10,11... | collective-permute-start | bytes 835592 | tf_op jit(solution)/shard_map/ppermute | solution.py:30
  10.3 0.5 %collective-permute-done.1.half_ref = f32[544,128]{1,0:T(8,128)S(1)} collective-permute-done((f32[544,128]{1,0:T(8,128)S(1)}, f32[544,128]{1,0:T(8,128)S(1)}, u32[]{:S(2)}, u32[]{:S(2)}) %collective-permute-start.1) | collective-permute-done | bytes 278560 | tf_op jit(solution)/shard_map/ppermute | solution.py:30
  10.8 0.1 shard_map.76
  11.0 0.3 %collective-permute-start.2 = (f32[136,128]{1,0:T(8,128)S(1)}, f32[136,128]{1,0:T(8,128)S(1)}, u32[]{:S(2)}, u32[]{:S(2)}) collective-permute-start(f32[136,128]{1,0:T(8,128)S(1)} %get-tuple-element.38), channel_id=1, source_target_pairs={{0,4},{1,5},{2,6},{3,7},{4,0},{5,1},{6,2},{7,3},{8,12},{9,13},{10,... | collective-permute-start | bytes 208904 | tf_op jit(solution)/shard_map/ppermute | solution.py:30
  11.3 0.7 %collective-permute-start.3 = (f32[136,128]{1,0:T(8,128)S(1)}, f32[136,128]{1,0:T(8,128)S(1)}, u32[]{:S(2)}, u32[]{:S(2)}) collective-permute-start(f32[136,128]{1,0:T(8,128)S(1)} %get-tuple-element.39), channel_id=1, source_target_pairs={{0,2},{1,3},{2,0},{3,1},{4,6},{5,7},{6,4},{7,5},{8,10},{9,11},{10,... | collective-permute-start | bytes 208904 | tf_op jit(solution)/shard_map/ppermute | solution.py:30
  12.0 2.5 %collective-permute-start.4 = (f32[136,128]{1,0:T(8,128)S(1)}, f32[136,128]{1,0:T(8,128)S(1)}, u32[]{:S(2)}, u32[]{:S(2)}) collective-permute-start(f32[136,128]{1,0:T(8,128)S(1)} %get-tuple-element.40), channel_id=1, source_target_pairs={{0,6},{1,7},{2,4},{3,5},{4,2},{5,3},{6,0},{7,1},{8,14},{9,15},{10,... | collective-permute-start | bytes 208904 | tf_op jit(solution)/shard_map/ppermute | solution.py:30
  14.5 0.0 collective-permute-done.6.got_ref
  14.6 0.5 %collective-permute-start.7 = (f32[136,128]{1,0:T(8,128)S(1)}, f32[136,128]{1,0:T(8,128)S(1)}, u32[]{:S(2)}, u32[]{:S(2)}) collective-permute-start(f32[136,128]{1,0:T(8,128)S(1)} %get-tuple-element.46), channel_id=1, source_target_pairs={{0,6},{1,7},{2,4},{3,5},{4,2},{5,3},{6,0},{7,1},{8,14},{9,15},{10,... | collective-permute-start | bytes 208904 | tf_op jit(solution)/shard_map/ppermute | solution.py:30
  15.0 1.0 %collective-permute-start.8 = (f32[136,128]{1,0:T(8,128)S(1)}, f32[136,128]{1,0:T(8,128)S(1)}, u32[]{:S(2)}, u32[]{:S(2)}) collective-permute-start(f32[136,128]{1,0:T(8,128)S(1)} %get-tuple-element.47), channel_id=1, source_target_pairs={{0,4},{1,5},{2,6},{3,7},{4,0},{5,1},{6,2},{7,3},{8,12},{9,13},{10,... | collective-permute-start | bytes 208904 | tf_op jit(solution)/shard_map/ppermute | solution.py:30
  16.1 0.0 collective-permute-done.2.b_ref
  16.1 2.0 %collective-permute-start.9 = (f32[136,128]{1,0:T(8,128)S(1)}, f32[136,128]{1,0:T(8,128)S(1)}, u32[]{:S(2)}, u32[]{:S(2)}) collective-permute-start(f32[136,128]{1,0:T(8,128)S(1)} %get-tuple-element.48), channel_id=1, source_target_pairs={{0,2},{1,3},{2,0},{3,1},{4,6},{5,7},{6,4},{7,5},{8,10},{9,11},{10,... | collective-permute-start | bytes 208904 | tf_op jit(solution)/shard_map/ppermute | solution.py:30
  18.1 0.0 collective-permute-done.3.c_ref
  18.1 0.0 collective-permute-done.4.d_ref
  18.1 2.7 %collective-permute-start.5 = (f32[136,128]{1,0:T(8,128)S(1)}, f32[136,128]{1,0:T(8,128)S(1)}, u32[]{:S(2)}, u32[]{:S(2)}) collective-permute-start(f32[136,128]{1,0:T(8,128)S(1)} %shard_map.77), channel_id=1, source_target_pairs={{0,8},{1,9},{2,10},{3,11},{4,12},{5,13},{6,14},{7,15},{8,0},{9,1},... | collective-permute-start | bytes 208904 | tf_op jit(solution)/shard_map/ppermute | solution.py:30
  20.8 0.0 collective-permute-done.7.refs_2_
  20.8 0.0 collective-permute-done.8.refs_3_
  20.8 0.0 collective-permute-done.9.refs_4_
  20.9 2.6 %collective-permute-done.5.refs_0_ = f32[136,128]{1,0:T(8,128)S(1)} collective-permute-done((f32[136,128]{1,0:T(8,128)S(1)}, f32[136,128]{1,0:T(8,128)S(1)}, u32[]{:S(2)}, u32[]{:S(2)}) %collective-permute-start.5) | collective-permute-done | bytes 69664 | tf_op jit(solution)/shard_map/ppermute | solution.py:30
  23.4 0.7 %shard_map.80 = f32[32,512]{1,0:T(8,128)} custom-call(f32[136,128]{1,0:T(8,128)S(1)} %collective-permute-done.5.refs_0_, f32[136,128]{1,0:T(8,128)S(1)} %get-tuple-element.45.refs_1_, f32[136,128]{1,0:T(8,128)S(1)} %collective-permute-done.7.refs_2_, f32[136,128]{1,0:T(8,128)S(1)} %collective-permute-done.8.refs_3_, ...), custom_call_target="tpu_custom_call" | custom-call | bytes 348160 | tf_op jit(solution)/shard_map/pallas_call | solution.py:35
  (2 shorter events, 0.0 us)
Async XLA Ops:
  0.0 2.7 %copy-start = (f32[1024,512]{1,0:T(8,128)S(1)}, f32[1024,512]{1,0:T(8,128)}, u32[]{:S(2)}) copy-start(f32[1024,512]{1,0:T(8,128)} %image.1) | copy-start | bytes 6291460
  2.2 6.9 %collective-permute-start = (f32[32,128]{1,0:T(8,128)S(1)}, f32[32,128]{1,0:T(8,128)S(1)}, u32[]{:S(2)}, u32[]{:S(2)}) collective-permute-start(f32[32,128]{1,0:T(8,128)S(1)} %get-tuple-element.27), channel_id=1, source_target_pairs={{0,1},{1,2},{2,3},{3,4},{4,5},{5,6},{6,7},{7,8},{8,9},{9,10},{10,1... | collective-permute-start | bytes 49160 | tf_op jit(solution)/shard_map/ppermute | solution.py:368
  9.2 1.6 %collective-permute-start.1 = (f32[544,128]{1,0:T(8,128)S(1)}, f32[544,128]{1,0:T(8,128)S(1)}, u32[]{:S(2)}, u32[]{:S(2)}) collective-permute-start(f32[544,128]{1,0:T(8,128)S(1)} %shard_map.75), channel_id=1, source_target_pairs={{0,1},{1,0},{2,3},{3,2},{4,5},{5,4},{6,7},{7,6},{8,9},{9,8},{10,11... | collective-permute-start | bytes 835592 | tf_op jit(solution)/shard_map/ppermute | solution.py:30
  9.7 4.8 %collective-permute-start.6 = (f32[544,128]{1,0:T(8,128)S(1)}, f32[544,128]{1,0:T(8,128)S(1)}, u32[]{:S(2)}, u32[]{:S(2)}) collective-permute-start(f32[544,128]{1,0:T(8,128)S(1)} %get-tuple-element.44), channel_id=1, source_target_pairs={{0,1},{1,0},{2,3},{3,2},{4,5},{5,4},{6,7},{7,6},{8,9},{9,8},{10,11... | collective-permute-start | bytes 835592 | tf_op jit(solution)/shard_map/ppermute | solution.py:30
  11.0 5.1 %collective-permute-start.2 = (f32[136,128]{1,0:T(8,128)S(1)}, f32[136,128]{1,0:T(8,128)S(1)}, u32[]{:S(2)}, u32[]{:S(2)}) collective-permute-start(f32[136,128]{1,0:T(8,128)S(1)} %get-tuple-element.38), channel_id=1, source_target_pairs={{0,4},{1,5},{2,6},{3,7},{4,0},{5,1},{6,2},{7,3},{8,12},{9,13},{10,... | collective-permute-start | bytes 208904 | tf_op jit(solution)/shard_map/ppermute | solution.py:30
  11.3 6.8 %collective-permute-start.3 = (f32[136,128]{1,0:T(8,128)S(1)}, f32[136,128]{1,0:T(8,128)S(1)}, u32[]{:S(2)}, u32[]{:S(2)}) collective-permute-start(f32[136,128]{1,0:T(8,128)S(1)} %get-tuple-element.39), channel_id=1, source_target_pairs={{0,2},{1,3},{2,0},{3,1},{4,6},{5,7},{6,4},{7,5},{8,10},{9,11},{10,... | collective-permute-start | bytes 208904 | tf_op jit(solution)/shard_map/ppermute | solution.py:30
  12.0 6.1 %collective-permute-start.4 = (f32[136,128]{1,0:T(8,128)S(1)}, f32[136,128]{1,0:T(8,128)S(1)}, u32[]{:S(2)}, u32[]{:S(2)}) collective-permute-start(f32[136,128]{1,0:T(8,128)S(1)} %get-tuple-element.40), channel_id=1, source_target_pairs={{0,6},{1,7},{2,4},{3,5},{4,2},{5,3},{6,0},{7,1},{8,14},{9,15},{10,... | collective-permute-start | bytes 208904 | tf_op jit(solution)/shard_map/ppermute | solution.py:30
  14.6 6.3 %collective-permute-start.7 = (f32[136,128]{1,0:T(8,128)S(1)}, f32[136,128]{1,0:T(8,128)S(1)}, u32[]{:S(2)}, u32[]{:S(2)}) collective-permute-start(f32[136,128]{1,0:T(8,128)S(1)} %get-tuple-element.46), channel_id=1, source_target_pairs={{0,6},{1,7},{2,4},{3,5},{4,2},{5,3},{6,0},{7,1},{8,14},{9,15},{10,... | collective-permute-start | bytes 208904 | tf_op jit(solution)/shard_map/ppermute | solution.py:30
  15.0 5.8 %collective-permute-start.8 = (f32[136,128]{1,0:T(8,128)S(1)}, f32[136,128]{1,0:T(8,128)S(1)}, u32[]{:S(2)}, u32[]{:S(2)}) collective-permute-start(f32[136,128]{1,0:T(8,128)S(1)} %get-tuple-element.47), channel_id=1, source_target_pairs={{0,4},{1,5},{2,6},{3,7},{4,0},{5,1},{6,2},{7,3},{8,12},{9,13},{10,... | collective-permute-start | bytes 208904 | tf_op jit(solution)/shard_map/ppermute | solution.py:30
  16.1 4.8 %collective-permute-start.9 = (f32[136,128]{1,0:T(8,128)S(1)}, f32[136,128]{1,0:T(8,128)S(1)}, u32[]{:S(2)}, u32[]{:S(2)}) collective-permute-start(f32[136,128]{1,0:T(8,128)S(1)} %get-tuple-element.48), channel_id=1, source_target_pairs={{0,2},{1,3},{2,0},{3,1},{4,6},{5,7},{6,4},{7,5},{8,10},{9,11},{10,... | collective-permute-start | bytes 208904 | tf_op jit(solution)/shard_map/ppermute | solution.py:30
  18.1 5.3 %collective-permute-start.5 = (f32[136,128]{1,0:T(8,128)S(1)}, f32[136,128]{1,0:T(8,128)S(1)}, u32[]{:S(2)}, u32[]{:S(2)}) collective-permute-start(f32[136,128]{1,0:T(8,128)S(1)} %shard_map.77), channel_id=1, source_target_pairs={{0,8},{1,9},{2,10},{3,11},{4,12},{5,13},{6,14},{7,15},{8,0},{9,1},... | collective-permute-start | bytes 208904 | tf_op jit(solution)/shard_map/ppermute | solution.py:30

commit v6 on v5

--- a/solution.py
+++ b/solution.py
@@ -14,8 +14,9 @@
 SUB = 8
 CHUNKS = 4
 QUAD = 4
+SHARED = 9
 FAR_ORDER = (2, 1, 3)
-NEAR_ORDER = (3, 2, 1)
+HOLD = 4_000_000_000
 VMEM_LIMIT = 32 * 1024 * 1024
 
 f32 = jnp.float32
@@ -30,14 +31,16 @@
     return lax.ppermute(block, "exp", [(i, i ^ mask) for i in range(count)])
 
 
-def call(body, outs, ins, args, scratch=(), flops=0):
-    moved = sum(a.size * a.dtype.itemsize for a in args)
+def call(body, outs, ins, args, scratch=(), flops=0, aliases=(), moved=None):
+    if moved is None:
+        moved = sum(a.size * a.dtype.itemsize for a in args)
     return pl.pallas_call(
         body,
         out_shape=outs,
         in_specs=ins,
         out_specs=jax.tree.map(lambda _: pl.BlockSpec(memory_space=pltpu.VMEM), outs),
         scratch_shapes=scratch,
+        input_output_aliases=dict(aliases),
         compiler_params=pltpu.CompilerParams(vmem_limit_bytes=VMEM_LIMIT),
         cost_estimate=pl.CostEstimate(flops=flops, bytes_accessed=moved, transcendentals=0),
     )(*args)
@@ -75,10 +78,45 @@
     }
 
 
+def block_sums(messages, cols, blocks_ref):
+    rows, width = blocks_ref.shape
+    nb = width // LANES
+    high, low = parts_of(blocks_ref[...])
+    stacked = jnp.concatenate([high.astype(f32), low.astype(f32)], axis=0).astype(bf16)
+    both = jnp.dot(stacked, cols[...], preferred_element_type=f32)
+    total = both[:rows] + both[rows:]
+    blocks_ref[...] = total
+    for b in range(nb):
+        for c in range(nb):
+            to = rows + b * nb + c
+            for ref in messages:
+                ref[to : to + 1] = total[b : b + 1, c * LANES : (c + 1) * LANES]
+
+
+def row_sums(messages, rows_ref, select_ref, lines_ref, blocks_ref):
+    nb = blocks_ref.shape[1] // LANES
+    partial = rows_ref[:, :LANES].astype(f32)
+    for i in range(1, rows_ref.shape[1] // LANES):
+        partial += rows_ref[:, i * LANES : (i + 1) * LANES].astype(f32)
+    ones = jnp.ones((2 * SUB, LANES), bf16)
+    high, low = parts_of(partial)
+    high, low = parts_of(lane_dot(ones, high) + lane_dot(ones, low))
+    line = lax.broadcasted_iota(jnp.int32, high.shape, 0)
+    left = jnp.where(line == 0, high.astype(f32), jnp.where(line == 1, low.astype(f32), 1.0))
+    found = lane_dot(left.astype(bf16), select_ref[...])
+    weight = found[0:1] + found[1:2]
+    lines_ref[0:1] = weight
+    lines_ref[1:2] = found[2:3]
+    base = blocks_ref.shape[0] + nb * nb
+    for i in range(weight.shape[1] // LANES):
+        for ref in messages:
+            ref[base + i : base + i + 1] = weight[:, i * LANES : (i + 1) * LANES]
+
+
 def weights_body(
     owner, taps, patch, prow, exposure, col_warp, row_warp,
-    ring_ref, own_ref, first_ref, band, cols, rows_ref, select_ref, lines_ref, blocks_ref,
-    owner_ref, taps_ref, patch_ref, prow_ref, first_rows, last_rows, sems,
+    ring_ref, pair_ref, own_ref, first_ref, band, cols, rows_ref, select_ref, lines_ref,
+    blocks_ref, owner_ref, taps_ref, patch_ref, prow_ref, first_rows, last_rows, sems,
 ):
     height, width = exposure.shape
     nb = width // LANES
@@ -91,11 +129,20 @@
         (row_warp, rows_ref),
     ]
     copies = [pltpu.make_async_copy(*move, sems.at[i]) for i, move in enumerate(moves)]
-    for i in (0, 1, 2, 3, 7, 5, 6, 4):
-        copies[i].start()
+    for copy in copies:
+        copy.start()
+    for ref in (ring_ref, pair_ref, own_ref, first_ref, lines_ref):
+        ref[...] = jnp.zeros_like(ref)
 
     copies[0].wait()
     tiles = band_tiles(taps_ref[...].astype(f32))
+    heads = {side: jnp.sum(tile, axis=0, keepdims=True) for side, tile in tiles.items()}
+    blank = jnp.zeros((1, LANES), f32)
+    lines = [
+        jnp.concatenate([heads.get(b - k, blank) for k in range(nb)], axis=1) for b in range(nb)
+    ]
+    lines.append(jnp.zeros((blocks_ref.shape[0] - nb, width), f32))
+    blocks_ref[...] = jnp.concatenate(lines, axis=0)
     tiles = {side: tile.astype(bf16) for side, tile in tiles.items()}
     for i in range(nb):
         for k in range(nb):
@@ -105,17 +152,14 @@
     for copy in copies[1:4]:
         copy.wait()
     me = lax.axis_index("exp")
+    odd = lax.rem(me, 2) == 1
     patch = patch_ref[...]
     slot = jnp.zeros_like(patch)
     for k in range(count):
-        slot = jnp.where(patch == owner_ref[k], place_of(me ^ k, count), slot)
+        slot = jnp.where(patch == owner_ref[k], place_of(me ^ k, count, lax.rem(me, 2)), slot)
     key = slot * PATCH_ROWS + prow_ref[...]
     slots = lax.broadcasted_iota(jnp.int32, select_ref.shape, 0)
     select_ref[...] = jnp.where(slots == key, 1.0, 0.0).astype(bf16)
-
-    for ref in (ring_ref, own_ref, first_ref, blocks_ref, lines_ref):
-        ref[...] = jnp.zeros_like(ref)
-    base = own_ref.shape[0]
 
     copies[5].wait()
     copies[6].wait()
@@ -130,40 +174,29 @@
         first, last = means
         own_ref[b : b + 1] = 0.5 * (first + last)
         first_ref[b : b + 1] = first
-        ring_ref[b : b + 1] = last
+        pair_ref[b : b + 1] = jnp.where(odd, first, last)
+        ring_ref[b : b + 1] = jnp.where(odd, last, 0.0)
+
+    copies[4].wait()
+
+    @pl.when(odd)
+    def _():
+        block_sums([pair_ref, ring_ref], cols, blocks_ref)
 
     copies[7].wait()
-    partial = rows_ref[:, :LANES].astype(f32)
-    for i in range(1, height // LANES):
-        partial += rows_ref[:, i * LANES : (i + 1) * LANES].astype(f32)
-    ones = jnp.ones((2 * SUB, LANES), bf16)
-    high, low = parts_of(partial)
-    high, low = parts_of(lane_dot(ones, high) + lane_dot(ones, low))
-    line = lax.broadcasted_iota(jnp.int32, high.shape, 0)
-    left = jnp.where(line == 0, high.astype(f32), jnp.where(line == 1, low.astype(f32), 1.0))
-    found = lane_dot(left.astype(bf16), select_ref[...])
-    weight = found[0:1] + found[1:2]
-    lines_ref[0:1] = weight
-    lines_ref[1:2] = found[2:3]
-    for i in range(weight.shape[1] // LANES):
-        ring_ref[base + nb * nb + i : base + nb * nb + i + 1] = weight[:, i * LANES : (i + 1) * LANES]
-
-    copies[4].wait()
-    heads = {side: jnp.sum(tile.astype(f32), axis=0, keepdims=True) for side, tile in tiles.items()}
-    blank = jnp.zeros((1, LANES), f32)
-    lines = [
-        jnp.concatenate([heads.get(b - k, blank) for k in range(nb)], axis=1) for b in range(nb)
-    ]
-    lines.append(jnp.zeros((base - nb, width), f32))
-    high, low = parts_of(jnp.concatenate(lines, axis=0))
-    stacked = jnp.concatenate([high.astype(f32), low.astype(f32)], axis=0).astype(bf16)
-    both = jnp.dot(stacked, cols[...], preferred_element_type=f32)
-    total = both[:base] + both[base:]
-    blocks_ref[...] = total
-    for b in range(nb):
-        for c in range(nb):
-            to = base + b * nb + c
-            ring_ref[to : to + 1] = total[b : b + 1, c * LANES : (c + 1) * LANES]
+
+    @pl.when(odd)
+    def _():
+        row_sums([pair_ref, ring_ref], rows_ref, select_ref, lines_ref, blocks_ref)
+
+
+def rest_body(*refs):
+    pair_ref, _, _, _, cols, rows_ref, select_ref, lines_ref, blocks_ref = refs[SHARED:]
+
+    @pl.when(lax.rem(lax.axis_index("exp"), 2) == 0)
+    def _():
+        block_sums([pair_ref], cols, blocks_ref)
+        row_sums([pair_ref], rows_ref, select_ref, lines_ref, blocks_ref)
 
 
 def local_body(
@@ -190,17 +223,26 @@
     )
 
 
-def place_of(mask, count):
-    other, at = mask & 1, lax.shift_right_logical(mask, 1)
-    far = count // 2 - QUAD
-    return jnp.where(at < QUAD, 2 * far + other * QUAD + at, other * far + at - QUAD)
+def place_of(mask, count, kind):
+    other, at = lax.rem(mask, 2), mask // 2
+    far = count // 2 - QUAD
+    wanted = (kind + other) % 2
+    side = (at == 1) | (at == 2)
+    taker = jnp.where(side, at - 1, wanted)
+    index = jnp.where(side, 2 + (wanted + taker) % 2, jnp.where(at == 0, 0, 1))
+    near = 2 * far + (taker + kind) % 2 * QUAD + index
+    return jnp.where(at < QUAD, near, other * far + at - QUAD)
 
 
 def mask_of(place, count):
+    kind = lax.rem(lax.axis_index("exp"), 2)
     far = count // 2 - QUAD
     if place < 2 * far:
         return (place % far + QUAD) * 2 + place // far
-    return (place - 2 * far) % QUAD * 2 + (place - 2 * far) // QUAD
+    part, index = (place - 2 * far) // QUAD, (place - 2 * far) % QUAD
+    if index < 2:
+        return 3 * index * 2 + part
+    return (1 + (kind + part) % 2) * 2 + (part + index) % 2
 
 
 def upright(line, start):
@@ -211,10 +253,19 @@
     return jnp.sum(jnp.where(wanted, line, 0.0), axis=1, keepdims=True)
 
 
+def ring_levels(count, *refs):
+    return Levels(lax.rem(lax.axis_index("exp") + count - 1, count), *refs, count)
+
+
+def pair_levels(count, *refs):
+    return Levels(lax.axis_index("exp") ^ 1, *refs, count)
+
+
 class Levels:
-    def __init__(self, got_ref, first_ref, blocks_ref, lines_ref, count):
+    def __init__(self, sender, got_ref, first_ref, blocks_ref, lines_ref, count):
         nb = blocks_ref.shape[1] // LANES
-        base = first_ref.shape[0]
+        base = -(-nb // SUB) * SUB
+        self.sender = sender
         self.count, self.lines_ref, self.got_ref = count, lines_ref, got_ref
         self.base = base + nb * nb
         self.own, self.other = [], []
@@ -233,8 +284,7 @@
         count, each = self.count, LANES // PATCH_ROWS
         me = lax.axis_index("exp")
         mask = mask_of(j, count)
-        sender = lax.rem(me + count - 1, count)
-        place = place_of(sender ^ me ^ mask, count)
+        place = place_of(self.sender ^ me ^ mask, count, lax.rem(self.sender, 2))
         at = j // each * LANES
         weight = upright(self.lines_ref[0:1, at : at + LANES], j % each * PATCH_ROWS)
         line = self.got_ref[pl.ds(self.base + place // each, 1)]
@@ -250,23 +300,25 @@
 
 
 def put_block(ref, at, size, sums, levels, place, got=None):
-    terms = levels.terms(place)
+    terms = [sum(each[1:], each[0]) for each in zip(*[level.terms(place) for level in levels])]
     for c, term in enumerate(terms):
         to = slice(at * size + c * PATCH_ROWS, at * size + (c + 1) * PATCH_ROWS)
         value = sums[:, c * LANES : (c + 1) * LANES] + term
         ref[to] = value if got is None else value + got[c * PATCH_ROWS : (c + 1) * PATCH_ROWS]
     to = at * size + len(terms) * PATCH_ROWS
-    held = levels.held(place)
+    held = levels[0].held(place)
     ref[to : to + SUB] = held if got is None else held + got[size - SUB :]
 
 
-def far_send_body(count, got_ref, first_ref, blocks_ref, lines_ref, sums_ref, out_ref):
-    far = count // 2 - QUAD
-    size = out_ref.shape[0] // far
-    levels = Levels(got_ref, first_ref, blocks_ref, lines_ref, count)
+def far_send_body(
+    count, size, got_ref, first_ref, blocks_ref, lines_ref, sums_ref, pair_ref, out_ref
+):
+    far = count // 2 - QUAD
+    levels = [ring_levels(count, got_ref, first_ref, blocks_ref, lines_ref)]
     for j in range(far):
         at = (far + j) * PATCH_ROWS
         put_block(out_ref, j, size, sums_ref[at : at + PATCH_ROWS], levels, far + j)
+    out_ref[far * size :] = pair_ref[...]
 
 
 def near_body(
@@ -274,7 +326,7 @@
 ):
     far = count // 2 - QUAD
     size = send_ref.shape[0] // QUAD
-    levels = Levels(got_ref, first_ref, blocks_ref, lines_ref, count)
+    levels = [ring_levels(count, got_ref, first_ref, blocks_ref, lines_ref)]
     near = select[2 * far * PATCH_ROWS :]
     sums = jnp.dot(near, high[...], preferred_element_type=f32) + jnp.dot(
         near, low[...], preferred_element_type=f32
@@ -287,11 +339,14 @@
 
 
 def far_merge_body(
-    count, got_ref, first_ref, blocks_ref, lines_ref, sums_ref, half_ref, *out_refs
-):
-    far = count // 2 - QUAD
-    size = half_ref.shape[0] // far
-    levels = Levels(got_ref, first_ref, blocks_ref, lines_ref, count)
+    count, size, got_ref, first_ref, blocks_ref, lines_ref, sums_ref, pair_ref, half_ref, *out_refs
+):
+    far = count // 2 - QUAD
+    other = half_ref.at[pl.ds(far * size, pair_ref.shape[0])]
+    levels = [
+        ring_levels(count, got_ref, first_ref, blocks_ref, lines_ref),
+        pair_levels(count, other, pair_ref, blocks_ref, lines_ref),
+    ]
     for j in range(far):
         at = j * PATCH_ROWS
         got = half_ref[j * size : (j + 1) * size]
@@ -300,11 +355,27 @@
         )
 
 
-def near_merge_body(keep_ref, got_ref, *out_refs):
-    size = out_refs[0].shape[0]
-    for j, ref in enumerate(out_refs):
-        at = slice(j * size, (j + 1) * size)
-        ref[...] = keep_ref[at] + got_ref[at]
+def near_merge_body(
+    count, blocks_ref, lines_ref, pair_ref, half_ref, keep_ref, got_ref, own_ref, across_ref, side_ref
+):
+    far = count // 2 - QUAD
+    size = own_ref.shape[0]
+    other = half_ref.at[pl.ds(far * size, pair_ref.shape[0])]
+    levels = pair_levels(count, other, pair_ref, blocks_ref, lines_ref)
+    for j, (ref, base) in enumerate(
+        ((own_ref, 0), (across_ref, 0), (side_ref, 0), (side_ref, size))
+    ):
+        terms = levels.terms(2 * far + j)
+        for c, term in enumerate(terms):
+            at = slice(j * size + c * PATCH_ROWS, j * size + (c + 1) * PATCH_ROWS)
+            to = slice(base + c * PATCH_ROWS, base + (c + 1) * PATCH_ROWS)
+            ref[to] = keep_ref[at] + term + got_ref[at]
+        at = slice((j + 1) * size - SUB, (j + 1) * size)
+        ref[base + size - SUB : base + size] = keep_ref[at] + got_ref[at]
+
+
+def second_body(ref, out_ref):
+    out_ref[...] = ref[out_ref.shape[0] :]
 
 
 def far_body(a_ref, b_ref, c_ref, d_ref, *out_refs):
@@ -318,7 +389,7 @@
     out_ref = refs[-1]
     total = refs[0][...]
     for ref in refs[1:-1]:
-        total = total + ref[...]
+        total = total + ref[: total.shape[0]]
     nb = out_ref.shape[1] // LANES
     number = jnp.maximum(upright(total[nb * PATCH_ROWS : nb * PATCH_ROWS + 1], 0), 1.0)
     for c in range(nb):
@@ -341,32 +412,34 @@
         return jax.ShapeDtypeStruct(dims, f32)
 
     tile = shape(-(-nb // SUB) * SUB, LANES)
+    far = half - QUAD
     ring_rows = tile.shape[0] + nb * nb + slots // LANES
-    ring, own, first, band, cols, rows, select, lines, blocks = call(
-        weights_body,
-        [shape(-(-ring_rows // SUB) * SUB, LANES), tile, tile,
-         jax.ShapeDtypeStruct((width, width), bf16), jax.ShapeDtypeStruct(col_warp.shape, bf16),
-         jax.ShapeDtypeStruct(row_warp.shape, bf16),
-         jax.ShapeDtypeStruct((slots, out_rows), bf16), shape(SUB, slots),
-         shape(tile.shape[0], width)],
-        [hbm] * 7,
-        tuple(in_hbm(array) for array in (
-            owner_map, psf_taps, row_patch.reshape(1, out_rows), row_prow.reshape(1, out_rows),
-            exposure, col_warp, row_warp,
-        )),
-        scratch=[
-            pltpu.SMEM(owner_map.shape, jnp.int32),
-            pltpu.VMEM(psf_taps.shape, bf16),
-            pltpu.VMEM((1, out_rows), jnp.int32),
-            pltpu.VMEM((1, out_rows), jnp.int32),
-            pltpu.VMEM((STRIP, width), f32),
-            pltpu.VMEM((STRIP, width), f32),
-            pltpu.SemaphoreType.DMA((8,)),
-        ],
-        flops=2 * width * width * width,
-    )
+    message = shape(-(-ring_rows // SUB) * SUB, LANES)
+    shared = [
+        message, tile, tile, jax.ShapeDtypeStruct((width, width), bf16),
+        jax.ShapeDtypeStruct(col_warp.shape, bf16), jax.ShapeDtypeStruct(row_warp.shape, bf16),
+        jax.ShapeDtypeStruct((slots, out_rows), bf16), shape(SUB, slots),
+        shape(tile.shape[0], width),
+    ]
+    arrays = tuple(in_hbm(array) for array in (
+        owner_map, psf_taps, row_patch.reshape(1, out_rows), row_prow.reshape(1, out_rows),
+        exposure, col_warp, row_warp,
+    ))
+    scratch = [
+        pltpu.SMEM(owner_map.shape, jnp.int32),
+        pltpu.VMEM(psf_taps.shape, bf16),
+        pltpu.VMEM((1, out_rows), jnp.int32),
+        pltpu.VMEM((1, out_rows), jnp.int32),
+        pltpu.VMEM((STRIP, width), f32),
+        pltpu.VMEM((STRIP, width), f32),
+        pltpu.SemaphoreType.DMA((8,)),
+    ]
+    ring, *made = call(weights_body, [message] + shared, [hbm] * 7, arrays, scratch=scratch)
     ring = lax.ppermute(ring, "exp", [(i, (i + 1) % count) for i in range(count)])
-    far = half - QUAD
+    pair, own, first, band, cols, rows, select, lines, blocks = call(
+        rest_body, shared, [vmem] * SHARED, tuple(made),
+        aliases={i: i for i in range(SHARED)},
+    )
     sums, high, low = call(
         local_body,
         [shape(2 * far * PATCH_ROWS, width)] + [jax.ShapeDtypeStruct((out_rows, width), bf16)] * 2,
@@ -376,8 +449,8 @@
     )
     common = (ring, first, blocks, lines)
     far_send = call(
-        functools.partial(far_send_body, count), shape(far * size, LANES), [vmem] * 5,
-        common + (sums,),
+        functools.partial(far_send_body, count, size),
+        shape(far * size + pair.shape[0], LANES), [vmem] * 6, common + (sums, pair),
     )
     far_got = swap(far_send, 1, count)
     near_send, near_keep = call(
@@ -386,15 +459,25 @@
     )
     near_got = swap(near_send, 1, count)
     parts = call(
-        functools.partial(far_merge_body, count),
-        [shape((high_groups - 1) * size, LANES)] * QUAD, [vmem] * 6, common + (sums, far_got),
+        functools.partial(far_merge_body, count, size),
+        [shape((high_groups - 1) * size, LANES)] * QUAD, [vmem] * 7,
+        common + (sums, pair, far_got),
     )
     terms = [parts[0]] + [swap(parts[q], 2 * q, count) for q in FAR_ORDER]
-    near = call(near_merge_body, [shape(size, LANES)] * QUAD, [vmem] * 2, (near_keep, near_got))
-    rest = [near[0]] + [swap(near[q], 2 * q, count) for q in NEAR_ORDER]
-    sent = call(far_body, [shape(size, LANES)] * (high_groups - 1), [vmem] * QUAD, terms)
-    rest = [swap(sent[h - 1], 2 * QUAD * h, count) for h in range(1, high_groups)] + rest
-    return call(final_body, shape(PATCH_ROWS, width), [vmem] * len(rest), tuple(rest))
+    kept, across, side = call(
+        functools.partial(near_merge_body, count),
+        [shape(size, LANES)] * 2 + [shape(2 * size, LANES)], [vmem] * 6,
+        (blocks, lines, pair, far_got, near_keep, near_got),
+    )
+    across = swap(across, 6, count)
+    side = lax.ppermute(side, "exp", [(i, i ^ (4 if i % 2 else 2)) for i in range(count)])
+    sent = call(
+        far_body, [shape(size, LANES)] * (high_groups - 1), [vmem] * QUAD, terms, flops=HOLD
+    )
+    sums = [swap(sent[h - 1], 2 * QUAD * h, count) for h in range(1, high_groups)]
+    passed = swap(call(second_body, shape(size, LANES), [vmem], (side,)), 1, count)
+    rest = (kept, across, side, passed, *sums)
+    return call(final_body, shape(PATCH_ROWS, width), [vmem] * len(rest), rest)
 
 
 def solution(mesh):

time: 24.3 us -> 23.7 us (0.975)
  starting transfers between devices: 10.9 us -> 9.99 us
    ppermute x9 -> x8, starting transfers between devices: 10.4 us -> 7.52 us  [swap(): return lax.ppermute(block, 'exp', [(i, i ^ mask) for i in range(count)])]
    ppermute x0 -> x1, starting transfers between devices: none -> 1.42 us  [on_device(): lax.ppermute(side, 'exp', [(i, i ^ (4 if i % 2 else 2)) for i in range(co...]
    ppermute x1, starting transfers between devices: 0.5 us -> 1.05 us  [on_device(): lax.ppermute(ring, 'exp', [(i, (i + 1) % count) for i in range(count)])]
    ppermute x1, waiting for transfers between devices: 4.39 us -> 3.86 us  [on_device(): lax.ppermute(ring, 'exp', [(i, (i + 1) % count) for i in range(count)])]
    ppermute x0 -> x1, waiting for transfers between devices: none -> 0.4 us  [on_device(): lax.ppermute(side, 'exp', [(i, i ^ (4 if i % 2 else 2)) for i in range(co...]
    ppermute x9 -> x8, waiting for transfers between devices: 3.13 us -> 3.33 us  [swap(): return lax.ppermute(block, 'exp', [(i, i ^ mask) for i in range(count)])]
    pallas_call x8 -> x10, Pallas kernels: 5.61 us -> 5.79 us  [call(): pl.pallas_call(body, out_shape=outs, in_specs=ins, out_specs=jax.tree.map...]
  transfers between devices with their start and end apart: 10 -> 10, of which waited for: 3 -> 6; matrix products, arithmetic and copies ran while one was open for 0% -> 0% of each run, Pallas kernels for 11% -> 14%
where the time goes in v6:
time: 23.7 us; the launch traced here: 23.5 us
  starting transfers between devices  9.99 us (42%)
  waiting for transfers between devices  7.59 us (32%)
  Pallas kernels  5.79 us (24%)
    ppermute x8, starting transfers between devices, swap(): return lax.ppermute(block, 'exp', [(i, i ^ mask) for i in range(count)])  7.52 us
    pallas_call x10, Pallas kernels, call(): pl.pallas_call(body, out_shape=outs, in_specs=ins, out_specs=jax.tree.map...  5.79 us
    ppermute x1, waiting for transfers between devices, on_device(): lax.ppermute(ring, 'exp', [(i, (i + 1) % count) for i in range(count)])  3.86 us
    ppermute x8, waiting for transfers between devices, swap(): return lax.ppermute(block, 'exp', [(i, i ^ mask) for i in range(count)])  3.33 us
    ppermute x1, starting transfers between devices, on_device(): lax.ppermute(side, 'exp', [(i, i ^ (4 if i % 2 else 2)) for i in range(co...  1.42 us
    ppermute x1, starting transfers between devices, on_device(): lax.ppermute(ring, 'exp', [(i, (i + 1) % count) for i in range(count)])  1.05 us
  transfers between devices with their start and end apart: 10, of which 6 were waited for; matrix products, arithmetic and copies ran while one was open for 0% of the time, Pallas kernels for 14%

profile of v6, /device:TPU:0, one launch (start us, length us, event | category | flops | bytes accessed | tf_op | source)
XLA Modules:
  0.0 23.5 jit_solution(4642550864887247374)
XLA Ops:
  0.0 1.5 %shard_map.73 = (f32[32,128]{1,0:T(8,128)S(1)}, f32[32,128]{1,0:T(8,128)S(1)}, f32[8,128]{1,0:T(8,128)S(1)}, f32[8,128]{1,0:T(8,128)S(1)}, bf16[512,512]{1,0:T(8...) custom-call(s32[16]{0:T(128)} %owner.1, ...), custom_call_target="tpu_custom_call" | custom-call | bytes 3674206 | tf_op jit(solution)/shard_map/pallas_call | solution.py:37
  1.5 0.0 copy-start
  1.6 1.0 %collective-permute-start = (f32[32,128]{1,0:T(8,128)S(1)}, f32[32,128]{1,0:T(8,128)S(1)}, u32[]{:S(2)}, u32[]{:S(2)}) collective-permute-start(f32[32,128]{1,0:T(8,128)S(1)} %get-tuple-element.48), channel_id=1, source_target_pairs={{0,1},{1,2},{2,3},{3,4},{4,5},{5,6},{6,7},{7,8},{8,9},{9,10},{10,1... | collective-permute-start | bytes 49160 | tf_op jit(solution)/shard_map/ppermute | solution.py:438
  2.6 0.5 %shard_map.74 = (f32[32,128]{1,0:T(8,128)S(1)}, f32[8,128]{1,0:T(8,128)S(1)}, f32[8,128]{1,0:T(8,128)S(1)}, bf16[512,512]{1,0:T(8,128)(2,1)S(1)}, bf16[512,512]{...) custom-call(f32[32,128]{1,0:T(8,128)S(1)} %get-tuple-element.36.refs, ...), custom_call_target="tpu_custom_call", output_to_operand_aliasing={{0}: (0, {}), {1}: (1, {}), {2}: (2, {}), {3}: (3, {}), {4}... | custom-call | bytes 2678784 | tf_op jit(solution)/shard_map/pallas_call | solution.py:37
  3.1 0.1 copy-done
  3.1 2.0 %shard_map.75 = (f32[256,512]{1,0:T(8,128)S(1)}, bf16[512,512]{1,0:T(8,128)(2,1)S(1)}, bf16[512,512]{1,0:T(8,128)(2,1)S(1)}) custom-call(f32[8,128]{1,0:T(8,128)S(1)} %get-tuple-element.50.own_ref, f32[1024,512]{1,0:T(8,128)S(1)} %copy-done, bf16[512,512]{1,0:T(8,128)(2,1)S(1)} %get-tuple-element.51.band, bf16[512,512]{1,0:T(8,128)(2,1)S(1)} %get-tuple-element.52.cols, ...), custom_call_target="tpu_custom_call" | custom-call | flops 1610612736 | bytes 4722688 | tf_op jit(solution)/shard_map/pallas_call | solution.py:37
  5.1 3.9 %collective-permute-done.got_ref = f32[32,128]{1,0:T(8,128)S(1)} collective-permute-done((f32[32,128]{1,0:T(8,128)S(1)}, f32[32,128]{1,0:T(8,128)S(1)}, u32[]{:S(2)}, u32[]{:S(2)}) %collective-permute-start) | collective-permute-done | bytes 16416 | tf_op jit(solution)/shard_map/ppermute | solution.py:438
  9.0 0.2 shard_map.76
  9.2 0.1 collective-permute-start.1
  9.3 0.5 %shard_map.77 = (f32[544,128]{1,0:T(8,128)S(1)}, f32[544,128]{1,0:T(8,128)S(1)}) custom-call(f32[32,128]{1,0:T(8,128)S(1)} %collective-permute-done.got_ref, f32[8,128]{1,0:T(8,128)S(1)} %get-tuple-element.49.first_ref, f32[8,512]{1,0:T(8,128)S(1)} %get-tuple-element.45.blocks_ref, f32[8,512]{1,0:T(8,128)S(1)} %get-tuple-element.46.lines_ref, ...), custom_call_target="tpu_custom_call" | custom-call | bytes 1626112 | tf_op jit(solution)/shard_map/pallas_call | solution.py:37
  9.7 0.6 %collective-permute-start.2 = (f32[544,128]{1,0:T(8,128)S(1)}, f32[544,128]{1,0:T(8,128)S(1)}, u32[]{:S(2)}, u32[]{:S(2)}) collective-permute-start(f32[544,128]{1,0:T(8,128)S(1)} %get-tuple-element.59), channel_id=1, source_target_pairs={{0,1},{1,0},{2,3},{3,2},{4,5},{5,4},{6,7},{7,6},{8,9},{9,8},{10,11... | collective-permute-start | bytes 835592 | tf_op jit(solution)/shard_map/ppermute | solution.py:31
  10.3 0.6 %collective-permute-done.1.half_ref = f32[576,128]{1,0:T(8,128)S(1)} collective-permute-done((f32[576,128]{1,0:T(8,128)S(1)}, f32[576,128]{1,0:T(8,128)S(1)}, u32[]{:S(2)}, u32[]{:S(2)}) %collective-permute-start.1) | collective-permute-done | bytes 294944 | tf_op jit(solution)/shard_map/ppermute | solution.py:31
  10.8 0.2 shard_map.80
  11.1 0.1 collective-permute-start.6
  11.1 0.7 %collective-permute-start.7 = (f32[136,128]{1,0:T(8,128)S(1)}, f32[136,128]{1,0:T(8,128)S(1)}, u32[]{:S(2)}, u32[]{:S(2)}) collective-permute-start(f32[136,128]{1,0:T(8,128)S(1)} %get-tuple-element.65), channel_id=1, source_target_pairs={{0,2},{1,3},{2,0},{3,1},{4,6},{5,7},{6,4},{7,5},{8,10},{9,11},{10,... | collective-permute-start | bytes 208904 | tf_op jit(solution)/shard_map/ppermute | solution.py:31
  11.8 2.8 %collective-permute-start.8 = (f32[136,128]{1,0:T(8,128)S(1)}, f32[136,128]{1,0:T(8,128)S(1)}, u32[]{:S(2)}, u32[]{:S(2)}) collective-permute-start(f32[136,128]{1,0:T(8,128)S(1)} %get-tuple-element.66), channel_id=1, source_target_pairs={{0,6},{1,7},{2,4},{3,5},{4,2},{5,3},{6,0},{7,1},{8,14},{9,15},{10,... | collective-permute-start | bytes 208904 | tf_op jit(solution)/shard_map/ppermute | solution.py:31
  14.6 0.0 collective-permute-done.2.got_ref
  14.6 0.2 shard_map.78
  14.8 0.2 collective-permute-start.3
  15.0 1.4 %collective-permute-start.4 = (f32[272,128]{1,0:T(8,128)S(1)}, f32[272,128]{1,0:T(8,128)S(1)}, u32[]{:S(2)}, u32[]{:S(2)}) collective-permute-start(f32[272,128]{1,0:T(8,128)S(1)} %get-tuple-element.62), channel_id=1, source_target_pairs={{0,2},{1,5},{2,0},{3,7},{4,6},{5,1},{6,4},{7,3},{8,10},{9,13},{10,... | collective-permute-start | bytes 417800 | tf_op jit(solution)/shard_map/ppermute | solution.py:473
  16.4 0.0 collective-permute-done.6.b_ref
  16.4 0.0 collective-permute-done.7.c_ref
  16.4 0.8 %collective-permute-done.8.d_ref = f32[136,128]{1,0:T(8,128)S(1)} collective-permute-done((f32[136,128]{1,0:T(8,128)S(1)}, f32[136,128]{1,0:T(8,128)S(1)}, u32[]{:S(2)}, u32[]{:S(2)}) %collective-permute-start.8) | collective-permute-done | bytes 69664 | tf_op jit(solution)/shard_map/ppermute | solution.py:31
  17.3 3.1 %collective-permute-start.9 = (f32[136,128]{1,0:T(8,128)S(1)}, f32[136,128]{1,0:T(8,128)S(1)}, u32[]{:S(2)}, u32[]{:S(2)}) collective-permute-start(f32[136,128]{1,0:T(8,128)S(1)} %shard_map.81), channel_id=1, source_target_pairs={{0,8},{1,9},{2,10},{3,11},{4,12},{5,13},{6,14},{7,15},{8,0},{9,1},... | collective-permute-start | bytes 208904 | tf_op jit(solution)/shard_map/ppermute | solution.py:31
  20.3 0.4 %collective-permute-done.4.ref.refs_2_ = f32[272,128]{1,0:T(8,128)S(1)} collective-permute-done((f32[272,128]{1,0:T(8,128)S(1)}, f32[272,128]{1,0:T(8,128)S(1)}, u32[]{:S(2)}, u32[]{:S(2)}) %collective-permute-start.4) | collective-permute-done | bytes 139296 | tf_op jit(solution)/shard_map/ppermute | solution.py:473
  20.7 0.1 collective-permute-start.5
  20.8 0.5 %collective-permute-done.3.refs_1_ = f32[136,128]{1,0:T(8,128)S(1)} collective-permute-done((f32[136,128]{1,0:T(8,128)S(1)}, f32[136,128]{1,0:T(8,128)S(1)}, u32[]{:S(2)}, u32[]{:S(2)}) %collective-permute-start.3) | collective-permute-done | bytes 69664 | tf_op jit(solution)/shard_map/ppermute | solution.py:31
  21.4 1.4 %collective-permute-done.9.refs_4_ = f32[136,128]{1,0:T(8,128)S(1)} collective-permute-done((f32[136,128]{1,0:T(8,128)S(1)}, f32[136,128]{1,0:T(8,128)S(1)}, u32[]{:S(2)}, u32[]{:S(2)}) %collective-permute-start.9) | collective-permute-done | bytes 69664 | tf_op jit(solution)/shard_map/ppermute | solution.py:31
  22.8 0.0 collective-permute-done.5.refs_3_
  22.8 0.7 %shard_map.82 = f32[32,512]{1,0:T(8,128)} custom-call(f32[136,128]{1,0:T(8,128)S(1)} %get-tuple-element.60.refs_0_, f32[136,128]{1,0:T(8,128)S(1)} %collective-permute-done.3.refs_1_, f32[272,128]{1,0:T(8,128)S(1)} %collective-permute-done.4.ref.refs_2_, f32[136,128]{1,0:T(8,128)S(1)} %collective-permute-done.5.refs_3_, ...), custom_call_target="tpu_custom_call" | custom-call | bytes 417792 | tf_op jit(solution)/shard_map/pallas_call | solution.py:37
  (2 shorter events, 0.0 us)
Async XLA Ops:
  1.5 1.6 %copy-start = (f32[1024,512]{1,0:T(8,128)S(1)}, f32[1024,512]{1,0:T(8,128)}, u32[]{:S(2)}) copy-start(f32[1024,512]{1,0:T(8,128)} %image.1) | copy-start | bytes 6291460
  1.6 7.4 %collective-permute-start = (f32[32,128]{1,0:T(8,128)S(1)}, f32[32,128]{1,0:T(8,128)S(1)}, u32[]{:S(2)}, u32[]{:S(2)}) collective-permute-start(f32[32,128]{1,0:T(8,128)S(1)} %get-tuple-element.48), channel_id=1, source_target_pairs={{0,1},{1,2},{2,3},{3,4},{4,5},{5,6},{6,7},{7,8},{8,9},{9,10},{10,1... | collective-permute-start | bytes 49160 | tf_op jit(solution)/shard_map/ppermute | solution.py:438
  9.2 1.6 %collective-permute-start.1 = (f32[576,128]{1,0:T(8,128)S(1)}, f32[576,128]{1,0:T(8,128)S(1)}, u32[]{:S(2)}, u32[]{:S(2)}) collective-permute-start(f32[576,128]{1,0:T(8,128)S(1)} %shard_map.76), channel_id=1, source_target_pairs={{0,1},{1,0},{2,3},{3,2},{4,5},{5,4},{6,7},{7,6},{8,9},{9,8},{10,11... | collective-permute-start | bytes 884744 | tf_op jit(solution)/shard_map/ppermute | solution.py:31
  9.7 4.9 %collective-permute-start.2 = (f32[544,128]{1,0:T(8,128)S(1)}, f32[544,128]{1,0:T(8,128)S(1)}, u32[]{:S(2)}, u32[]{:S(2)}) collective-permute-start(f32[544,128]{1,0:T(8,128)S(1)} %get-tuple-element.59), channel_id=1, source_target_pairs={{0,1},{1,0},{2,3},{3,2},{4,5},{5,4},{6,7},{7,6},{8,9},{9,8},{10,11... | collective-permute-start | bytes 835592 | tf_op jit(solution)/shard_map/ppermute | solution.py:31
  11.1 5.3 %collective-permute-start.6 = (f32[136,128]{1,0:T(8,128)S(1)}, f32[136,128]{1,0:T(8,128)S(1)}, u32[]{:S(2)}, u32[]{:S(2)}) collective-permute-start(f32[136,128]{1,0:T(8,128)S(1)} %get-tuple-element.64), channel_id=1, source_target_pairs={{0,4},{1,5},{2,6},{3,7},{4,0},{5,1},{6,2},{7,3},{8,12},{9,13},{10,... | collective-permute-start | bytes 208904 | tf_op jit(solution)/shard_map/ppermute | solution.py:31
  11.1 5.3 %collective-permute-start.7 = (f32[136,128]{1,0:T(8,128)S(1)}, f32[136,128]{1,0:T(8,128)S(1)}, u32[]{:S(2)}, u32[]{:S(2)}) collective-permute-start(f32[136,128]{1,0:T(8,128)S(1)} %get-tuple-element.65), channel_id=1, source_target_pairs={{0,2},{1,3},{2,0},{3,1},{4,6},{5,7},{6,4},{7,5},{8,10},{9,11},{10,... | collective-permute-start | bytes 208904 | tf_op jit(solution)/shard_map/ppermute | solution.py:31
  11.8 5.4 %collective-permute-start.8 = (f32[136,128]{1,0:T(8,128)S(1)}, f32[136,128]{1,0:T(8,128)S(1)}, u32[]{:S(2)}, u32[]{:S(2)}) collective-permute-start(f32[136,128]{1,0:T(8,128)S(1)} %get-tuple-element.66), channel_id=1, source_target_pairs={{0,6},{1,7},{2,4},{3,5},{4,2},{5,3},{6,0},{7,1},{8,14},{9,15},{10,... | collective-permute-start | bytes 208904 | tf_op jit(solution)/shard_map/ppermute | solution.py:31
  14.8 6.6 %collective-permute-start.3 = (f32[136,128]{1,0:T(8,128)S(1)}, f32[136,128]{1,0:T(8,128)S(1)}, u32[]{:S(2)}, u32[]{:S(2)}) collective-permute-start(f32[136,128]{1,0:T(8,128)S(1)} %get-tuple-element.61), channel_id=1, source_target_pairs={{0,6},{1,7},{2,4},{3,5},{4,2},{5,3},{6,0},{7,1},{8,14},{9,15},{10,... | collective-permute-start | bytes 208904 | tf_op jit(solution)/shard_map/ppermute | solution.py:31
  15.0 5.8 %collective-permute-start.4 = (f32[272,128]{1,0:T(8,128)S(1)}, f32[272,128]{1,0:T(8,128)S(1)}, u32[]{:S(2)}, u32[]{:S(2)}) collective-permute-start(f32[272,128]{1,0:T(8,128)S(1)} %get-tuple-element.62), channel_id=1, source_target_pairs={{0,2},{1,5},{2,0},{3,7},{4,6},{5,1},{6,4},{7,3},{8,10},{9,13},{10,... | collective-permute-start | bytes 417800 | tf_op jit(solution)/shard_map/ppermute | solution.py:473
  17.3 5.5 %collective-permute-start.9 = (f32[136,128]{1,0:T(8,128)S(1)}, f32[136,128]{1,0:T(8,128)S(1)}, u32[]{:S(2)}, u32[]{:S(2)}) collective-permute-start(f32[136,128]{1,0:T(8,128)S(1)} %shard_map.81), channel_id=1, source_target_pairs={{0,8},{1,9},{2,10},{3,11},{4,12},{5,13},{6,14},{7,15},{8,0},{9,1},... | collective-permute-start | bytes 208904 | tf_op jit(solution)/shard_map/ppermute | solution.py:31
  20.7 2.0 %collective-permute-start.5 = (f32[136,128]{1,0:T(8,128)S(1)}, f32[136,128]{1,0:T(8,128)S(1)}, u32[]{:S(2)}, u32[]{:S(2)}) collective-permute-start(f32[136,128]{1,0:T(8,128)S(1)} %shard_map.79), channel_id=1, source_target_pairs={{0,1},{1,0},{2,3},{3,2},{4,5},{5,4},{6,7},{7,6},{8,9},{9,8},{10,11... | collective-permute-start | bytes 208904 | tf_op jit(solution)/shard_map/ppermute | solution.py:31

commit v7 on v6

--- a/solution.py
+++ b/solution.py
@@ -15,7 +15,7 @@
 CHUNKS = 4
 QUAD = 4
 SHARED = 9
-FAR_ORDER = (2, 1, 3)
+FAR_ORDER = (3, 1, 2)
 HOLD = 4_000_000_000
 VMEM_LIMIT = 32 * 1024 * 1024
 
@@ -338,21 +338,25 @@
             put_block(ref, j, size, sums[at : at + PATCH_ROWS], levels, place)
 
 
-def far_merge_body(
-    count, size, got_ref, first_ref, blocks_ref, lines_ref, sums_ref, pair_ref, half_ref, *out_refs
-):
+def far_keep_body(count, size, got_ref, first_ref, blocks_ref, lines_ref, sums_ref, out_ref):
+    levels = [ring_levels(count, got_ref, first_ref, blocks_ref, lines_ref)]
+    for j in range(count // 2 - QUAD):
+        at = j * PATCH_ROWS
+        put_block(out_ref, j, size, sums_ref[at : at + PATCH_ROWS], levels, j)
+
+
+def far_merge_body(count, size, blocks_ref, lines_ref, pair_ref, keep_ref, half_ref, *out_refs):
     far = count // 2 - QUAD
     other = half_ref.at[pl.ds(far * size, pair_ref.shape[0])]
-    levels = [
-        ring_levels(count, got_ref, first_ref, blocks_ref, lines_ref),
-        pair_levels(count, other, pair_ref, blocks_ref, lines_ref),
-    ]
+    levels = pair_levels(count, other, pair_ref, blocks_ref, lines_ref)
     for j in range(far):
-        at = j * PATCH_ROWS
-        got = half_ref[j * size : (j + 1) * size]
-        put_block(
-            out_refs[j % QUAD], j // QUAD, size, sums_ref[at : at + PATCH_ROWS], levels, j, got
-        )
+        ref, base = out_refs[j % QUAD], j // QUAD * size
+        for c, term in enumerate(levels.terms(j)):
+            at = slice(j * size + c * PATCH_ROWS, j * size + (c + 1) * PATCH_ROWS)
+            to = slice(base + c * PATCH_ROWS, base + (c + 1) * PATCH_ROWS)
+            ref[to] = keep_ref[at] + term + half_ref[at]
+        at = slice((j + 1) * size - SUB, (j + 1) * size)
+        ref[base + size - SUB : base + size] = keep_ref[at] + half_ref[at]
 
 
 def near_merge_body(
@@ -452,7 +456,12 @@
         functools.partial(far_send_body, count, size),
         shape(far * size + pair.shape[0], LANES), [vmem] * 6, common + (sums, pair),
     )
+    far_send, kept_sums = lax.optimization_barrier((far_send, sums))
     far_got = swap(far_send, 1, count)
+    far_keep = call(
+        functools.partial(far_keep_body, count, size), shape(far * size, LANES), [vmem] * 5,
+        common + (kept_sums,),
+    )
     near_send, near_keep = call(
         functools.partial(near_body, count), [shape(QUAD * size, LANES)] * 2, [vmem] * 7,
         common + (select, high, low),
@@ -460,8 +469,8 @@
     near_got = swap(near_send, 1, count)
     parts = call(
         functools.partial(far_merge_body, count, size),
-        [shape((high_groups - 1) * size, LANES)] * QUAD, [vmem] * 7,
-        common + (sums, pair, far_got),
+        [shape((high_groups - 1) * size, LANES)] * QUAD, [vmem] * 5,
+        (blocks, lines, pair, far_keep, far_got),
     )
     terms = [parts[0]] + [swap(parts[q], 2 * q, count) for q in FAR_ORDER]
     kept, across, side = call(
@@ -469,6 +478,7 @@
         [shape(size, LANES)] * 2 + [shape(2 * size, LANES)], [vmem] * 6,
         (blocks, lines, pair, far_got, near_keep, near_got),
     )
+    across, terms[1] = lax.optimization_barrier((across, terms[1]))
     across = swap(across, 6, count)
     side = lax.ppermute(side, "exp", [(i, i ^ (4 if i % 2 else 2)) for i in range(count)])
     sent = call(

time: 23.7 us -> 23.5 us (level)
  starting transfers between devices: 9.99 us -> 8.12 us
  waiting for transfers between devices: 7.59 us -> 9.21 us
    ppermute x8, waiting for transfers between devices: 3.33 us -> 4.78 us  [swap(): return lax.ppermute(block, 'exp', [(i, i ^ mask) for i in range(count)])]
    ppermute x1, starting transfers between devices: 1.42 us -> 0.07 us  [on_device(): lax.ppermute(side, 'exp', [(i, i ^ (4 if i % 2 else 2)) for i in range(co...]
    ppermute x8, starting transfers between devices: 7.52 us -> 7 us  [swap(): return lax.ppermute(block, 'exp', [(i, i ^ mask) for i in range(count)])]
    pallas_call x10 -> x11, Pallas kernels: 5.79 us -> 5.88 us  [call(): pl.pallas_call(body, out_shape=outs, in_specs=ins, out_specs=jax.tree.map...]
  transfers between devices with their start and end apart: 10 -> 10, of which waited for: 6 -> 7; matrix products, arithmetic and copies ran while one was open for 0% -> 0% of each run, Pallas kernels for 14% -> 15%
where the time goes in v7:
time: 23.5 us; the launch traced here: 23.3 us
  waiting for transfers between devices  9.21 us (39%)
  starting transfers between devices  8.12 us (35%)
  Pallas kernels  5.88 us (25%)
    ppermute x8, starting transfers between devices, swap(): return lax.ppermute(block, 'exp', [(i, i ^ mask) for i in range(count)])  7 us
    pallas_call x11, Pallas kernels, call(): pl.pallas_call(body, out_shape=outs, in_specs=ins, out_specs=jax.tree.map...  5.88 us
    ppermute x8, waiting for transfers between devices, swap(): return lax.ppermute(block, 'exp', [(i, i ^ mask) for i in range(count)])  4.78 us
    ppermute x1, waiting for transfers between devices, on_device(): lax.ppermute(ring, 'exp', [(i, (i + 1) % count) for i in range(count)])  3.86 us
    ppermute x1, starting transfers between devices, on_device(): lax.ppermute(ring, 'exp', [(i, (i + 1) % count) for i in range(count)])  1.05 us
    ppermute x1, waiting for transfers between devices, on_device(): lax.ppermute(side, 'exp', [(i, i ^ (4 if i % 2 else 2)) for i in range(co...  0.57 us
  transfers between devices with their start and end apart: 10, of which 7 were waited for; matrix products, arithmetic and copies ran while one was open for 0% of the time, Pallas kernels for 15%

profile of v7, /device:TPU:0, one launch (start us, length us, event | category | flops | bytes accessed | tf_op | source)
XLA Modules:
  0.0 23.3 jit_solution(10795058829382761918)
XLA Ops:
  0.0 1.5 %shard_map.73 = (f32[32,128]{1,0:T(8,128)S(1)}, f32[32,128]{1,0:T(8,128)S(1)}, f32[8,128]{1,0:T(8,128)S(1)}, f32[8,128]{1,0:T(8,128)S(1)}, bf16[512,512]{1,0:T(8...) custom-call(s32[16]{0:T(128)} %owner.1, ...), custom_call_target="tpu_custom_call" | custom-call | bytes 3674206 | tf_op jit(solution)/shard_map/pallas_call | solution.py:37
  1.5 0.0 copy-start
  1.6 1.0 %collective-permute-start = (f32[32,128]{1,0:T(8,128)S(1)}, f32[32,128]{1,0:T(8,128)S(1)}, u32[]{:S(2)}, u32[]{:S(2)}) collective-permute-start(f32[32,128]{1,0:T(8,128)S(1)} %get-tuple-element.52), channel_id=1, source_target_pairs={{0,1},{1,2},{2,3},{3,4},{4,5},{5,6},{6,7},{7,8},{8,9},{9,10},{10,1... | collective-permute-start | bytes 49160 | tf_op jit(solution)/shard_map/ppermute | solution.py:442
  2.6 0.5 %shard_map.74 = (f32[32,128]{1,0:T(8,128)S(1)}, f32[8,128]{1,0:T(8,128)S(1)}, f32[8,128]{1,0:T(8,128)S(1)}, bf16[512,512]{1,0:T(8,128)(2,1)S(1)}, bf16[512,512]{...) custom-call(f32[32,128]{1,0:T(8,128)S(1)} %get-tuple-element.40.refs, ...), custom_call_target="tpu_custom_call", output_to_operand_aliasing={{0}: (0, {}), {1}: (1, {}), {2}: (2, {}), {3}: (3, {}), {4}... | custom-call | bytes 2678784 | tf_op jit(solution)/shard_map/pallas_call | solution.py:37
  3.1 0.1 copy-done
  3.1 2.0 %shard_map.75 = (f32[256,512]{1,0:T(8,128)S(1)}, bf16[512,512]{1,0:T(8,128)(2,1)S(1)}, bf16[512,512]{1,0:T(8,128)(2,1)S(1)}) custom-call(f32[8,128]{1,0:T(8,128)S(1)} %get-tuple-element.54.own_ref, f32[1024,512]{1,0:T(8,128)S(1)} %copy-done, bf16[512,512]{1,0:T(8,128)(2,1)S(1)} %get-tuple-element.55.band, bf16[512,512]{1,0:T(8,128)(2,1)S(1)} %get-tuple-element.56.cols, ...), custom_call_target="tpu_custom_call" | custom-call | flops 1610612736 | bytes 4722688 | tf_op jit(solution)/shard_map/pallas_call | solution.py:37
  5.1 3.9 %collective-permute-done.got_ref = f32[32,128]{1,0:T(8,128)S(1)} collective-permute-done((f32[32,128]{1,0:T(8,128)S(1)}, f32[32,128]{1,0:T(8,128)S(1)}, u32[]{:S(2)}, u32[]{:S(2)}) %collective-permute-start) | collective-permute-done | bytes 16416 | tf_op jit(solution)/shard_map/ppermute | solution.py:442
  9.0 0.2 shard_map.76
  9.2 0.1 collective-permute-start.1
  9.3 0.5 %shard_map.77 = (f32[544,128]{1,0:T(8,128)S(1)}, f32[544,128]{1,0:T(8,128)S(1)}) custom-call(f32[32,128]{1,0:T(8,128)S(1)} %collective-permute-done.got_ref, f32[8,128]{1,0:T(8,128)S(1)} %get-tuple-element.53.first_ref, f32[8,512]{1,0:T(8,128)S(1)} %get-tuple-element.49.blocks_ref, f32[8,512]{1,0:T(8,128)S(1)} %get-tuple-element.50.lines_ref, ...), custom_call_target="tpu_custom_call" | custom-call | bytes 1626112 | tf_op jit(solution)/shard_map/pallas_call | solution.py:37
  9.7 0.6 %collective-permute-start.2 = (f32[544,128]{1,0:T(8,128)S(1)}, f32[544,128]{1,0:T(8,128)S(1)}, u32[]{:S(2)}, u32[]{:S(2)}) collective-permute-start(f32[544,128]{1,0:T(8,128)S(1)} %get-tuple-element.64), channel_id=1, source_target_pairs={{0,1},{1,0},{2,3},{3,2},{4,5},{5,4},{6,7},{7,6},{8,9},{9,8},{10,11... | collective-permute-start | bytes 835592 | tf_op jit(solution)/shard_map/ppermute | solution.py:31
  10.3 0.2 shard_map.79.keep_ref
  10.5 0.4 %collective-permute-done.1.half_ref = f32[576,128]{1,0:T(8,128)S(1)} collective-permute-done((f32[576,128]{1,0:T(8,128)S(1)}, f32[576,128]{1,0:T(8,128)S(1)}, u32[]{:S(2)}, u32[]{:S(2)}) %collective-permute-start.1) | collective-permute-done | bytes 294944 | tf_op jit(solution)/shard_map/ppermute | solution.py:31
  10.8 0.1 shard_map.80
  11.0 0.2 collective-permute-start.3
  11.2 1.0 %collective-permute-start.7 = (f32[136,128]{1,0:T(8,128)S(1)}, f32[136,128]{1,0:T(8,128)S(1)}, u32[]{:S(2)}, u32[]{:S(2)}) collective-permute-start(f32[136,128]{1,0:T(8,128)S(1)} %get-tuple-element.73), channel_id=1, source_target_pairs={{0,2},{1,3},{2,0},{3,1},{4,6},{5,7},{6,4},{7,5},{8,10},{9,11},{10,... | collective-permute-start | bytes 208904 | tf_op jit(solution)/shard_map/ppermute | solution.py:31
  12.2 2.3 %collective-permute-start.8 = (f32[136,128]{1,0:T(8,128)S(1)}, f32[136,128]{1,0:T(8,128)S(1)}, u32[]{:S(2)}, u32[]{:S(2)}) collective-permute-start(f32[136,128]{1,0:T(8,128)S(1)} %get-tuple-element.74), channel_id=1, source_target_pairs={{0,4},{1,5},{2,6},{3,7},{4,0},{5,1},{6,2},{7,3},{8,12},{9,13},{10,... | collective-permute-start | bytes 208904 | tf_op jit(solution)/shard_map/ppermute | solution.py:31
  14.5 0.0 collective-permute-done.2.got_ref
  14.5 0.2 shard_map.78
  14.7 0.1 collective-permute-start.5
  14.8 2.2 %collective-permute-done.3.b_ref = f32[136,128]{1,0:T(8,128)S(1)} collective-permute-done((f32[136,128]{1,0:T(8,128)S(1)}, f32[136,128]{1,0:T(8,128)S(1)}, u32[]{:S(2)}, u32[]{:S(2)}) %collective-permute-start.3) | collective-permute-done | bytes 69664 | tf_op jit(solution)/shard_map/ppermute | solution.py:31
  17.0 0.0 collective-permute-start.4
  17.0 0.0 collective-permute-done.7.c_ref
  17.0 0.2 collective-permute-done.8.d_ref
  17.2 2.8 %collective-permute-start.9 = (f32[136,128]{1,0:T(8,128)S(1)}, f32[136,128]{1,0:T(8,128)S(1)}, u32[]{:S(2)}, u32[]{:S(2)}) collective-permute-start(f32[136,128]{1,0:T(8,128)S(1)} %shard_map.82), channel_id=1, source_target_pairs={{0,8},{1,9},{2,10},{3,11},{4,12},{5,13},{6,14},{7,15},{8,0},{9,1},... | collective-permute-start | bytes 208904 | tf_op jit(solution)/shard_map/ppermute | solution.py:31
  20.0 0.6 %collective-permute-done.5.ref.refs_2_ = f32[272,128]{1,0:T(8,128)S(1)} collective-permute-done((f32[272,128]{1,0:T(8,128)S(1)}, f32[272,128]{1,0:T(8,128)S(1)}, u32[]{:S(2)}, u32[]{:S(2)}) %collective-permute-start.5) | collective-permute-done | bytes 139296 | tf_op jit(solution)/shard_map/ppermute | solution.py:483
  20.6 0.0 collective-permute-start.6
  20.6 1.6 %collective-permute-done.4.refs_1_ = f32[136,128]{1,0:T(8,128)S(1)} collective-permute-done((f32[136,128]{1,0:T(8,128)S(1)}, f32[136,128]{1,0:T(8,128)S(1)}, u32[]{:S(2)}, u32[]{:S(2)}) %collective-permute-start.4) | collective-permute-done | bytes 69664 | tf_op jit(solution)/shard_map/ppermute | solution.py:31
  22.2 0.4 %collective-permute-done.9.refs_4_ = f32[136,128]{1,0:T(8,128)S(1)} collective-permute-done((f32[136,128]{1,0:T(8,128)S(1)}, f32[136,128]{1,0:T(8,128)S(1)}, u32[]{:S(2)}, u32[]{:S(2)}) %collective-permute-start.9) | collective-permute-done | bytes 69664 | tf_op jit(solution)/shard_map/ppermute | solution.py:31
  22.6 0.0 collective-permute-done.6.refs_3_
  22.6 0.7 %shard_map.83 = f32[32,512]{1,0:T(8,128)} custom-call(f32[136,128]{1,0:T(8,128)S(1)} %get-tuple-element.65.refs_0_, f32[136,128]{1,0:T(8,128)S(1)} %collective-permute-done.4.refs_1_, f32[272,128]{1,0:T(8,128)S(1)} %collective-permute-done.5.ref.refs_2_, f32[136,128]{1,0:T(8,128)S(1)} %collective-permute-done.6.refs_3_, ...), custom_call_target="tpu_custom_call" | custom-call | bytes 417792 | tf_op jit(solution)/shard_map/pallas_call | solution.py:37
  (2 shorter events, 0.0 us)
Async XLA Ops:
  1.5 1.6 %copy-start = (f32[1024,512]{1,0:T(8,128)S(1)}, f32[1024,512]{1,0:T(8,128)}, u32[]{:S(2)}) copy-start(f32[1024,512]{1,0:T(8,128)} %image.1) | copy-start | bytes 6291460
  1.6 7.4 %collective-permute-start = (f32[32,128]{1,0:T(8,128)S(1)}, f32[32,128]{1,0:T(8,128)S(1)}, u32[]{:S(2)}, u32[]{:S(2)}) collective-permute-start(f32[32,128]{1,0:T(8,128)S(1)} %get-tuple-element.52), channel_id=1, source_target_pairs={{0,1},{1,2},{2,3},{3,4},{4,5},{5,6},{6,7},{7,8},{8,9},{9,10},{10,1... | collective-permute-start | bytes 49160 | tf_op jit(solution)/shard_map/ppermute | solution.py:442
  9.2 1.6 %collective-permute-start.1 = (f32[576,128]{1,0:T(8,128)S(1)}, f32[576,128]{1,0:T(8,128)S(1)}, u32[]{:S(2)}, u32[]{:S(2)}) collective-permute-start(f32[576,128]{1,0:T(8,128)S(1)} %shard_map.76), channel_id=1, source_target_pairs={{0,1},{1,0},{2,3},{3,2},{4,5},{5,4},{6,7},{7,6},{8,9},{9,8},{10,11... | collective-permute-start | bytes 884744 | tf_op jit(solution)/shard_map/ppermute | solution.py:31
  9.7 4.8 %collective-permute-start.2 = (f32[544,128]{1,0:T(8,128)S(1)}, f32[544,128]{1,0:T(8,128)S(1)}, u32[]{:S(2)}, u32[]{:S(2)}) collective-permute-start(f32[544,128]{1,0:T(8,128)S(1)} %get-tuple-element.64), channel_id=1, source_target_pairs={{0,1},{1,0},{2,3},{3,2},{4,5},{5,4},{6,7},{7,6},{8,9},{9,8},{10,11... | collective-permute-start | bytes 835592 | tf_op jit(solution)/shard_map/ppermute | solution.py:31
  11.0 6.0 %collective-permute-start.3 = (f32[136,128]{1,0:T(8,128)S(1)}, f32[136,128]{1,0:T(8,128)S(1)}, u32[]{:S(2)}, u32[]{:S(2)}) collective-permute-start(f32[136,128]{1,0:T(8,128)S(1)} %get-tuple-element.68), channel_id=1, source_target_pairs={{0,6},{1,7},{2,4},{3,5},{4,2},{5,3},{6,0},{7,1},{8,14},{9,15},{10,... | collective-permute-start | bytes 208904 | tf_op jit(solution)/shard_map/ppermute | solution.py:31
  11.2 5.8 %collective-permute-start.7 = (f32[136,128]{1,0:T(8,128)S(1)}, f32[136,128]{1,0:T(8,128)S(1)}, u32[]{:S(2)}, u32[]{:S(2)}) collective-permute-start(f32[136,128]{1,0:T(8,128)S(1)} %get-tuple-element.73), channel_id=1, source_target_pairs={{0,2},{1,3},{2,0},{3,1},{4,6},{5,7},{6,4},{7,5},{8,10},{9,11},{10,... | collective-permute-start | bytes 208904 | tf_op jit(solution)/shard_map/ppermute | solution.py:31
  12.2 4.9 %collective-permute-start.8 = (f32[136,128]{1,0:T(8,128)S(1)}, f32[136,128]{1,0:T(8,128)S(1)}, u32[]{:S(2)}, u32[]{:S(2)}) collective-permute-start(f32[136,128]{1,0:T(8,128)S(1)} %get-tuple-element.74), channel_id=1, source_target_pairs={{0,4},{1,5},{2,6},{3,7},{4,0},{5,1},{6,2},{7,3},{8,12},{9,13},{10,... | collective-permute-start | bytes 208904 | tf_op jit(solution)/shard_map/ppermute | solution.py:31
  14.7 5.9 %collective-permute-start.5 = (f32[272,128]{1,0:T(8,128)S(1)}, f32[272,128]{1,0:T(8,128)S(1)}, u32[]{:S(2)}, u32[]{:S(2)}) collective-permute-start(f32[272,128]{1,0:T(8,128)S(1)} %get-tuple-element.70), channel_id=1, source_target_pairs={{0,2},{1,5},{2,0},{3,7},{4,6},{5,1},{6,4},{7,3},{8,10},{9,13},{10,... | collective-permute-start | bytes 417800 | tf_op jit(solution)/shard_map/ppermute | solution.py:483
  17.0 5.2 %collective-permute-start.4 = (f32[136,128]{1,0:T(8,128)S(1)}, f32[136,128]{1,0:T(8,128)S(1)}, u32[]{:S(2)}, u32[]{:S(2)}) collective-permute-start(f32[136,128]{1,0:T(8,128)S(1)} %get-tuple-element.69), channel_id=1, source_target_pairs={{0,6},{1,7},{2,4},{3,5},{4,2},{5,3},{6,0},{7,1},{8,14},{9,15},{10,... | collective-permute-start | bytes 208904 | tf_op jit(solution)/shard_map/ppermute | solution.py:31
  17.2 5.4 %collective-permute-start.9 = (f32[136,128]{1,0:T(8,128)S(1)}, f32[136,128]{1,0:T(8,128)S(1)}, u32[]{:S(2)}, u32[]{:S(2)}) collective-permute-start(f32[136,128]{1,0:T(8,128)S(1)} %shard_map.82), channel_id=1, source_target_pairs={{0,8},{1,9},{2,10},{3,11},{4,12},{5,13},{6,14},{7,15},{8,0},{9,1},... | collective-permute-start | bytes 208904 | tf_op jit(solution)/shard_map/ppermute | solution.py:31
  20.6 2.1 %collective-permute-start.6 = (f32[136,128]{1,0:T(8,128)S(1)}, f32[136,128]{1,0:T(8,128)S(1)}, u32[]{:S(2)}, u32[]{:S(2)}) collective-permute-start(f32[136,128]{1,0:T(8,128)S(1)} %shard_map.81), channel_id=1, source_target_pairs={{0,1},{1,0},{2,3},{3,2},{4,5},{5,4},{6,7},{7,6},{8,9},{9,8},{10,11... | collective-permute-start | bytes 208904 | tf_op jit(solution)/shard_map/ppermute | solution.py:31

commit v8 on v7

--- a/solution.py
+++ b/solution.py
@@ -228,7 +228,7 @@
     far = count // 2 - QUAD
     wanted = (kind + other) % 2
     side = (at == 1) | (at == 2)
-    taker = jnp.where(side, at - 1, wanted)
+    taker = jnp.where(side, 2 - at, wanted)
     index = jnp.where(side, 2 + (wanted + taker) % 2, jnp.where(at == 0, 0, 1))
     near = 2 * far + (taker + kind) % 2 * QUAD + index
     return jnp.where(at < QUAD, near, other * far + at - QUAD)
@@ -242,7 +242,7 @@
     part, index = (place - 2 * far) // QUAD, (place - 2 * far) % QUAD
     if index < 2:
         return 3 * index * 2 + part
-    return (1 + (kind + part) % 2) * 2 + (part + index) % 2
+    return (2 - (kind + part) % 2) * 2 + (part + index) % 2
 
 
 def upright(line, start):
@@ -480,7 +480,7 @@
     )
     across, terms[1] = lax.optimization_barrier((across, terms[1]))
     across = swap(across, 6, count)
-    side = lax.ppermute(side, "exp", [(i, i ^ (4 if i % 2 else 2)) for i in range(count)])
+    side = lax.ppermute(side, "exp", [(i, i ^ (2 if i % 2 else 4)) for i in range(count)])
     sent = call(
         far_body, [shape(size, LANES)] * (high_groups - 1), [vmem] * QUAD, terms, flops=HOLD
     )

time: 23.5 us -> 23.4 us (level)
    ppermute x8, waiting for transfers between devices: 4.78 us -> 4.25 us  [swap(): return lax.ppermute(block, 'exp', [(i, i ^ mask) for i in range(count)])]
    ppermute x1, waiting for transfers between devices: 0.57 us -> 1.06 us  [on_device(): lax.ppermute(side, 'exp', [(i, i ^ (2 if i % 2 else 4)) for i in range(co...]
  transfers between devices with their start and end apart: 10 -> 10, of which waited for: 7 -> 6; matrix products, arithmetic and copies ran while one was open for 0% -> 0% of each run, Pallas kernels for 15% -> 15%
where the time goes in v8:
time: 23.4 us; the launch traced here: 23.3 us
  waiting for transfers between devices  9.17 us (39%)
  starting transfers between devices  8.09 us (35%)
  Pallas kernels  5.88 us (25%)
    ppermute x8, starting transfers between devices, swap(): return lax.ppermute(block, 'exp', [(i, i ^ mask) for i in range(count)])  6.98 us
    pallas_call x11, Pallas kernels, call(): pl.pallas_call(body, out_shape=outs, in_specs=ins, out_specs=jax.tree.map...  5.88 us
    ppermute x8, waiting for transfers between devices, swap(): return lax.ppermute(block, 'exp', [(i, i ^ mask) for i in range(count)])  4.25 us
    ppermute x1, waiting for transfers between devices, on_device(): lax.ppermute(ring, 'exp', [(i, (i + 1) % count) for i in range(count)])  3.86 us
    ppermute x1, waiting for transfers between devices, on_device(): lax.ppermute(side, 'exp', [(i, i ^ (2 if i % 2 else 4)) for i in range(co...  1.06 us
    ppermute x1, starting transfers between devices, on_device(): lax.ppermute(ring, 'exp', [(i, (i + 1) % count) for i in range(count)])  1.05 us
  transfers between devices with their start and end apart: 10, of which 6 were waited for; matrix products, arithmetic and copies ran while one was open for 0% of the time, Pallas kernels for 15%

profile of v8, /device:TPU:0, one launch (start us, length us, event | category | flops | bytes accessed | tf_op | source)
XLA Modules:
  0.0 23.3 jit_solution(13766211528002079095)
XLA Ops:
  0.0 1.5 %shard_map.73 = (f32[32,128]{1,0:T(8,128)S(1)}, f32[32,128]{1,0:T(8,128)S(1)}, f32[8,128]{1,0:T(8,128)S(1)}, f32[8,128]{1,0:T(8,128)S(1)}, bf16[512,512]{1,0:T(8...) custom-call(s32[16]{0:T(128)} %owner.1, ...), custom_call_target="tpu_custom_call" | custom-call | bytes 3674206 | tf_op jit(solution)/shard_map/pallas_call | solution.py:37
  1.5 0.0 copy-start
  1.6 1.0 %collective-permute-start = (f32[32,128]{1,0:T(8,128)S(1)}, f32[32,128]{1,0:T(8,128)S(1)}, u32[]{:S(2)}, u32[]{:S(2)}) collective-permute-start(f32[32,128]{1,0:T(8,128)S(1)} %get-tuple-element.52), channel_id=1, source_target_pairs={{0,1},{1,2},{2,3},{3,4},{4,5},{5,6},{6,7},{7,8},{8,9},{9,10},{10,1... | collective-permute-start | bytes 49160 | tf_op jit(solution)/shard_map/ppermute | solution.py:442
  2.6 0.5 %shard_map.74 = (f32[32,128]{1,0:T(8,128)S(1)}, f32[8,128]{1,0:T(8,128)S(1)}, f32[8,128]{1,0:T(8,128)S(1)}, bf16[512,512]{1,0:T(8,128)(2,1)S(1)}, bf16[512,512]{...) custom-call(f32[32,128]{1,0:T(8,128)S(1)} %get-tuple-element.40.refs, ...), custom_call_target="tpu_custom_call", output_to_operand_aliasing={{0}: (0, {}), {1}: (1, {}), {2}: (2, {}), {3}: (3, {}), {4}... | custom-call | bytes 2678784 | tf_op jit(solution)/shard_map/pallas_call | solution.py:37
  3.1 0.1 copy-done
  3.1 2.0 %shard_map.75 = (f32[256,512]{1,0:T(8,128)S(1)}, bf16[512,512]{1,0:T(8,128)(2,1)S(1)}, bf16[512,512]{1,0:T(8,128)(2,1)S(1)}) custom-call(f32[8,128]{1,0:T(8,128)S(1)} %get-tuple-element.54.own_ref, f32[1024,512]{1,0:T(8,128)S(1)} %copy-done, bf16[512,512]{1,0:T(8,128)(2,1)S(1)} %get-tuple-element.55.band, bf16[512,512]{1,0:T(8,128)(2,1)S(1)} %get-tuple-element.56.cols, ...), custom_call_target="tpu_custom_call" | custom-call | flops 1610612736 | bytes 4722688 | tf_op jit(solution)/shard_map/pallas_call | solution.py:37
  5.1 3.9 %collective-permute-done.got_ref = f32[32,128]{1,0:T(8,128)S(1)} collective-permute-done((f32[32,128]{1,0:T(8,128)S(1)}, f32[32,128]{1,0:T(8,128)S(1)}, u32[]{:S(2)}, u32[]{:S(2)}) %collective-permute-start) | collective-permute-done | bytes 16416 | tf_op jit(solution)/shard_map/ppermute | solution.py:442
  9.0 0.2 shard_map.76
  9.2 0.1 collective-permute-start.1
  9.3 0.5 %shard_map.77 = (f32[544,128]{1,0:T(8,128)S(1)}, f32[544,128]{1,0:T(8,128)S(1)}) custom-call(f32[32,128]{1,0:T(8,128)S(1)} %collective-permute-done.got_ref, f32[8,128]{1,0:T(8,128)S(1)} %get-tuple-element.53.first_ref, f32[8,512]{1,0:T(8,128)S(1)} %get-tuple-element.49.blocks_ref, f32[8,512]{1,0:T(8,128)S(1)} %get-tuple-element.50.lines_ref, ...), custom_call_target="tpu_custom_call" | custom-call | bytes 1626112 | tf_op jit(solution)/shard_map/pallas_call | solution.py:37
  9.7 0.6 %collective-permute-start.2 = (f32[544,128]{1,0:T(8,128)S(1)}, f32[544,128]{1,0:T(8,128)S(1)}, u32[]{:S(2)}, u32[]{:S(2)}) collective-permute-start(f32[544,128]{1,0:T(8,128)S(1)} %get-tuple-element.64), channel_id=1, source_target_pairs={{0,1},{1,0},{2,3},{3,2},{4,5},{5,4},{6,7},{7,6},{8,9},{9,8},{10,11... | collective-permute-start | bytes 835592 | tf_op jit(solution)/shard_map/ppermute | solution.py:31
  10.3 0.2 shard_map.79.keep_ref
  10.5 0.4 %collective-permute-done.1.half_ref = f32[576,128]{1,0:T(8,128)S(1)} collective-permute-done((f32[576,128]{1,0:T(8,128)S(1)}, f32[576,128]{1,0:T(8,128)S(1)}, u32[]{:S(2)}, u32[]{:S(2)}) %collective-permute-start.1) | collective-permute-done | bytes 294944 | tf_op jit(solution)/shard_map/ppermute | solution.py:31
  10.8 0.1 shard_map.80
  11.0 0.2 collective-permute-start.3
  11.2 1.0 %collective-permute-start.7 = (f32[136,128]{1,0:T(8,128)S(1)}, f32[136,128]{1,0:T(8,128)S(1)}, u32[]{:S(2)}, u32[]{:S(2)}) collective-permute-start(f32[136,128]{1,0:T(8,128)S(1)} %get-tuple-element.73), channel_id=1, source_target_pairs={{0,2},{1,3},{2,0},{3,1},{4,6},{5,7},{6,4},{7,5},{8,10},{9,11},{10,... | collective-permute-start | bytes 208904 | tf_op jit(solution)/shard_map/ppermute | solution.py:31
  12.2 2.3 %collective-permute-start.8 = (f32[136,128]{1,0:T(8,128)S(1)}, f32[136,128]{1,0:T(8,128)S(1)}, u32[]{:S(2)}, u32[]{:S(2)}) collective-permute-start(f32[136,128]{1,0:T(8,128)S(1)} %get-tuple-element.74), channel_id=1, source_target_pairs={{0,4},{1,5},{2,6},{3,7},{4,0},{5,1},{6,2},{7,3},{8,12},{9,13},{10,... | collective-permute-start | bytes 208904 | tf_op jit(solution)/shard_map/ppermute | solution.py:31
  14.5 0.0 collective-permute-done.2.got_ref
  14.5 0.2 shard_map.78
  14.7 0.1 collective-permute-start.5
  14.8 2.1 %collective-permute-done.3.b_ref = f32[136,128]{1,0:T(8,128)S(1)} collective-permute-done((f32[136,128]{1,0:T(8,128)S(1)}, f32[136,128]{1,0:T(8,128)S(1)}, u32[]{:S(2)}, u32[]{:S(2)}) %collective-permute-start.3) | collective-permute-done | bytes 69664 | tf_op jit(solution)/shard_map/ppermute | solution.py:31
  16.9 0.0 collective-permute-start.4
  16.9 0.0 collective-permute-done.7.c_ref
  16.9 0.0 collective-permute-done.8.d_ref
  17.0 2.8 %collective-permute-start.9 = (f32[136,128]{1,0:T(8,128)S(1)}, f32[136,128]{1,0:T(8,128)S(1)}, u32[]{:S(2)}, u32[]{:S(2)}) collective-permute-start(f32[136,128]{1,0:T(8,128)S(1)} %shard_map.82), channel_id=1, source_target_pairs={{0,8},{1,9},{2,10},{3,11},{4,12},{5,13},{6,14},{7,15},{8,0},{9,1},... | collective-permute-start | bytes 208904 | tf_op jit(solution)/shard_map/ppermute | solution.py:31
  19.8 1.1 %collective-permute-done.5.ref.refs_2_ = f32[272,128]{1,0:T(8,128)S(1)} collective-permute-done((f32[272,128]{1,0:T(8,128)S(1)}, f32[272,128]{1,0:T(8,128)S(1)}, u32[]{:S(2)}, u32[]{:S(2)}) %collective-permute-start.5) | collective-permute-done | bytes 139296 | tf_op jit(solution)/shard_map/ppermute | solution.py:483
  20.8 0.0 collective-permute-start.6
  20.8 1.3 %collective-permute-done.4.refs_1_ = f32[136,128]{1,0:T(8,128)S(1)} collective-permute-done((f32[136,128]{1,0:T(8,128)S(1)}, f32[136,128]{1,0:T(8,128)S(1)}, u32[]{:S(2)}, u32[]{:S(2)}) %collective-permute-start.4) | collective-permute-done | bytes 69664 | tf_op jit(solution)/shard_map/ppermute | solution.py:31
  22.1 0.4 %collective-permute-done.9.refs_4_ = f32[136,128]{1,0:T(8,128)S(1)} collective-permute-done((f32[136,128]{1,0:T(8,128)S(1)}, f32[136,128]{1,0:T(8,128)S(1)}, u32[]{:S(2)}, u32[]{:S(2)}) %collective-permute-start.9) | collective-permute-done | bytes 69664 | tf_op jit(solution)/shard_map/ppermute | solution.py:31
  22.6 0.0 collective-permute-done.6.refs_3_
  22.6 0.7 %shard_map.83 = f32[32,512]{1,0:T(8,128)} custom-call(f32[136,128]{1,0:T(8,128)S(1)} %get-tuple-element.65.refs_0_, f32[136,128]{1,0:T(8,128)S(1)} %collective-permute-done.4.refs_1_, f32[272,128]{1,0:T(8,128)S(1)} %collective-permute-done.5.ref.refs_2_, f32[136,128]{1,0:T(8,128)S(1)} %collective-permute-done.6.refs_3_, ...), custom_call_target="tpu_custom_call" | custom-call | bytes 417792 | tf_op jit(solution)/shard_map/pallas_call | solution.py:37
  (2 shorter events, 0.0 us)
Async XLA Ops:
  1.5 1.6 %copy-start = (f32[1024,512]{1,0:T(8,128)S(1)}, f32[1024,512]{1,0:T(8,128)}, u32[]{:S(2)}) copy-start(f32[1024,512]{1,0:T(8,128)} %image.1) | copy-start | bytes 6291460
  1.6 7.4 %collective-permute-start = (f32[32,128]{1,0:T(8,128)S(1)}, f32[32,128]{1,0:T(8,128)S(1)}, u32[]{:S(2)}, u32[]{:S(2)}) collective-permute-start(f32[32,128]{1,0:T(8,128)S(1)} %get-tuple-element.52), channel_id=1, source_target_pairs={{0,1},{1,2},{2,3},{3,4},{4,5},{5,6},{6,7},{7,8},{8,9},{9,10},{10,1... | collective-permute-start | bytes 49160 | tf_op jit(solution)/shard_map/ppermute | solution.py:442
  9.2 1.6 %collective-permute-start.1 = (f32[576,128]{1,0:T(8,128)S(1)}, f32[576,128]{1,0:T(8,128)S(1)}, u32[]{:S(2)}, u32[]{:S(2)}) collective-permute-start(f32[576,128]{1,0:T(8,128)S(1)} %shard_map.76), channel_id=1, source_target_pairs={{0,1},{1,0},{2,3},{3,2},{4,5},{5,4},{6,7},{7,6},{8,9},{9,8},{10,11... | collective-permute-start | bytes 884744 | tf_op jit(solution)/shard_map/ppermute | solution.py:31
  9.7 4.8 %collective-permute-start.2 = (f32[544,128]{1,0:T(8,128)S(1)}, f32[544,128]{1,0:T(8,128)S(1)}, u32[]{:S(2)}, u32[]{:S(2)}) collective-permute-start(f32[544,128]{1,0:T(8,128)S(1)} %get-tuple-element.64), channel_id=1, source_target_pairs={{0,1},{1,0},{2,3},{3,2},{4,5},{5,4},{6,7},{7,6},{8,9},{9,8},{10,11... | collective-permute-start | bytes 835592 | tf_op jit(solution)/shard_map/ppermute | solution.py:31
  11.0 5.9 %collective-permute-start.3 = (f32[136,128]{1,0:T(8,128)S(1)}, f32[136,128]{1,0:T(8,128)S(1)}, u32[]{:S(2)}, u32[]{:S(2)}) collective-permute-start(f32[136,128]{1,0:T(8,128)S(1)} %get-tuple-element.68), channel_id=1, source_target_pairs={{0,6},{1,7},{2,4},{3,5},{4,2},{5,3},{6,0},{7,1},{8,14},{9,15},{10,... | collective-permute-start | bytes 208904 | tf_op jit(solution)/shard_map/ppermute | solution.py:31
  11.2 5.8 %collective-permute-start.7 = (f32[136,128]{1,0:T(8,128)S(1)}, f32[136,128]{1,0:T(8,128)S(1)}, u32[]{:S(2)}, u32[]{:S(2)}) collective-permute-start(f32[136,128]{1,0:T(8,128)S(1)} %get-tuple-element.73), channel_id=1, source_target_pairs={{0,2},{1,3},{2,0},{3,1},{4,6},{5,7},{6,4},{7,5},{8,10},{9,11},{10,... | collective-permute-start | bytes 208904 | tf_op jit(solution)/shard_map/ppermute | solution.py:31
  12.2 4.7 %collective-permute-start.8 = (f32[136,128]{1,0:T(8,128)S(1)}, f32[136,128]{1,0:T(8,128)S(1)}, u32[]{:S(2)}, u32[]{:S(2)}) collective-permute-start(f32[136,128]{1,0:T(8,128)S(1)} %get-tuple-element.74), channel_id=1, source_target_pairs={{0,4},{1,5},{2,6},{3,7},{4,0},{5,1},{6,2},{7,3},{8,12},{9,13},{10,... | collective-permute-start | bytes 208904 | tf_op jit(solution)/shard_map/ppermute | solution.py:31
  14.7 6.1 %collective-permute-start.5 = (f32[272,128]{1,0:T(8,128)S(1)}, f32[272,128]{1,0:T(8,128)S(1)}, u32[]{:S(2)}, u32[]{:S(2)}) collective-permute-start(f32[272,128]{1,0:T(8,128)S(1)} %get-tuple-element.70), channel_id=1, source_target_pairs={{0,4},{1,3},{2,6},{3,1},{4,0},{5,7},{6,2},{7,5},{8,12},{9,11},{10,... | collective-permute-start | bytes 417800 | tf_op jit(solution)/shard_map/ppermute | solution.py:483
  16.9 5.2 %collective-permute-start.4 = (f32[136,128]{1,0:T(8,128)S(1)}, f32[136,128]{1,0:T(8,128)S(1)}, u32[]{:S(2)}, u32[]{:S(2)}) collective-permute-start(f32[136,128]{1,0:T(8,128)S(1)} %get-tuple-element.69), channel_id=1, source_target_pairs={{0,6},{1,7},{2,4},{3,5},{4,2},{5,3},{6,0},{7,1},{8,14},{9,15},{10,... | collective-permute-start | bytes 208904 | tf_op jit(solution)/shard_map/ppermute | solution.py:31
  17.0 5.6 %collective-permute-start.9 = (f32[136,128]{1,0:T(8,128)S(1)}, f32[136,128]{1,0:T(8,128)S(1)}, u32[]{:S(2)}, u32[]{:S(2)}) collective-permute-start(f32[136,128]{1,0:T(8,128)S(1)} %shard_map.82), channel_id=1, source_target_pairs={{0,8},{1,9},{2,10},{3,11},{4,12},{5,13},{6,14},{7,15},{8,0},{9,1},... | collective-permute-start | bytes 208904 | tf_op jit(solution)/shard_map/ppermute | solution.py:31
  20.8 1.7 %collective-permute-start.6 = (f32[136,128]{1,0:T(8,128)S(1)}, f32[136,128]{1,0:T(8,128)S(1)}, u32[]{:S(2)}, u32[]{:S(2)}) collective-permute-start(f32[136,128]{1,0:T(8,128)S(1)} %shard_map.81), channel_id=1, source_target_pairs={{0,1},{1,0},{2,3},{3,2},{4,5},{5,4},{6,7},{7,6},{8,9},{9,8},{10,11... | collective-permute-start | bytes 208904 | tf_op jit(solution)/shard_map/ppermute | solution.py:31
